TPU v7x, 32 devices: a whole 2x2x4 slice. The times are simulated.
32 devices in a mesh: groups: 2 (over x), ctx: 16 (over z, y, core).
Axes of the slice: x: 2, y: 2, z: 4, core: 2. Of those that a mesh axis runs over, the one named last changes fastest.
Arguments:
- queries: bfloat16 [2048, 4096], P(('groups', 'ctx')), parts along dimension 0, may hold values from -36 to 36
- keys: bfloat16 [2048, 512], P(('groups', 'ctx')), parts along dimension 0, may hold values from -12 to 12
- values: bfloat16 [2048, 512], P(('groups', 'ctx')), parts along dimension 0, may hold values from -6 to 6
- owner: int32 [2048], P('groups'), parts along dimension 0, may hold values from 0 to 15, as said below
- rollout_lengths: int32 [8], P('groups'), parts along dimension 0, may hold values from 1 to 512, 1024 in all
Outputs:
- attended: bfloat16 [2048, 4096], P(('groups', 'ctx')), parts along dimension 0
There are 2 independent parts, one for each index of `groups`. A program takes and returns all parts, laid end to end along the dimension named above; each array names one. Nothing has to cross between parts.
Inputs may be any that keep to these rules, and one draw needn't show every extreme that they name: `owner`: each device index owns exactly 64 tokens. The 64 tokens of one device go to half of the devices, 8 tokens to each, and these owners' indices are alike modulo 2.
All inputs are finite; a program needn't handle non-finite values.
Results may differ from a plain program's by a relative error of at most 0.005.
Values may be sent and summed in bfloat16 or wider, within the bound.
No kernel may reach another device: no remote copies, remote signals or barrier semaphores. Data moves between devices by JAX's collectives and lax.ppermute only.
A program may use at most 64 MiB of HBM per device.

v0:
```python
import math

import jax
import jax.numpy as jnp
from jax import lax
from jax.sharding import PartitionSpec as P

H = 32
KVH = 4
HD = 128


NEGATIVE = -1e30


def segment_of(position, rollout_ends):
    return jnp.sum((position[:, None] >= rollout_ends[None, :]).astype(jnp.int32), axis=1)


def attend_block(
    softmax_state, query_rows, query_pos, query_seg, key_block, value_block, key_pos, key_seg
):
    running_max, running_sum, weighted = softmax_state
    block_rows = key_block.shape[0]
    key_heads = key_block.reshape(block_rows, KVH, HD)
    value_heads = value_block.reshape(block_rows, KVH, HD)
    scores = jnp.einsum(
        "tkgd,ukd->kgtu", query_rows, key_heads, preferred_element_type=jnp.float32
    ) * (1.0 / math.sqrt(HD))
    visible = (key_pos[None, :] <= query_pos[:, None]) & (key_seg[None, :] == query_seg[:, None])
    scores = jnp.where(visible, scores, NEGATIVE)
    new_max = jnp.maximum(running_max, jnp.max(scores, axis=-1))
    weights = jnp.where(visible, jnp.exp(scores - new_max[..., None]), 0.0)
    factor = jnp.exp(running_max - new_max)
    weighted = weighted * factor[..., None] + jnp.einsum(
        "kgtu,ukd->kgtd",
        weights.astype(jnp.bfloat16),
        value_heads,
        preferred_element_type=jnp.float32,
    )
    running_sum = running_sum * factor + jnp.sum(weights, axis=-1)
    return (new_max, running_sum, weighted)


def on_device(queries, keys, values, owner, rollout_lengths):
    row_count = queries.shape[0]
    node_count = lax.axis_size("ctx")
    my_index = lax.axis_index("ctx")
    capacity = 2 * row_count // node_count
    group_size = H // KVH
    kv_width = KVH * HD
    rollout_ends = jnp.cumsum(rollout_lengths)
    owner_order = jnp.argsort(owner, stable=True)
    local_index = jnp.arange(row_count, dtype=jnp.int32)
    local_dest = lax.dynamic_slice_in_dim(owner, my_index * row_count, row_count)
    same_dest = (local_dest[:, None] == local_dest[None, :]) & (
        local_index[None, :] < local_index[:, None]
    )
    send_slot = local_dest * capacity + jnp.sum(same_dest.astype(jnp.int32), axis=1)
    held_pos = lax.dynamic_slice_in_dim(owner_order, my_index * row_count, row_count)
    mine_flags = (owner.reshape(node_count, row_count) == my_index).astype(jnp.int32)
    before_mine = (jnp.cumsum(mine_flags, axis=1) - mine_flags).reshape(-1)
    recv_slot = held_pos // row_count * capacity + before_mine[held_pos]

    def pack_rows(rows_in):
        return (
            jnp.zeros((node_count * capacity, rows_in.shape[1]), rows_in.dtype)
            .at[send_slot]
            .set(rows_in)
        )

    moved_q, moved_kv = (
        lax.all_to_all(pack_rows(queries), "ctx", split_axis=0, concat_axis=0, tiled=True),
        lax.all_to_all(
            pack_rows(jnp.concatenate((keys, values), axis=1)),
            "ctx",
            split_axis=0,
            concat_axis=0,
            tiled=True,
        ),
    )
    query_local = moved_q[recv_slot]
    kv_local = moved_kv[recv_slot]
    query_seg = segment_of(held_pos, rollout_ends)
    query_rows = query_local.reshape(row_count, KVH, group_size, HD)
    initial = (
        jnp.full((KVH, group_size, row_count), NEGATIVE, jnp.float32),
        jnp.zeros((KVH, group_size, row_count), jnp.float32),
        jnp.zeros((KVH, group_size, row_count, HD), jnp.float32),
    )
    kv_piece = lax.all_gather(kv_local, "ctx", axis=0, tiled=True)
    piece_rows = kv_piece.shape[0]
    key_seg = segment_of(owner_order, rollout_ends)
    needed = (jnp.min(owner_order) <= jnp.max(held_pos)) & (jnp.max(key_seg) >= jnp.min(query_seg))
    block_size = min(piece_rows, 512)
    block_count = piece_rows // block_size

    def compute(current):

        def one_block(inner_state, block_parts):
            kv_block, pos_block, seg_block = block_parts
            return (
                attend_block(
                    inner_state,
                    query_rows,
                    held_pos,
                    query_seg,
                    kv_block[:, :kv_width],
                    kv_block[:, kv_width:],
                    pos_block,
                    seg_block,
                ),
                None,
            )

        blocks = (
            kv_piece.reshape(block_count, block_size, 2 * kv_width),
            owner_order.reshape(block_count, block_size),
            key_seg.reshape(block_count, block_size),
        )
        result, unused = lax.scan(one_block, current, blocks)
        return result

    final_state = lax.cond(needed, compute, lambda current: current, initial)
    running_max, running_sum, weighted = final_state
    attended = (
        (weighted / running_sum[..., None])
        .transpose(2, 0, 1, 3)
        .reshape(row_count, H * HD)
        .astype(jnp.bfloat16)
    )
    return attended


def solution(mesh):
    placed = (
        P(("groups", "ctx"), None),
        P(("groups", "ctx"), None),
        P(("groups", "ctx"), None),
        P("groups"),
        P("groups"),
    )
    return jax.shard_map(
        on_device, mesh=mesh, in_specs=placed, out_specs=P(("groups", "ctx"), None), check_vma=False
    )
```

profile of v0, /device:TPU:0, one launch (start us, length us, event | category | flops | bytes accessed | tf_op | source)
XLA Modules:
  0.0 104.5 jit_solution(12768097611134879955)
XLA Ops:
  6.5 0.0 copy-start
  6.5 0.8 dynamic_slice.18
  7.3 0.2 convert_reduce_fusion
  7.5 0.8 compare_select_fusion.1
  8.3 1.9 %scatter_custom_fusion = bf16[128,1024]{1,0:T(8,128)(2,1)} fusion(s32[64]{0:T(128)S(1)} %compare_select_fusion.1, bf16[64,512]{1,0:T(8,128)(2,1)} %param.11, bf16[]{:T(256)} %constant.71, bf16[64,512]{1,0:T(8,128)(2,1)} %param.10, bf16[]{:T(256)} %constant.64.clone.1), kind=kCustom, calls=%fused_computation.31 | custom fusion | flops 262144 | bytes 393220 | tf_op jit(solution)/shard_map/scatter | solution.py:69
  10.2 7.4 %all-to-all-start = ((bf16[16,8,1024]{2,1,0:T(8,128)(2,1)}), bf16[16,8,1024]{2,1,0:T(8,128)(2,1)S(1)}, u32[]{:S(2)}, u32[]{:S(2)}) async-start(bf16[16,8,1024]{2,1,0:T(8,128)(2,1)} %bitcast.5), calls=%async_computation | async-start | bytes 524288 | tf_op jit(solution)/shard_map/all_to_all | solution.py:74
  17.6 0.0 all-gather.3.cloned.1.call-start
  17.6 0.7 compare_convert_fusion
  18.3 0.1 reshape.68
  18.4 0.2 reduce_window_sum.20
  18.6 0.1 reduce_window_sum.21
  18.7 0.7 fusion.26
  19.4 5.1 %sort.17 = (s32[1024]{0:T(1024)}, s32[1024]{0:T(1024)S(1)}) sort(s32[1024]{0:T(1024)} %param.12, s32[1024]{0:T(1024)S(1)} %iota.11), dimensions={0}, to_apply=%region_0.0 | sort | flops 10240 | bytes 16384 | tf_op jit(solution)/shard_map/jit(argsort)/sort | solution.py:53
  24.4 0.1 compare_select_fusion.2
  24.5 0.7 gather_fusion.1
  25.2 0.6 compare_select_fusion
  25.8 1.8 %all-to-all-done = bf16[16,8,1024]{2,1,0:T(8,128)(2,1)S(1)} async-done(((bf16[16,8,1024]{2,1,0:T(8,128)(2,1)}), bf16[16,8,1024]{2,1,0:T(8,128)(2,1)S(1)}, u32[]{:S(2)}, u32[]{:S(2)}) %all-to-all-start) | async-done | bytes 262176 | tf_op jit(solution)/shard_map/all_to_all | solution.py:74
  27.6 1.4 %gather_fusion.2 = bf16[64,1024]{1,0:T(8,128)(2,1)} fusion(bf16[128,1024]{1,0:T(8,128)(2,1)S(1)} %bitcast.77, s32[1024]{0:T(1024)S(1)} %pad_clamp_fusion.1), kind=kCustom, calls=%fused_computation.2 | custom fusion | bytes 262400 | tf_op jit(solution)/shard_map/gather | solution.py:83
  29.0 0.0 all-gather.3.cloned.1.call-update
  29.0 2.9 %scatter_custom_fusion.1 = bf16[128,4096]{1,0:T(8,128)(2,1)} fusion(s32[64]{0:T(128)S(1)} %compare_select_fusion.1, bf16[64,4096]{1,0:T(8,128)(2,1)} %param.9, bf16[]{:T(256)} %constant.64.clone.1), kind=kCustom, calls=%fused_computation.28 | custom fusion | bytes 1049088 | tf_op jit(solution)/shard_map/scatter | solution.py:69
  31.9 4.2 %all-to-all-start.1 = ((bf16[16,8,4096]{2,1,0:T(8,128)(2,1)}), bf16[16,8,4096]{2,1,0:T(8,128)(2,1)S(1)}, u32[]{:S(2)}, u32[]{:S(2)}) async-start(bf16[16,8,4096]{2,1,0:T(8,128)(2,1)} %bitcast.7), calls=%async_computation.1 | async-start | bytes 2097152 | tf_op jit(solution)/shard_map/all_to_all | solution.py:73
  36.2 0.0 copy-done
  36.2 0.2 reduce-window.8
  36.3 0.6 reduce_min.18
  37.0 0.1 convert_reduce_fusion.2
  37.1 0.6 reduce_min.19
  37.7 0.1 convert_reduce_fusion.1
  37.8 0.7 reduce_max.28
  40.9 22.7 %all-to-all-done.1 = bf16[16,8,4096]{2,1,0:T(8,128)(2,1)S(1)} async-done(((bf16[16,8,4096]{2,1,0:T(8,128)(2,1)}), bf16[16,8,4096]{2,1,0:T(8,128)(2,1)S(1)}, u32[]{:S(2)}, u32[]{:S(2)}) %all-to-all-start.1) | async-done | bytes 1048608 | tf_op jit(solution)/shard_map/all_to_all | solution.py:73
  63.6 13.8 %all-gather.3.cloned.1.call-done = bf16[1024,1024]{1,0:T(8,128)(2,1)} async-done(((bf16[64,1024]{1,0:T(8,128)(2,1)}), bf16[1024,1024]{1,0:T(8,128)(2,1)}) %all-gather.3.cloned.1.call-update) | async-done | bytes 2097168 | tf_op jit(solution)/shard_map/all_gather | solution.py:91
  77.4 17.3 %conditional.1 = (f32[4,8,64]{2,1,0:T(8,128)}, f32[4,8,64,128]{3,2,1,0:T(8,128)}) conditional(s32[]{:T(128)} %convert_element_type.35, () %tuple.17, (bf16[1024,1024]{1,0:T(8,128)(2,1)}, s32[1024]{0:T(1024)S(1)}, s32[1024]{0:T(1024)S(1)}, bf16[16,8,4096]{2,1,0:T(8,128)(2,1)S(1)}, s32[64,1]{0,1:T(1,128)S(1)}, /*index=5*/s32[64]{0:T(128)S(1)}, ...), branch_computations={%region_12.13_spmd, %region_13.18_spmd} | conditional | flops 551398400 | bytes 25986312 | solution.py:124
  77.4 0.9 gather_fusion
  78.3 0.1 copy.29
  78.4 0.2 copy.20
  78.6 16.1 %while.14 = (s32[]{:T(128)}, f32[4,8,64]{2,1,0:T(8,128)S(1)}, f32[4,8,64]{2,1,0:T(8,128)}, f32[4,8,64,128]{3,2,1,0:T(8,128)}, s32[2,512]{1,0:T(2,128)S(1)}, /*in...) while((s32[]{:T(128)}, f32[4,8,64]{2,1,0:T(8,128)S(1)}, ...), condition=%wide.region_17.17_spmd.clone, body=%wide.region_14.16_spmd.clone.sunk | while | flops 551397376 | bytes 22819472 | solution.py:121
  78.7 0.1 compare_and_fusion.2
  78.8 1.3 %constant_dynamic-slice_fusion.6 = bf16[1,512,1024]{2,1,0:T(8,128)(2,1)S(1)} fusion(bf16[2,512,1024]{2,1,0:T(8,128)(2,1)} %get-tuple-element.302, s32[]{:T(128)S(6)} %copy.39), kind=kLoop, calls=%fused_computation.19.clone.1 | loop fusion | bytes 2097156 | tf_op jit(solution)/shard_map/cond/branch_1_fun/while/body/jit(dynamic_index_in_dim)/dynamic_slice | solution.py:121
  80.1 0.5 copy.34
  80.6 0.1 fusion.40
  80.7 0.8 fusion.41
  81.5 1.4 %fusion.42 = f32[4,8,64]{2,1,0:T(8,128)S(1)} fusion(f32[4,512,64,8]{1,2,3,0:T(8,128)S(1)} %get-tuple-element.266, f32[4,8,64]{2,1,0:T(8,128)S(1)} %select_maximum_fusion.2, pred[64,512]{1,0:T(8,128)(4,1)S(1)} %compare_and_fusion.2), kind=kLoop, calls=%fused_computation.9.clone.1 | loop fusion | flops 5240832 | bytes 4243456 | tf_op jit(solution)/shard_map/cond/branch_1_fun/while/body/eval_jaxpr/reduce_sum | solution.py:41
  82.9 0.6 fusion.43
  83.5 2.3 %fusion.44 = f32[4,8,64,128]{3,2,1,0:T(8,128)} fusion(bf16[512,4,128,1]{0,2,3,1:T(8,128)(2,1)S(1)} %bitcast.76, f32[4,512,64,8]{1,2,3,0:T(8,128)S(1)} %get-tuple-element.266, f32[4,8,64]{2,1,0:T(8,128)S(1)} %select_maximum_fusion.2, pred[64,512]{1,0:T(8,128)(4,1)S(1)} %compare_and_fusion.2, f32[4,8,64,128]{3,2,1,0:T(8,128)} %get-tuple-element.285, ...), kind=kOutput, calls=%fused_computation.12.clone.1 | convolution fusion | flops 274464768 | bytes 6864897 | tf_op jit(solution)/shard_map/cond/branch_1_fun/while/body/eval_jaxpr/kgtu,ukd->kgtd/dot_general | solution.py:35
  85.8 0.1 compare_and_fusion.2
  85.9 1.3 %constant_dynamic-slice_fusion.6 = bf16[1,512,1024]{2,1,0:T(8,128)(2,1)S(1)} fusion(bf16[2,512,1024]{2,1,0:T(8,128)(2,1)} %get-tuple-element.302, s32[]{:T(128)S(6)} %copy.39), kind=kLoop, calls=%fused_computation.19.clone.1 | loop fusion | bytes 2097156 | tf_op jit(solution)/shard_map/cond/branch_1_fun/while/body/jit(dynamic_index_in_dim)/dynamic_slice | solution.py:121
  87.2 0.5 copy.34
  87.8 0.1 fusion.40
  87.8 0.8 fusion.41
  88.7 1.4 %fusion.42 = f32[4,8,64]{2,1,0:T(8,128)S(1)} fusion(f32[4,512,64,8]{1,2,3,0:T(8,128)S(1)} %get-tuple-element.266, f32[4,8,64]{2,1,0:T(8,128)S(1)} %select_maximum_fusion.2, pred[64,512]{1,0:T(8,128)(4,1)S(1)} %compare_and_fusion.2), kind=kLoop, calls=%fused_computation.9.clone.1 | loop fusion | flops 5240832 | bytes 4243456 | tf_op jit(solution)/shard_map/cond/branch_1_fun/while/body/eval_jaxpr/reduce_sum | solution.py:41
  90.0 1.3 %fusion.43 = (f32[4,8,64]{2,1,0:T(8,128)}, f32[4,8,64]{2,1,0:T(8,128)S(1)}) fusion(f32[4,8,64]{2,1,0:T(8,128)S(1)} %fusion.42, f32[4,8,64]{2,1,0:T(8,128)} %get-tuple-element.284, pred[]{:T(512)S(6)} %compare.9, f32[4,8,64]{2,1,0:T(8,128)S(1)} %select_maximum_fusion.2, f32[4,8,64]{2,1,0:T(8,128)S(1)} %get-tuple-element.283), kind=kLoop, calls=%fused_computation.16.clone.1 | loop fusion | flops 10240 | bytes 49153 | tf_op jit(solution)/shard_map/cond/branch_1_fun/while/body/eval_jaxpr/add | solution.py:41
  91.4 3.3 %fusion.44 = f32[4,8,64,128]{3,2,1,0:T(8,128)} fusion(bf16[512,4,128,1]{0,2,3,1:T(8,128)(2,1)S(1)} %bitcast.76, f32[4,512,64,8]{1,2,3,0:T(8,128)S(1)} %get-tuple-element.266, f32[4,8,64]{2,1,0:T(8,128)S(1)} %select_maximum_fusion.2, pred[64,512]{1,0:T(8,128)(4,1)S(1)} %compare_and_fusion.2, f32[4,8,64,128]{3,2,1,0:T(8,128)} %get-tuple-element.285, ...), kind=kOutput, calls=%fused_computation.12.clone.1 | convolution fusion | flops 274464768 | bytes 6864897 | tf_op jit(solution)/shard_map/cond/branch_1_fun/while/body/eval_jaxpr/kgtu,ukd->kgtd/dot_general | solution.py:35
  94.7 1.6 %fusion.15 = bf16[64,4,8,128]{3,0,2,1:T(8,128)(2,1)S(1)} fusion(f32[4,8,64,128]{3,2,1,0:T(8,128)} %get-tuple-element.86, f32[4,8,64]{2,1,0:T(8,128)} %get-tuple-element.87), kind=kLoop, calls=%fused_computation.30 | loop fusion | flops 524288 | bytes 1581056 | tf_op jit(solution)/shard_map/convert_element_type | solution.py:130
  96.3 0.3 copy.21
  96.6 1.0 copy.32
  (15 shorter events, 0.1 us)
Async XLA Ops:
  6.5 29.6 %copy-start = (s32[4]{0:T(128)S(1)}, s32[4]{0:T(128)}, u32[]{:S(2)}) copy-start(s32[4]{0:T(128)} %param.13) | copy-start | bytes 52
  10.2 17.4 %all-to-all-start = ((bf16[16,8,1024]{2,1,0:T(8,128)(2,1)}), bf16[16,8,1024]{2,1,0:T(8,128)(2,1)S(1)}, u32[]{:S(2)}, u32[]{:S(2)}) async-start(bf16[16,8,1024]{2,1,0:T(8,128)(2,1)} %bitcast.5), calls=%async_computation | async-start | bytes 524288 | tf_op jit(solution)/shard_map/all_to_all | solution.py:74
  17.6 59.8 %all-gather.3.cloned.1.call-start = ((), (), s32[]{:S(2)}) async-start(), calls=%async_computation.2 | async-start | bytes 2228224 | tf_op jit(solution)/shard_map/all_gather | solution.py:91
  31.9 31.7 %all-to-all-start.1 = ((bf16[16,8,4096]{2,1,0:T(8,128)(2,1)}), bf16[16,8,4096]{2,1,0:T(8,128)(2,1)S(1)}, u32[]{:S(2)}, u32[]{:S(2)}) async-start(bf16[16,8,4096]{2,1,0:T(8,128)(2,1)} %bitcast.7), calls=%async_computation.1 | async-start | bytes 2097152 | tf_op jit(solution)/shard_map/all_to_all | solution.py:73
Sparse Core Ops, SparseCore 0:
  29.1 48.2 all-gather.2
where the time goes:
time: 105 us; the launch traced here: 104 us
  waiting for transfers between devices  38.2 us (36%)
  other arithmetic  19 us (18%)
  between operations  15.9 us (15%)
  local copies, waits for them, and re-layouts  12.3 us (12%)
  starting transfers between devices  11.7 us (11%)
  matrix products  7.23 us (7%)
    all_to_all x1, waiting for transfers between devices, on_device(): lax.all_to_all(pack_rows(queries), 'ctx', split_axis=0, concat_axis=0, ti...  22.7 us
    all_gather x1, waiting for transfers between devices, on_device(): kv_piece = lax.all_gather(kv_local, 'ctx', axis=0, tiled=True)  13.8 us
    all_to_all x1, starting transfers between devices, on_device(): lax.all_to_all(pack_rows(jnp.concatenate((keys, values), axis=1)), 'ctx',...  7.39 us
    dot_general x2, matrix products, attend_block(): jnp.einsum('kgtu,ukd->kgtd', weights.astype(jnp.bfloat16), value_heads, p...  5.63 us
    sort x1, other arithmetic, on_device(): owner_order = jnp.argsort(owner, stable=True)  5.05 us
    all_to_all x1, starting transfers between devices, on_device(): lax.all_to_all(pack_rows(queries), 'ctx', split_axis=0, concat_axis=0, ti...  4.25 us
    dynamic_slice x6, local copies, waits for them, and re-layouts, compute(): result, unused = lax.scan(one_block, current, blocks)  3.7 us
    scatter x1, local copies, waits for them, and re-layouts, pack_rows(): return jnp.zeros((node_count * capacity, rows_in.shape[1]), rows_in.dtype...  2.92 us
  transfers between devices with their start and end apart: 3, of which 3 were waited for; matrix products, arithmetic and copies ran while one was open for 13% of the time, Pallas kernels for 0%

commit v1 on v0

v1 whole, which is shorter than its diff:
```python
import functools
import math

import jax
import jax.numpy as jnp
from jax import lax
from jax.experimental import pallas as pl
from jax.experimental.pallas import tpu as pltpu
from jax.sharding import PartitionSpec as P

H = 32
KVH = 4
HD = 128
GROUP = H // KVH
WIDE = GROUP * HD
NEGATIVE = -1e30
LANES = 128
TILE = 16
VMEM = pltpu.CompilerParams(vmem_limit_bytes=40 * 2**20)


def row_to_column(row):
    size = row.shape[1]
    here = lax.broadcasted_iota(jnp.int32, (size, size), 0)
    there = lax.broadcasted_iota(jnp.int32, (size, size), 1)
    return jnp.sum(jnp.where(here == there, row, 0), axis=1, keepdims=True)


def column_to_row(column):
    size = column.shape[0]
    here = lax.broadcasted_iota(jnp.int32, (size, size), 0)
    there = lax.broadcasted_iota(jnp.int32, (size, size), 1)
    return jnp.sum(jnp.where(here == there, column, 0), axis=0, keepdims=True)


def pack_kernel(levels, per_level, owner_ref, q_ref, k_ref, v_ref, out_ref):
    me = lax.axis_index("ctx")
    rows = q_ref.shape[0]
    both = owner_ref[pl.ds(me // 2, 1), :]
    swapped = jnp.concatenate((both[:, rows:], both[:, :rows]), axis=1)
    own = jnp.where(me % 2 == 1, swapped, both)[:, :rows]
    token = lax.broadcasted_iota(jnp.int32, (1, rows), 1)
    key_row = own * rows + token
    rank = jnp.sum((row_to_column(key_row) < key_row).astype(jnp.int32), axis=0, keepdims=True)
    place = lax.broadcasted_iota(jnp.int32, (rows, rows), 0)
    order = (place == rank).astype(jnp.float32).astype(jnp.bfloat16)
    for member in range(KVH):
        wide = slice(member * WIDE, (member + 1) * WIDE)
        head = slice(member * HD, (member + 1) * HD)
        sorted_q = jnp.dot(order, q_ref[:, wide], preferred_element_type=jnp.float32)
        sorted_q = sorted_q.astype(jnp.bfloat16)
        for level in range(levels):
            dest = level * KVH + member
            part = sorted_q[level * per_level : (level + 1) * per_level]
            if per_level < TILE:
                part = jnp.concatenate((part, jnp.zeros((TILE - per_level, WIDE), part.dtype)), 0)
            out_ref[dest, :TILE, :] = part
            for block in range(rows // TILE):
                here = slice(block * TILE, (block + 1) * TILE)
                col = block * 2 * HD
                out_ref[dest, TILE:, col : col + HD] = k_ref[here, head]
                out_ref[dest, TILE:, col + HD : col + 2 * HD] = v_ref[here, head]


def place_kernel(per_level, lengths_ref, owner_ref, pos_ref, start_ref, order_ref):
    me = lax.axis_index("ctx")
    level, member = me // KVH, me % KVH
    table_rows = owner_ref.shape[0]
    total = table_rows * LANES
    held = pos_ref.shape[0]
    rows = LANES // 2
    shift = per_level.bit_length() - 1
    block_rows = 32
    table_step = table_rows // (held // block_rows)
    first = lax.broadcasted_iota(jnp.int32, (LANES, LANES), 0)
    second = lax.broadcasted_iota(jnp.int32, (LANES, LANES), 1)
    same = (first < rows) == (second < rows)
    lane = lax.broadcasted_iota(jnp.int32, (1, LANES), 1)
    line = lax.broadcasted_iota(jnp.int32, (block_rows, 1), 0)
    wanted = level * per_level + jnp.bitwise_and(line, per_level - 1)
    source = jnp.right_shift(line, shift)
    keys = []
    for block in range(held // block_rows):
        pos = jnp.zeros((block_rows, 1), jnp.int32)
        own = jnp.zeros((block_rows, 1), jnp.int32)
        for step in range(table_step):
            table = block * table_step + step
            owners = owner_ref[table : table + 1, :]
            key_row = owners * LANES + lane
            below = same & (row_to_column(key_row) < key_row)
            rank = jnp.sum(below.astype(jnp.int32), axis=0, keepdims=True)
            lane_source = 2 * step + (lane >= rows).astype(jnp.int32)
            hit = (wanted == rank) & (source == lane_source)
            pos += jnp.sum(jnp.where(hit, lane + table * LANES, 0), axis=1, keepdims=True)
            own += jnp.sum(jnp.where(hit, owners, 0), axis=1, keepdims=True)
        start = jnp.zeros((block_rows, 1), jnp.int32)
        end = jnp.int32(0)
        for rollout in range(lengths_ref.shape[0]):
            end = end + lengths_ref[rollout]
            start = jnp.where(pos >= end, end, start)
        here = slice(block * block_rows, (block + 1) * block_rows)
        pos_ref[here, :] = jnp.broadcast_to(pos, (block_rows, LANES))
        start_ref[here, :] = jnp.broadcast_to(start, (block_rows, LANES))
        keys.append((own - level * KVH) * total + pos)
    key_col = jnp.concatenate(keys, axis=0)
    key_row = column_to_row(key_col)
    slot = jnp.sum((key_col < key_row).astype(jnp.int32), axis=0, keepdims=True)
    slot = jnp.bitwise_xor(slot, member * rows)
    place = lax.broadcasted_iota(jnp.int32, (held, held), 0)
    order_ref[...] = (place == slot).astype(jnp.float32).astype(jnp.bfloat16)


def attend_kernel(q_ref, kv_ref, pos_ref, start_ref, order_ref, *refs):
    out_refs, (k_all, v_all, context) = refs[:KVH], refs[KVH:]
    nodes = kv_ref.shape[0]
    total = k_all.shape[0]
    held = context.shape[0]
    block_rows = 32
    blocks = held // block_rows
    span = total // blocks
    tokens = total // nodes
    scale = math.log2(math.e) / math.sqrt(HD)

    def unpack(node, carry):
        for block in range(tokens // TILE):
            row = pl.ds(pl.multiple_of(node * tokens + block * TILE, TILE), TILE)
            col = block * 2 * HD
            k_all[row, :] = kv_ref[node, :, col : col + HD]
            v_all[row, :HD] = kv_ref[node, :, col + HD : col + 2 * HD]
        return carry

    v_all[:, HD:] = jnp.ones((total, HD), jnp.bfloat16)
    lax.fori_loop(0, nodes, unpack, 0, unroll=nodes <= 16)

    for block in range(blocks):
        here = slice(block * block_rows, (block + 1) * block_rows)
        pieces = []
        for head in range(GROUP):
            for part in range(block_rows // TILE):
                at = block * (block_rows // TILE) + part
                pieces.append(q_ref[at, :, head * HD : (head + 1) * HD])
        queries = jnp.concatenate(pieces, axis=0)
        pos = pos_ref[here, :1]
        start = start_ref[here, :1]
        low, high = max(0, block - blocks // 2) * span, (block + 1) * span
        chunk = high - low if high - low <= 1024 else span
        peak, acc = None, None
        for lower in range(low, high, chunk):
            keys = slice(lower, lower + chunk)
            scores = lax.dot_general(
                queries, k_all[keys, :], (((1,), (1,)), ((), ())), preferred_element_type=jnp.float32
            )
            at = lower + lax.broadcasted_iota(jnp.int32, (block_rows, chunk), 1)
            bias = jnp.where((at <= pos) & (at >= start), 0.0, NEGATIVE)
            scores = scores.reshape(GROUP, block_rows, chunk) + bias[None]
            scores = scores.reshape(GROUP * block_rows, chunk)
            top = jnp.max(scores, axis=1, keepdims=True)
            if peak is not None:
                top = jnp.maximum(peak, top)
            probs = jnp.exp2((scores - top) * scale)
            if chunk != high - low:
                seen = (at <= pos) & (at >= start)
                probs = probs.reshape(GROUP, block_rows, chunk)
                probs = jnp.where(seen[None], probs, 0.0).reshape(GROUP * block_rows, chunk)
            new = jnp.dot(probs.astype(jnp.bfloat16), v_all[keys, :], preferred_element_type=jnp.float32)
            acc = new if acc is None else acc * jnp.exp2((peak - top) * scale) + new
            peak = top
        result = (acc[:, :HD] / acc[:, HD:]).astype(jnp.bfloat16)
        for head in range(GROUP):
            part = result[head * block_rows : (head + 1) * block_rows]
            context[here, head * HD : (head + 1) * HD] = part
    rows = held // KVH
    for member in range(KVH):
        order = order_ref[member * rows : (member + 1) * rows, :]
        moved = jnp.dot(order, context[...], preferred_element_type=jnp.float32)
        out_refs[member][...] = moved.astype(jnp.bfloat16)


def assemble_kernel(*refs):
    member = lax.axis_index("ctx") % KVH
    out_ref = refs[KVH]
    for index in range(KVH):
        col = pl.multiple_of(jnp.bitwise_xor(member, index) * WIDE, WIDE)
        out_ref[:, pl.ds(col, WIDE)] = refs[index][...]


def on_device(queries, keys, values, owner, rollout_lengths):
    rows = queries.shape[0]
    nodes = lax.axis_size("ctx")
    total = owner.shape[0]
    levels = nodes // KVH
    per_level = rows // levels
    held = rows * KVH
    table = owner.reshape(total // LANES, LANES)
    whole = pl.BlockSpec(memory_space=pltpu.VMEM)

    packed = pl.pallas_call(
        functools.partial(pack_kernel, levels, per_level),
        out_shape=jax.ShapeDtypeStruct((nodes, 2 * TILE, WIDE), jnp.bfloat16),
        in_specs=[whole] * 4,
        out_specs=whole,
        compiler_params=VMEM,
        name="pack",
    )(table, queries, keys, values)
    moved = lax.all_to_all(packed, "ctx", split_axis=0, concat_axis=0, tiled=True)

    pos, start, order = pl.pallas_call(
        functools.partial(place_kernel, per_level),
        out_shape=(
            jax.ShapeDtypeStruct((held, LANES), jnp.int32),
            jax.ShapeDtypeStruct((held, LANES), jnp.int32),
            jax.ShapeDtypeStruct((held, held), jnp.bfloat16),
        ),
        in_specs=[pl.BlockSpec(memory_space=pltpu.SMEM), whole],
        out_specs=(whole, whole, whole),
        compiler_params=VMEM,
        name="place",
    )(rollout_lengths, table)

    half = functools.partial(pl.BlockSpec, (nodes, TILE, WIDE))
    q_part, q_spec = moved, half(lambda i: (0, 0, 0))
    if per_level < TILE:
        q_part = moved[:, :per_level].reshape(held // TILE, TILE, WIDE)
        q_spec = pl.BlockSpec((held // TILE, TILE, WIDE), lambda i: (0, 0, 0))
    flat = lambda shape: pl.BlockSpec(shape, lambda i: (0, 0))
    blocks = pl.pallas_call(
        attend_kernel,
        grid=(1,),
        out_shape=tuple(jax.ShapeDtypeStruct((rows, WIDE), jnp.bfloat16) for _ in range(KVH)),
        in_specs=[
            q_spec,
            half(lambda i: (0, 1, 0)),
            flat((held, LANES)),
            flat((held, LANES)),
            flat((held, held)),
        ],
        out_specs=tuple(flat((rows, WIDE)) for _ in range(KVH)),
        scratch_shapes=[
            pltpu.VMEM((total, HD), jnp.bfloat16),
            pltpu.VMEM((total, 2 * HD), jnp.bfloat16),
            pltpu.VMEM((held, WIDE), jnp.bfloat16),
        ],
        compiler_params=VMEM,
        name="attend",
    )(q_part, moved, pos, start, order)

    returned = [blocks[0]]
    for index in range(1, KVH):
        pairs = [(node, node ^ index) for node in range(nodes)]
        returned.append(lax.ppermute(blocks[index], "ctx", pairs))
    return pl.pallas_call(
        assemble_kernel,
        out_shape=jax.ShapeDtypeStruct((rows, H * HD), jnp.bfloat16),
        in_specs=[whole] * KVH,
        out_specs=whole,
        compiler_params=VMEM,
        name="assemble",
    )(*returned)


def solution(mesh):
    placed = (
        P(("groups", "ctx"), None),
        P(("groups", "ctx"), None),
        P(("groups", "ctx"), None),
        P("groups"),
        P("groups"),
    )
    return jax.shard_map(
        on_device, mesh=mesh, in_specs=placed, out_specs=P(("groups", "ctx"), None), check_vma=False
    )
```

time: 105 us -> 49.3 us (0.47)
  the two profiles are of different devices: /device:TPU:0 before, /device:TPU:17 now
where the time goes in v1:
time: 49.3 us; the launch traced here: 49 us
  waiting for transfers between devices  29.3 us (59%)
  starting transfers between devices  9.28 us (19%)
  Pallas kernels  6.98 us (14%)
  local copies, waits for them, and re-layouts  3.41 us (7%)
    all_to_all x1, waiting for transfers between devices, on_device(): lax.all_to_all(packed, 'ctx', split_axis=0, concat_axis=0, tiled=True)  22.9 us
    all_to_all x1, starting transfers between devices, on_device(): lax.all_to_all(packed, 'ctx', split_axis=0, concat_axis=0, tiled=True)  6.64 us
    ppermute x3, waiting for transfers between devices, on_device(): returned.append(lax.ppermute(blocks[index], 'ctx', pairs))  6.33 us
    unnamed x12, local copies, waits for them, and re-layouts  3.41 us
    pallas_call x1, Pallas kernels, on_device(): pl.pallas_call(attend_kernel, grid=(1,), out_shape=tuple((jax.ShapeDtypeS...  2.98 us
    ppermute x3, starting transfers between devices, on_device(): returned.append(lax.ppermute(blocks[index], 'ctx', pairs))  2.64 us
    pallas_call x1, Pallas kernels, on_device(): pl.pallas_call(functools.partial(place_kernel, per_level), out_shape=(jax...  1.72 us
    pallas_call x1, Pallas kernels, on_device(): pl.pallas_call(functools.partial(pack_kernel, levels, per_level), out_sha...  1.44 us
  transfers between devices with their start and end apart: 4, of which 3 were waited for; matrix products, arithmetic and copies ran while one was open for 0% of the time, Pallas kernels for 4%

profile of v1, /device:TPU:17, one launch (start us, length us, event | category | flops | bytes accessed | tf_op | source)
XLA Modules:
  0.0 49.0 jit_solution(16461691987787679526)
XLA Ops:
  0.0 0.0 copy-start
  0.0 1.0 %copy-done = bf16[64,4096]{1,0:T(8,128)(2,1)S(1)} copy-done((bf16[64,4096]{1,0:T(8,128)(2,1)S(1)}, bf16[64,4096]{1,0:T(8,128)(2,1)}, u32[]{:S(2)}) %copy-start) | copy-done | bytes 524312
  1.0 0.0 copy-start.1
  1.0 0.8 %copy-done.1 = bf16[64,512]{1,0:T(8,128)(2,1)S(1)} copy-done((bf16[64,512]{1,0:T(8,128)(2,1)S(1)}, bf16[64,512]{1,0:T(8,128)(2,1)}, u32[]{:S(2)}) %copy-start.1) | copy-done | bytes 65560
  1.9 0.0 copy-start.2
  1.9 0.8 %copy-done.2 = bf16[64,512]{1,0:T(8,128)(2,1)S(1)} copy-done((bf16[64,512]{1,0:T(8,128)(2,1)S(1)}, bf16[64,512]{1,0:T(8,128)(2,1)}, u32[]{:S(2)}) %copy-start.2) | copy-done | bytes 65560
  2.7 0.0 copy-start.3
  2.7 0.7 %copy-done.3 = s32[1024]{0:T(1024)S(1)} copy-done((s32[1024]{0:T(1024)S(1)}, s32[1024]{0:T(1024)}, u32[]{:S(2)}) %copy-start.3) | copy-done | bytes 4120
  3.4 1.4 %pack.1 = bf16[16,32,1024]{2,1,0:T(8,128)(2,1)} custom-call(s32[8,128]{1,0:T(8,128)S(1)} %bitcast.1, bf16[64,4096]{1,0:T(8,128)(2,1)S(1)} %copy-done, bf16[64,512]{1,0:T(8,128)(2,1)S(1)} %copy-done.1, bf16[64,512]{1,0:T(8,128)(2,1)S(1)} %copy-done.2), custom_call_target="tpu_custom_call" | custom-call | tf_op jit(solution)/shard_map/pack/pallas_call | solution.py:197
  4.9 0.0 copy-start.4
  4.9 0.0 copy-start.5
  4.9 6.6 %all-to-all-start = ((bf16[16,32,1024]{2,1,0:T(8,128)(2,1)}), bf16[16,32,1024]{2,1,0:T(8,128)(2,1)S(1)}, u32[]{:S(2)}, u32[]{:S(2)}) async-start(bf16[16,32,1024]{2,1,0:T(8,128)(2,1)} %pack.1), calls=%async_computation | async-start | bytes 2097152 | tf_op jit(solution)/shard_map/all_to_all | solution.py:205
  11.5 0.0 copy-done.4
  11.5 0.0 copy-done.5
  11.5 1.7 %place.1 = (s32[256,128]{1,0:T(8,128)S(1)}, s32[256,128]{1,0:T(8,128)S(1)}, bf16[256,256]{1,0:T(8,128)(2,1)S(1)}) custom-call(s32[4]{0:T(128)S(1)} %copy-done.5, s32[8,128]{1,0:T(8,128)S(1)} %bitcast.2), custom_call_target="tpu_custom_call" | custom-call | tf_op jit(solution)/shard_map/place/pallas_call | solution.py:207
  13.2 22.9 %all-to-all-done.q_ref.kv_ref = bf16[16,32,1024]{2,1,0:T(8,128)(2,1)S(1)} async-done(((bf16[16,32,1024]{2,1,0:T(8,128)(2,1)}), bf16[16,32,1024]{2,1,0:T(8,128)(2,1)S(1)}, u32[]{:S(2)}, u32[]{:S(2)}) %all-to-all-start) | async-done | bytes 1048608 | tf_op jit(solution)/shard_map/all_to_all | solution.py:205
  36.2 3.0 %attend.1 = (bf16[64,1024]{1,0:T(8,128)(2,1)S(1)}, bf16[64,1024]{1,0:T(8,128)(2,1)S(1)}, bf16[64,1024]{1,0:T(8,128)(2,1)S(1)}, bf16[64,1024]{1,0:T(8,128)(2,1)S(1)}) custom-call(bf16[16,32,1024]{2,1,0:T(8,128)(2,1)S(1)} %all-to-all-done.q_ref.kv_ref, bf16[16,32,1024]{2,1,0:T(8,128)(2,1)S(1)} %all-to-all-done.q_ref.kv_ref, ...), custom_call_target="tpu_custom_call" | custom-call | tf_op jit(solution)/shard_map/attend/pallas_call | solution.py:226
  39.1 0.9 %collective-permute-start = (bf16[64,1024]{1,0:T(8,128)(2,1)S(1)}, bf16[64,1024]{1,0:T(8,128)(2,1)S(1)}, u32[]{:S(2)}, u32[]{:S(2)}) collective-permute-start(bf16[64,1024]{1,0:T(8,128)(2,1)S(1)} %get-tuple-element.16), channel_id=1, source_target_pairs={{0,1},{1,0},{2,3},{3,2},{4,5},{5,4},{6,7},{7,6},{8,9},{9,8},{10,11... | collective-permute-start | bytes 393224 | tf_op jit(solution)/shard_map/ppermute | solution.py:250
  40.1 0.0 collective-permute-start.1
  40.1 1.7 %collective-permute-start.2 = (bf16[64,1024]{1,0:T(8,128)(2,1)S(1)}, bf16[64,1024]{1,0:T(8,128)(2,1)S(1)}, u32[]{:S(2)}, u32[]{:S(2)}) collective-permute-start(bf16[64,1024]{1,0:T(8,128)(2,1)S(1)} %get-tuple-element.18), channel_id=1, source_target_pairs={{0,3},{1,2},{2,1},{3,0},{4,7},{5,6},{6,5},{7,4},{8,11},{9,10},{10,... | collective-permute-start | bytes 393224 | tf_op jit(solution)/shard_map/ppermute | solution.py:250
  41.8 0.0 collective-permute-done.refs_1_
  41.8 3.4 %collective-permute-done.1.refs_2_ = bf16[64,1024]{1,0:T(8,128)(2,1)S(1)} collective-permute-done((bf16[64,1024]{1,0:T(8,128)(2,1)S(1)}, bf16[64,1024]{1,0:T(8,128)(2,1)S(1)}, u32[]{:S(2)}, u32[]{:S(2)}) %collective-permute-start.1) | collective-permute-done | bytes 131104 | tf_op jit(solution)/shard_map/ppermute | solution.py:250
  45.2 3.0 %collective-permute-done.2.refs_3_ = bf16[64,1024]{1,0:T(8,128)(2,1)S(1)} collective-permute-done((bf16[64,1024]{1,0:T(8,128)(2,1)S(1)}, bf16[64,1024]{1,0:T(8,128)(2,1)S(1)}, u32[]{:S(2)}, u32[]{:S(2)}) %collective-permute-start.2) | collective-permute-done | bytes 131104 | tf_op jit(solution)/shard_map/ppermute | solution.py:250
  48.1 0.8 %assemble.1 = bf16[64,4096]{1,0:T(8,128)(2,1)} custom-call(bf16[64,1024]{1,0:T(8,128)(2,1)S(1)} %get-tuple-element.15.refs_0_, bf16[64,1024]{1,0:T(8,128)(2,1)S(1)} %collective-permute-done.refs_1_, bf16[64,1024]{1,0:T(8,128)(2,1)S(1)} %collective-permute-done.1.refs_2_, bf16[64,1024]{1,0:T(8,128)(2,1)S(1)} %collective-permute-done.2.refs_3_), custom_call_target="tpu_custom_call" | custom-call | tf_op jit(solution)/shard_map/assemble/pallas_call | solution.py:251
Async XLA Ops:
  0.0 1.0 %copy-start = (bf16[64,4096]{1,0:T(8,128)(2,1)S(1)}, bf16[64,4096]{1,0:T(8,128)(2,1)}, u32[]{:S(2)}) copy-start(bf16[64,4096]{1,0:T(8,128)(2,1)} %q_ref.1) | copy-start | bytes 1572868
  1.0 0.8 %copy-start.1 = (bf16[64,512]{1,0:T(8,128)(2,1)S(1)}, bf16[64,512]{1,0:T(8,128)(2,1)}, u32[]{:S(2)}) copy-start(bf16[64,512]{1,0:T(8,128)(2,1)} %k_ref.1) | copy-start | bytes 196612
  1.9 0.8 %copy-start.2 = (bf16[64,512]{1,0:T(8,128)(2,1)S(1)}, bf16[64,512]{1,0:T(8,128)(2,1)}, u32[]{:S(2)}) copy-start(bf16[64,512]{1,0:T(8,128)(2,1)} %v_ref.1) | copy-start | bytes 196612
  2.7 0.7 %copy-start.3 = (s32[1024]{0:T(1024)S(1)}, s32[1024]{0:T(1024)}, u32[]{:S(2)}) copy-start(s32[1024]{0:T(1024)} %param.8) | copy-start | bytes 12292
  4.9 6.6 %copy-start.4 = (s32[1024]{0:T(1024)S(1)}, s32[1024]{0:T(1024)}, u32[]{:S(2)}) copy-start(s32[1024]{0:T(1024)} %param.8) | copy-start | bytes 12292
  4.9 6.6 %copy-start.5 = (s32[4]{0:T(128)S(1)}, s32[4]{0:T(128)}, u32[]{:S(2)}) copy-start(s32[4]{0:T(128)} %lengths_ref.1) | copy-start | bytes 52
  4.9 31.3 %all-to-all-start = ((bf16[16,32,1024]{2,1,0:T(8,128)(2,1)}), bf16[16,32,1024]{2,1,0:T(8,128)(2,1)S(1)}, u32[]{:S(2)}, u32[]{:S(2)}) async-start(bf16[16,32,1024]{2,1,0:T(8,128)(2,1)} %pack.1), calls=%async_computation | async-start | bytes 2097152 | tf_op jit(solution)/shard_map/all_to_all | solution.py:205
  39.1 2.6 %collective-permute-start = (bf16[64,1024]{1,0:T(8,128)(2,1)S(1)}, bf16[64,1024]{1,0:T(8,128)(2,1)S(1)}, u32[]{:S(2)}, u32[]{:S(2)}) collective-permute-start(bf16[64,1024]{1,0:T(8,128)(2,1)S(1)} %get-tuple-element.16), channel_id=1, source_target_pairs={{0,1},{1,0},{2,3},{3,2},{4,5},{5,4},{6,7},{7,6},{8,9},{9,8},{10,11... | collective-permute-start | bytes 393224 | tf_op jit(solution)/shard_map/ppermute | solution.py:250
  40.1 5.1 %collective-permute-start.1 = (bf16[64,1024]{1,0:T(8,128)(2,1)S(1)}, bf16[64,1024]{1,0:T(8,128)(2,1)S(1)}, u32[]{:S(2)}, u32[]{:S(2)}) collective-permute-start(bf16[64,1024]{1,0:T(8,128)(2,1)S(1)} %get-tuple-element.17), channel_id=1, source_target_pairs={{0,2},{1,3},{2,0},{3,1},{4,6},{5,7},{6,4},{7,5},{8,10},{9,11},{10,... | collective-permute-start | bytes 393224 | tf_op jit(solution)/shard_map/ppermute | solution.py:250
  40.1 8.0 %collective-permute-start.2 = (bf16[64,1024]{1,0:T(8,128)(2,1)S(1)}, bf16[64,1024]{1,0:T(8,128)(2,1)S(1)}, u32[]{:S(2)}, u32[]{:S(2)}) collective-permute-start(bf16[64,1024]{1,0:T(8,128)(2,1)S(1)} %get-tuple-element.18), channel_id=1, source_target_pairs={{0,3},{1,2},{2,1},{3,0},{4,7},{5,6},{6,5},{7,4},{8,11},{9,10},{10,... | collective-permute-start | bytes 393224 | tf_op jit(solution)/shard_map/ppermute | solution.py:250

commit v2 on v1

--- a/solution.py
+++ b/solution.py
@@ -17,6 +17,7 @@
 LANES = 128
 TILE = 16
 VMEM = pltpu.CompilerParams(vmem_limit_bytes=40 * 2**20)
+ALL_VMEM = pltpu.CompilerParams(vmem_limit_bytes=64 * 2**20 - 2**17)
 
 
 def row_to_column(row):
@@ -33,9 +34,26 @@
     return jnp.sum(jnp.where(here == there, column, 0), axis=0, keepdims=True)
 
 
-def pack_kernel(levels, per_level, owner_ref, q_ref, k_ref, v_ref, out_ref):
+def pack_kernel(levels, per_level, owner_hbm, q_hbm, k_hbm, v_hbm, out_hbm, *scratch):
+    owner_ref, q_ref, k_ref, v_ref, out_ref, in_sems, q_sems, out_sems = scratch
     me = lax.axis_index("ctx")
     rows = q_ref.shape[0]
+    arrivals = []
+    for index, (source, target) in enumerate(((owner_hbm, owner_ref), (k_hbm, k_ref), (v_hbm, v_ref))):
+        arrivals.append(pltpu.make_async_copy(source, target, in_sems.at[index]))
+    queries = []
+    for member in range(KVH):
+        wide = pl.ds(member * WIDE, WIDE)
+        queries.append(
+            pltpu.make_async_copy(q_hbm.at[:, wide], q_ref.at[:, wide], q_sems.at[member])
+        )
+    arrivals[0].start()
+    queries[0].start()
+    arrivals[1].start()
+    arrivals[2].start()
+    for copy in queries[1:]:
+        copy.start()
+    arrivals[0].wait()
     both = owner_ref[pl.ds(me // 2, 1), :]
     swapped = jnp.concatenate((both[:, rows:], both[:, :rows]), axis=1)
     own = jnp.where(me % 2 == 1, swapped, both)[:, :rows]
@@ -44,11 +62,16 @@
     rank = jnp.sum((row_to_column(key_row) < key_row).astype(jnp.int32), axis=0, keepdims=True)
     place = lax.broadcasted_iota(jnp.int32, (rows, rows), 0)
     order = (place == rank).astype(jnp.float32).astype(jnp.bfloat16)
+    departures = []
     for member in range(KVH):
         wide = slice(member * WIDE, (member + 1) * WIDE)
         head = slice(member * HD, (member + 1) * HD)
+        queries[member].wait()
         sorted_q = jnp.dot(order, q_ref[:, wide], preferred_element_type=jnp.float32)
         sorted_q = sorted_q.astype(jnp.bfloat16)
+        if member == 0:
+            arrivals[1].wait()
+            arrivals[2].wait()
         for level in range(levels):
             dest = level * KVH + member
             part = sorted_q[level * per_level : (level + 1) * per_level]
@@ -60,6 +83,11 @@
                 col = block * 2 * HD
                 out_ref[dest, TILE:, col : col + HD] = k_ref[here, head]
                 out_ref[dest, TILE:, col + HD : col + 2 * HD] = v_ref[here, head]
+            copy = pltpu.make_async_copy(out_ref.at[dest], out_hbm.at[dest], out_sems.at[dest])
+            copy.start()
+            departures.append(copy)
+    for copy in departures:
+        copy.wait()
 
 
 def place_kernel(per_level, lengths_ref, owner_ref, pos_ref, start_ref, order_ref):
@@ -193,13 +221,24 @@
     held = rows * KVH
     table = owner.reshape(total // LANES, LANES)
     whole = pl.BlockSpec(memory_space=pltpu.VMEM)
+    hbm = pl.BlockSpec(memory_space=pltpu.HBM)
 
     packed = pl.pallas_call(
         functools.partial(pack_kernel, levels, per_level),
         out_shape=jax.ShapeDtypeStruct((nodes, 2 * TILE, WIDE), jnp.bfloat16),
-        in_specs=[whole] * 4,
-        out_specs=whole,
-        compiler_params=VMEM,
+        in_specs=[hbm] * 4,
+        out_specs=hbm,
+        scratch_shapes=[
+            pltpu.VMEM(table.shape, jnp.int32),
+            pltpu.VMEM(queries.shape, jnp.bfloat16),
+            pltpu.VMEM(keys.shape, jnp.bfloat16),
+            pltpu.VMEM(values.shape, jnp.bfloat16),
+            pltpu.VMEM((nodes, 2 * TILE, WIDE), jnp.bfloat16),
+            pltpu.SemaphoreType.DMA((3,)),
+            pltpu.SemaphoreType.DMA((KVH,)),
+            pltpu.SemaphoreType.DMA((nodes,)),
+        ],
+        compiler_params=ALL_VMEM,
         name="pack",
     )(table, queries, keys, values)
     moved = lax.all_to_all(packed, "ctx", split_axis=0, concat_axis=0, tiled=True)

time: 49.3 us -> 46.8 us (0.949)
  local copies, waits for them, and re-layouts: 3.41 us -> 0.01 us
  Pallas kernels: 6.98 us -> 8.09 us
    unnamed x12 -> x4, local copies, waits for them, and re-layouts: 3.41 us -> 0.01 us
    pallas_call x1, Pallas kernels: 1.44 us -> 2.56 us  [on_device(): pl.pallas_call(functools.partial(pack_kernel, levels, per_level), out_sha...]
where the time goes in v2:
time: 46.8 us; the launch traced here: 46.6 us
  waiting for transfers between devices  29.3 us (63%)
  starting transfers between devices  9.15 us (20%)
  Pallas kernels  8.09 us (17%)
    all_to_all x1, waiting for transfers between devices, on_device(): lax.all_to_all(packed, 'ctx', split_axis=0, concat_axis=0, tiled=True)  22.9 us
    all_to_all x1, starting transfers between devices, on_device(): lax.all_to_all(packed, 'ctx', split_axis=0, concat_axis=0, tiled=True)  6.5 us
    ppermute x3, waiting for transfers between devices, on_device(): returned.append(lax.ppermute(blocks[index], 'ctx', pairs))  6.33 us
    pallas_call x1, Pallas kernels, on_device(): pl.pallas_call(attend_kernel, grid=(1,), out_shape=tuple((jax.ShapeDtypeS...  2.98 us
    ppermute x3, starting transfers between devices, on_device(): returned.append(lax.ppermute(blocks[index], 'ctx', pairs))  2.65 us
    pallas_call x1, Pallas kernels, on_device(): pl.pallas_call(functools.partial(pack_kernel, levels, per_level), out_sha...  2.56 us
    pallas_call x1, Pallas kernels, on_device(): pl.pallas_call(functools.partial(place_kernel, per_level), out_shape=(jax...  1.72 us
  transfers between devices with their start and end apart: 4, of which 3 were waited for; matrix products, arithmetic and copies ran while one was open for 0% of the time, Pallas kernels for 4%

profile of v2, /device:TPU:17, one launch (start us, length us, event | category | flops | bytes accessed | tf_op | source)
XLA Modules:
  0.0 46.6 jit_solution(13007272499020297857)
XLA Ops:
  0.0 2.6 %pack.1 = bf16[16,32,1024]{2,1,0:T(8,128)(2,1)} custom-call(s32[8,128]{1,0:T(8,128)} %bitcast.1, bf16[64,4096]{1,0:T(8,128)(2,1)} %q_hbm.1, bf16[64,512]{1,0:T(8,128)(2,1)} %k_hbm.1, bf16[64,512]{1,0:T(8,128)(2,1)} %v_hbm.1), custom_call_target="tpu_custom_call" | custom-call | tf_op jit(solution)/shard_map/pack/pallas_call | solution.py:226
  2.6 0.0 copy-start
  2.6 0.0 copy-start.1
  2.6 6.5 %all-to-all-start = ((bf16[16,32,1024]{2,1,0:T(8,128)(2,1)}), bf16[16,32,1024]{2,1,0:T(8,128)(2,1)S(1)}, u32[]{:S(2)}, u32[]{:S(2)}) async-start(bf16[16,32,1024]{2,1,0:T(8,128)(2,1)} %pack.1), calls=%async_computation | async-start | bytes 2097152 | tf_op jit(solution)/shard_map/all_to_all | solution.py:244
  9.1 0.0 copy-done
  9.1 0.0 copy-done.1
  9.1 1.7 %place.1 = (s32[256,128]{1,0:T(8,128)S(1)}, s32[256,128]{1,0:T(8,128)S(1)}, bf16[256,256]{1,0:T(8,128)(2,1)S(1)}) custom-call(s32[4]{0:T(128)S(1)} %copy-done.1, s32[8,128]{1,0:T(8,128)S(1)} %bitcast.2), custom_call_target="tpu_custom_call" | custom-call | tf_op jit(solution)/shard_map/place/pallas_call | solution.py:246
  10.8 22.9 %all-to-all-done.q_ref.kv_ref = bf16[16,32,1024]{2,1,0:T(8,128)(2,1)S(1)} async-done(((bf16[16,32,1024]{2,1,0:T(8,128)(2,1)}), bf16[16,32,1024]{2,1,0:T(8,128)(2,1)S(1)}, u32[]{:S(2)}, u32[]{:S(2)}) %all-to-all-start) | async-done | bytes 1048608 | tf_op jit(solution)/shard_map/all_to_all | solution.py:244
  33.8 3.0 %attend.1 = (bf16[64,1024]{1,0:T(8,128)(2,1)S(1)}, bf16[64,1024]{1,0:T(8,128)(2,1)S(1)}, bf16[64,1024]{1,0:T(8,128)(2,1)S(1)}, bf16[64,1024]{1,0:T(8,128)(2,1)S(1)}) custom-call(bf16[16,32,1024]{2,1,0:T(8,128)(2,1)S(1)} %all-to-all-done.q_ref.kv_ref, bf16[16,32,1024]{2,1,0:T(8,128)(2,1)S(1)} %all-to-all-done.q_ref.kv_ref, ...), custom_call_target="tpu_custom_call" | custom-call | tf_op jit(solution)/shard_map/attend/pallas_call | solution.py:265
  36.7 0.9 %collective-permute-start = (bf16[64,1024]{1,0:T(8,128)(2,1)S(1)}, bf16[64,1024]{1,0:T(8,128)(2,1)S(1)}, u32[]{:S(2)}, u32[]{:S(2)}) collective-permute-start(bf16[64,1024]{1,0:T(8,128)(2,1)S(1)} %get-tuple-element.16), channel_id=1, source_target_pairs={{0,1},{1,0},{2,3},{3,2},{4,5},{5,4},{6,7},{7,6},{8,9},{9,8},{10,11... | collective-permute-start | bytes 393224 | tf_op jit(solution)/shard_map/ppermute | solution.py:289
  37.7 0.0 collective-permute-start.1
  37.7 1.7 %collective-permute-start.2 = (bf16[64,1024]{1,0:T(8,128)(2,1)S(1)}, bf16[64,1024]{1,0:T(8,128)(2,1)S(1)}, u32[]{:S(2)}, u32[]{:S(2)}) collective-permute-start(bf16[64,1024]{1,0:T(8,128)(2,1)S(1)} %get-tuple-element.18), channel_id=1, source_target_pairs={{0,3},{1,2},{2,1},{3,0},{4,7},{5,6},{6,5},{7,4},{8,11},{9,10},{10,... | collective-permute-start | bytes 393224 | tf_op jit(solution)/shard_map/ppermute | solution.py:289
  39.4 0.0 collective-permute-done.refs_1_
  39.4 3.4 %collective-permute-done.1.refs_2_ = bf16[64,1024]{1,0:T(8,128)(2,1)S(1)} collective-permute-done((bf16[64,1024]{1,0:T(8,128)(2,1)S(1)}, bf16[64,1024]{1,0:T(8,128)(2,1)S(1)}, u32[]{:S(2)}, u32[]{:S(2)}) %collective-permute-start.1) | collective-permute-done | bytes 131104 | tf_op jit(solution)/shard_map/ppermute | solution.py:289
  42.8 3.0 %collective-permute-done.2.refs_3_ = bf16[64,1024]{1,0:T(8,128)(2,1)S(1)} collective-permute-done((bf16[64,1024]{1,0:T(8,128)(2,1)S(1)}, bf16[64,1024]{1,0:T(8,128)(2,1)S(1)}, u32[]{:S(2)}, u32[]{:S(2)}) %collective-permute-start.2) | collective-permute-done | bytes 131104 | tf_op jit(solution)/shard_map/ppermute | solution.py:289
  45.7 0.8 %assemble.1 = bf16[64,4096]{1,0:T(8,128)(2,1)} custom-call(bf16[64,1024]{1,0:T(8,128)(2,1)S(1)} %get-tuple-element.15.refs_0_, bf16[64,1024]{1,0:T(8,128)(2,1)S(1)} %collective-permute-done.refs_1_, bf16[64,1024]{1,0:T(8,128)(2,1)S(1)} %collective-permute-done.1.refs_2_, bf16[64,1024]{1,0:T(8,128)(2,1)S(1)} %collective-permute-done.2.refs_3_), custom_call_target="tpu_custom_call" | custom-call | tf_op jit(solution)/shard_map/assemble/pallas_call | solution.py:290
Async XLA Ops:
  2.6 6.5 %copy-start = (s32[1024]{0:T(1024)S(1)}, s32[1024]{0:T(1024)}, u32[]{:S(2)}) copy-start(s32[1024]{0:T(1024)} %param.8) | copy-start | bytes 12292
  2.6 6.5 %copy-start.1 = (s32[4]{0:T(128)S(1)}, s32[4]{0:T(128)}, u32[]{:S(2)}) copy-start(s32[4]{0:T(128)} %lengths_ref.1) | copy-start | bytes 52
  2.6 31.2 %all-to-all-start = ((bf16[16,32,1024]{2,1,0:T(8,128)(2,1)}), bf16[16,32,1024]{2,1,0:T(8,128)(2,1)S(1)}, u32[]{:S(2)}, u32[]{:S(2)}) async-start(bf16[16,32,1024]{2,1,0:T(8,128)(2,1)} %pack.1), calls=%async_computation | async-start | bytes 2097152 | tf_op jit(solution)/shard_map/all_to_all | solution.py:244
  36.7 2.7 %collective-permute-start = (bf16[64,1024]{1,0:T(8,128)(2,1)S(1)}, bf16[64,1024]{1,0:T(8,128)(2,1)S(1)}, u32[]{:S(2)}, u32[]{:S(2)}) collective-permute-start(bf16[64,1024]{1,0:T(8,128)(2,1)S(1)} %get-tuple-element.16), channel_id=1, source_target_pairs={{0,1},{1,0},{2,3},{3,2},{4,5},{5,4},{6,7},{7,6},{8,9},{9,8},{10,11... | collective-permute-start | bytes 393224 | tf_op jit(solution)/shard_map/ppermute | solution.py:289
  37.7 5.1 %collective-permute-start.1 = (bf16[64,1024]{1,0:T(8,128)(2,1)S(1)}, bf16[64,1024]{1,0:T(8,128)(2,1)S(1)}, u32[]{:S(2)}, u32[]{:S(2)}) collective-permute-start(bf16[64,1024]{1,0:T(8,128)(2,1)S(1)} %get-tuple-element.17), channel_id=1, source_target_pairs={{0,2},{1,3},{2,0},{3,1},{4,6},{5,7},{6,4},{7,5},{8,10},{9,11},{10,... | collective-permute-start | bytes 393224 | tf_op jit(solution)/shard_map/ppermute | solution.py:289
  37.7 8.0 %collective-permute-start.2 = (bf16[64,1024]{1,0:T(8,128)(2,1)S(1)}, bf16[64,1024]{1,0:T(8,128)(2,1)S(1)}, u32[]{:S(2)}, u32[]{:S(2)}) collective-permute-start(bf16[64,1024]{1,0:T(8,128)(2,1)S(1)} %get-tuple-element.18), channel_id=1, source_target_pairs={{0,3},{1,2},{2,1},{3,0},{4,7},{5,6},{6,5},{7,4},{8,11},{9,10},{10,... | collective-permute-start | bytes 393224 | tf_op jit(solution)/shard_map/ppermute | solution.py:289

commit v3 on v1

v3 whole, which is shorter than its diff:
```python
import functools
import math

import jax
import jax.numpy as jnp
from jax import lax
from jax.experimental import pallas as pl
from jax.experimental.pallas import tpu as pltpu
from jax.sharding import PartitionSpec as P

H = 32
KVH = 4
HD = 128
GROUP = H // KVH
WIDE = GROUP * HD
CORES = 2
HEADS = KVH // CORES
NEGATIVE = -1e30
LANES = 128
SUB = 8
Q_ROWS = HEADS * SUB
VMEM = pltpu.CompilerParams(vmem_limit_bytes=40 * 2**20)
ALL_VMEM = pltpu.CompilerParams(vmem_limit_bytes=64 * 2**20 - 2**17)


def row_to_column(row):
    size = row.shape[1]
    here = lax.broadcasted_iota(jnp.int32, (size, size), 0)
    there = lax.broadcasted_iota(jnp.int32, (size, size), 1)
    return jnp.sum(jnp.where(here == there, row, 0), axis=1, keepdims=True)


def column_to_row(column):
    size = column.shape[0]
    here = lax.broadcasted_iota(jnp.int32, (size, size), 0)
    there = lax.broadcasted_iota(jnp.int32, (size, size), 1)
    return jnp.sum(jnp.where(here == there, column, 0), axis=0, keepdims=True)


def pack_kernel(chips, owner_hbm, q_hbm, *refs):
    with_kv = len(refs) > 6
    kv_hbm, refs = (refs[:2], refs[2:]) if with_kv else ((), refs)
    out_hbm, owner_ref, q_ref, out_ref, in_sems, out_sems = refs[:6]
    kv_refs = refs[6:]
    me = lax.axis_index("ctx")
    rows = q_ref.shape[0]
    per_chip = rows // chips
    first = pltpu.make_async_copy(owner_hbm, owner_ref, in_sems.at[KVH])
    queries = []
    for head in range(KVH):
        wide = pl.ds(head * WIDE, WIDE)
        queries.append(pltpu.make_async_copy(q_hbm.at[:, wide], q_ref.at[:, wide], in_sems.at[head]))
    arrivals = []
    for index, (source, target) in enumerate(zip(kv_hbm, kv_refs)):
        arrivals.append(pltpu.make_async_copy(source, target, in_sems.at[KVH + 1 + index]))
    for copy in [first] + queries + arrivals:
        copy.start()
    first.wait()
    both = owner_ref[pl.ds(me // 2, 1), :]
    swapped = jnp.concatenate((both[:, rows:], both[:, :rows]), axis=1)
    own = jnp.where(me % 2 == 1, swapped, both)[:, :rows]
    token = lax.broadcasted_iota(jnp.int32, (1, rows), 1)
    key_row = own * rows + token
    rank = jnp.sum((row_to_column(key_row) < key_row).astype(jnp.int32), axis=0, keepdims=True)
    place = lax.broadcasted_iota(jnp.int32, (rows, rows), 0)
    order = (place == rank).astype(jnp.float32).astype(jnp.bfloat16)
    for copy in arrivals:
        copy.wait()
    departures = []
    for core in range(CORES):
        sorted_q = []
        for head in range(core * HEADS, (core + 1) * HEADS):
            queries[head].wait()
            wide = slice(head * WIDE, (head + 1) * WIDE)
            sorted_q.append(jnp.dot(order, q_ref[:, wide], preferred_element_type=jnp.float32))
        for chip in range(chips):
            dest = chip * CORES + core
            parts = []
            for array in sorted_q:
                parts.append(array[chip * per_chip : (chip + 1) * per_chip])
                if per_chip < SUB:
                    parts.append(jnp.zeros((SUB - per_chip, WIDE), jnp.float32))
            out_ref[dest, :Q_ROWS, :] = jnp.concatenate(parts, axis=0).astype(jnp.bfloat16)
            if with_kv:
                width = HEADS * HD
                side = slice(core * width, (core + 1) * width)
                half = rows // 2
                for part in range(2):
                    here = slice(part * half, (part + 1) * half)
                    for index in range(2):
                        col = (2 * part + index) * width
                        out_ref[dest, Q_ROWS:, col : col + width] = kv_refs[index][here, side]
            copy = pltpu.make_async_copy(out_ref.at[dest], out_hbm.at[dest], out_sems.at[dest])
            copy.start()
            departures.append(copy)
    for copy in departures:
        copy.wait()


def join_kernel(k_hbm, v_hbm, out_ref, sems):
    width = k_hbm.shape[1]
    copies = [
        pltpu.make_async_copy(k_hbm, out_ref.at[:, pl.ds(0, width)], sems.at[0]),
        pltpu.make_async_copy(v_hbm, out_ref.at[:, pl.ds(width, width)], sems.at[1]),
    ]
    for copy in copies:
        copy.start()
    for copy in copies:
        copy.wait()


def heads_kernel(*refs):
    lanes, outs = refs[:-CORES], refs[-CORES:]
    core = lax.axis_index("ctx") % CORES
    rows = lanes[0].shape[0]
    width = HEADS * HD
    for index in range(CORES):
        col = jnp.bitwise_xor(core, index) * width
        for lane, ref in enumerate(lanes):
            here = slice(lane * rows, (lane + 1) * rows)
            for half in range(2):
                side = pl.ds(pl.multiple_of(col + half * KVH * HD, width), width)
                outs[index][here, half * width : (half + 1) * width] = ref[:, side]


def place_kernel(per_chip, lengths_ref, owner_ref, pos_ref, start_ref, order_ref):
    me = lax.axis_index("ctx")
    chip, core = me // CORES, me % CORES
    table_rows = owner_ref.shape[0]
    total = table_rows * LANES
    held = pos_ref.shape[0]
    rows = LANES // 2
    shift = per_chip.bit_length() - 1
    block_rows = 32
    table_step = table_rows // (held // block_rows)
    first = lax.broadcasted_iota(jnp.int32, (LANES, LANES), 0)
    second = lax.broadcasted_iota(jnp.int32, (LANES, LANES), 1)
    same = (first < rows) == (second < rows)
    lane = lax.broadcasted_iota(jnp.int32, (1, LANES), 1)
    line = lax.broadcasted_iota(jnp.int32, (block_rows, 1), 0)
    wanted = chip * per_chip + jnp.bitwise_and(line, per_chip - 1)
    source = jnp.right_shift(line, shift)
    keys = []
    for block in range(held // block_rows):
        pos = jnp.zeros((block_rows, 1), jnp.int32)
        own = jnp.zeros((block_rows, 1), jnp.int32)
        for step in range(table_step):
            table = block * table_step + step
            owners = owner_ref[table : table + 1, :]
            key_row = owners * LANES + lane
            below = same & (row_to_column(key_row) < key_row)
            rank = jnp.sum(below.astype(jnp.int32), axis=0, keepdims=True)
            lane_source = 2 * step + (lane >= rows).astype(jnp.int32)
            hit = (wanted == rank) & (source == lane_source)
            pos += jnp.sum(jnp.where(hit, lane + table * LANES, 0), axis=1, keepdims=True)
            own += jnp.sum(jnp.where(hit, owners, 0), axis=1, keepdims=True)
        start = jnp.zeros((block_rows, 1), jnp.int32)
        end = jnp.int32(0)
        for rollout in range(lengths_ref.shape[0]):
            end = end + lengths_ref[rollout]
            start = jnp.where(pos >= end, end, start)
        here = slice(block * block_rows, (block + 1) * block_rows)
        pos_ref[here, :] = jnp.broadcast_to(pos, (block_rows, LANES))
        start_ref[here, :] = jnp.broadcast_to(start, (block_rows, LANES))
        keys.append((own - chip * CORES) * total + pos)
    key_col = jnp.concatenate(keys, axis=0)
    key_row = column_to_row(key_col)
    slot = jnp.sum((key_col < key_row).astype(jnp.int32), axis=0, keepdims=True)
    slot = jnp.bitwise_xor(slot, core * rows)
    place = lax.broadcasted_iota(jnp.int32, (held, held), 0)
    order_ref[...] = (place == slot).astype(jnp.float32).astype(jnp.bfloat16)


def unpack_moved(moved_ref, k_all, v_all):
    nodes = moved_ref.shape[0]
    tokens = k_all.shape[0] // nodes
    half = tokens // 2
    width = HEADS * HD

    def unpack(node, carry):
        for part in range(2):
            row = pl.ds(pl.multiple_of(node * tokens + part * half, half), half)
            col = 2 * part * width
            k_all[row, :] = moved_ref[node, Q_ROWS:, col : col + width]
            for head in range(HEADS):
                at = col + width + head * HD
                v_all[row, 2 * head * HD : (2 * head + 1) * HD] = moved_ref[node, Q_ROWS:, at : at + HD]
        return carry

    lax.fori_loop(0, nodes, unpack, 0)


def unpack_pieces(pieces, tokens, k_all, v_all):
    me = lax.axis_index("ctx")
    width = HEADS * HD
    for index, ref in enumerate(pieces):
        for lane in range(ref.shape[0] // tokens):
            node = jnp.bitwise_xor(me, index ^ (lane * len(pieces)))
            row = pl.ds(pl.multiple_of(node * tokens, tokens), tokens)
            here = slice(lane * tokens, (lane + 1) * tokens)
            k_all[row, :] = ref[here, :width]
            for head in range(HEADS):
                at = width + head * HD
                v_all[row, 2 * head * HD : (2 * head + 1) * HD] = ref[here, at : at + HD]


def attend_kernel(q_ref, pos_ref, start_ref, order_ref, *refs):
    kv_refs, refs = refs[: -CORES - 3], refs[-CORES - 3 :]
    out_refs, (k_all, v_all, context) = refs[:CORES], refs[CORES:]
    total = k_all.shape[0]
    held = context.shape[0]
    block_rows = 32
    blocks = held // block_rows
    span = total // blocks
    scale = math.log2(math.e) / math.sqrt(HD)

    for head in range(HEADS):
        v_all[:, (2 * head + 1) * HD : (2 * head + 2) * HD] = jnp.ones((total, HD), jnp.bfloat16)
    if len(kv_refs) == 1:
        unpack_moved(kv_refs[0], k_all, v_all)
    else:
        unpack_pieces(kv_refs, held // CORES, k_all, v_all)

    for block in range(blocks):
        here = slice(block * block_rows, (block + 1) * block_rows)
        parts = block_rows // SUB
        messages = [q_ref[block * parts + part].astype(jnp.float32) for part in range(parts)]
        pos = pos_ref[here, :1]
        start = start_ref[here, :1]
        low, high = max(0, block - blocks // 2) * span, (block + 1) * span
        chunk = min(high - low, 1024)
        for head in range(HEADS):
            pieces = []
            for group in range(GROUP):
                for message in messages:
                    rows = slice(head * SUB, (head + 1) * SUB)
                    pieces.append(message[rows, group * HD : (group + 1) * HD])
            queries = jnp.concatenate(pieces, axis=0).astype(jnp.bfloat16)
            peak, acc = None, None
            for lower in range(low, high, chunk):
                keys = slice(lower, lower + chunk)
                scores = lax.dot_general(
                    queries,
                    k_all[keys, head * HD : (head + 1) * HD],
                    (((1,), (1,)), ((), ())),
                    preferred_element_type=jnp.float32,
                )
                at = lower + lax.broadcasted_iota(jnp.int32, (block_rows, chunk), 1)
                seen = (at <= pos) & (at >= start)
                bias = jnp.where(seen, 0.0, NEGATIVE)
                scores = scores.reshape(GROUP, block_rows, chunk) + bias[None]
                scores = scores.reshape(GROUP * block_rows, chunk)
                top = jnp.max(scores, axis=1, keepdims=True)
                if peak is not None:
                    top = jnp.maximum(peak, top)
                probs = jnp.exp2((scores - top) * scale)
                if chunk != high - low:
                    probs = probs.reshape(GROUP, block_rows, chunk)
                    probs = jnp.where(seen[None], probs, 0.0).reshape(GROUP * block_rows, chunk)
                new = jnp.dot(
                    probs.astype(jnp.bfloat16),
                    v_all[keys, 2 * head * HD : (2 * head + 2) * HD],
                    preferred_element_type=jnp.float32,
                )
                acc = new if acc is None else acc * jnp.exp2((peak - top) * scale) + new
                peak = top
            result = (acc[:, :HD] / acc[:, HD:]).astype(jnp.bfloat16)
            for group in range(GROUP):
                col = head * WIDE + group * HD
                context[here, col : col + HD] = result[group * block_rows : (group + 1) * block_rows]
    rows = held // CORES
    for core in range(CORES):
        order = order_ref[core * rows : (core + 1) * rows, :]
        moved = jnp.dot(order, context[...], preferred_element_type=jnp.float32)
        out_refs[core][...] = moved.astype(jnp.bfloat16)


def assemble_kernel(*refs):
    core = lax.axis_index("ctx") % CORES
    width = HEADS * WIDE
    for index in range(CORES):
        col = pl.multiple_of(jnp.bitwise_xor(core, index) * width, width)
        refs[CORES][:, pl.ds(col, width)] = refs[index][...]


def on_device(queries, keys, values, owner, rollout_lengths):
    rows = queries.shape[0]
    nodes = lax.axis_size("ctx")
    total = owner.shape[0]
    chips = nodes // CORES
    per_chip = rows // chips
    held = rows * CORES
    table = owner.reshape(total // LANES, LANES)
    whole = pl.BlockSpec(memory_space=pltpu.VMEM)
    hbm = pl.BlockSpec(memory_space=pltpu.HBM)
    near = 4
    apart = nodes == 4 * near

    def swap(array, offset):
        return lax.ppermute(array, "ctx", [(node, node ^ offset) for node in range(nodes)])

    if apart:
        joined = pl.pallas_call(
            join_kernel,
            out_shape=jax.ShapeDtypeStruct((rows, 2 * KVH * HD), jnp.bfloat16),
            in_specs=[hbm] * 2,
            out_specs=whole,
            scratch_shapes=[pltpu.SemaphoreType.DMA((2,))],
            compiler_params=ALL_VMEM,
            name="join",
        )(keys, values)
        lanes = [joined] + [swap(joined, offset) for offset in range(near, nodes, near)]

    kv_rows = 0 if apart else rows // 2
    message = (nodes, Q_ROWS + kv_rows, WIDE)
    kv_scratch = [pltpu.VMEM(keys.shape, jnp.bfloat16), pltpu.VMEM(values.shape, jnp.bfloat16)]
    operands = (table, queries) if apart else (table, queries, keys, values)
    packed = pl.pallas_call(
        functools.partial(pack_kernel, chips),
        out_shape=jax.ShapeDtypeStruct(message, jnp.bfloat16),
        in_specs=[hbm] * len(operands),
        out_specs=hbm,
        scratch_shapes=[
            pltpu.VMEM(table.shape, jnp.int32),
            pltpu.VMEM(queries.shape, jnp.bfloat16),
            pltpu.VMEM(message, jnp.bfloat16),
            pltpu.SemaphoreType.DMA((KVH + 3,)),
            pltpu.SemaphoreType.DMA((nodes,)),
        ]
        + ([] if apart else kv_scratch),
        compiler_params=ALL_VMEM,
        cost_estimate=pl.CostEstimate(
            flops=2 * rows * rows * H * HD, bytes_accessed=4 * rows * H * HD, transcendentals=0
        ),
        name="pack",
    )(*operands)
    moved = lax.all_to_all(packed, "ctx", split_axis=0, concat_axis=0, tiled=True)

    if apart:
        mine, others = pl.pallas_call(
            heads_kernel,
            out_shape=(jax.ShapeDtypeStruct((near * rows, 2 * HEADS * HD), jnp.bfloat16),) * CORES,
            in_specs=[whole] * len(lanes),
            out_specs=(whole,) * CORES,
            compiler_params=VMEM,
            cost_estimate=pl.CostEstimate(
                flops=2 * 10**10, bytes_accessed=64 * 2**20, transcendentals=0
            ),
            name="heads",
        )(*lanes)
        kv_parts = [mine, swap(others, 1), swap(mine, 2), swap(others, 3)]
        q_part = moved
    else:
        kv_parts = [moved]
        groups = held // SUB
        q_part = moved[:, :Q_ROWS].reshape(groups, nodes // groups, HEADS, SUB, WIDE)[:, :, :, :per_chip]
        q_part = q_part.transpose(0, 2, 1, 3, 4).reshape(groups, Q_ROWS, WIDE)

    pos, start, order = pl.pallas_call(
        functools.partial(place_kernel, per_chip),
        out_shape=(
            jax.ShapeDtypeStruct((held, LANES), jnp.int32),
            jax.ShapeDtypeStruct((held, LANES), jnp.int32),
            jax.ShapeDtypeStruct((held, held), jnp.bfloat16),
        ),
        in_specs=[pl.BlockSpec(memory_space=pltpu.SMEM), whole],
        out_specs=(whole, whole, whole),
        compiler_params=VMEM,
        name="place",
    )(rollout_lengths, table)

    own, other = pl.pallas_call(
        attend_kernel,
        out_shape=(jax.ShapeDtypeStruct((rows, HEADS * WIDE), jnp.bfloat16),) * CORES,
        in_specs=[whole] * (4 + len(kv_parts)),
        out_specs=(whole,) * CORES,
        scratch_shapes=[
            pltpu.VMEM((total, HEADS * HD), jnp.bfloat16),
            pltpu.VMEM((total, HEADS * 2 * HD), jnp.bfloat16),
            pltpu.VMEM((held, HEADS * WIDE), jnp.bfloat16),
        ],
        compiler_params=VMEM,
        name="attend",
    )(q_part, pos, start, order, *kv_parts)

    return pl.pallas_call(
        assemble_kernel,
        out_shape=jax.ShapeDtypeStruct((rows, H * HD), jnp.bfloat16),
        in_specs=[whole] * CORES,
        out_specs=whole,
        compiler_params=VMEM,
        name="assemble",
    )(own, swap(other, 1))


def solution(mesh):
    placed = (
        P(("groups", "ctx"), None),
        P(("groups", "ctx"), None),
        P(("groups", "ctx"), None),
        P("groups"),
        P("groups"),
    )
    return jax.shard_map(
        on_device, mesh=mesh, in_specs=placed, out_specs=P(("groups", "ctx"), None), check_vma=False
    )
```

time: 49.3 us -> 41.2 us (0.84)
  the two profiles are of different devices: /device:TPU:17 before, /device:TPU:0 now
where the time goes in v3:
time: 41.2 us; the launch traced here: 40.9 us
  waiting for transfers between devices  16.8 us (41%)
  starting transfers between devices  14.1 us (34%)
  Pallas kernels  9.93 us (24%)
    ppermute x7, waiting for transfers between devices, swap(): lax.ppermute(array, 'ctx', [(node, node ^ offset) for node in range(nodes)])  16.8 us
    ppermute x7, starting transfers between devices, swap(): lax.ppermute(array, 'ctx', [(node, node ^ offset) for node in range(nodes)])  7.83 us
    all_to_all x1, starting transfers between devices, on_device(): lax.all_to_all(packed, 'ctx', split_axis=0, concat_axis=0, tiled=True)  6.3 us
    pallas_call x1, Pallas kernels, on_device(): pl.pallas_call(functools.partial(pack_kernel, chips), out_shape=jax.Shape...  2.47 us
    pallas_call x1, Pallas kernels, on_device(): pl.pallas_call(attend_kernel, out_shape=(jax.ShapeDtypeStruct((rows, HEAD...  2.4 us
    pallas_call x1, Pallas kernels, on_device(): pl.pallas_call(functools.partial(place_kernel, per_chip), out_shape=(jax....  1.57 us
    pallas_call x1, Pallas kernels, on_device(): pl.pallas_call(join_kernel, out_shape=jax.ShapeDtypeStruct((rows, 2 * KVH...  1.54 us
    pallas_call x1, Pallas kernels, on_device(): pl.pallas_call(heads_kernel, out_shape=(jax.ShapeDtypeStruct((near * rows...  1.11 us
  transfers between devices with their start and end apart: 8, of which 4 were waited for; matrix products, arithmetic and copies ran while one was open for 0% of the time, Pallas kernels for 13%

profile of v3, /device:TPU:0, one launch (start us, length us, event | category | flops | bytes accessed | tf_op | source)
XLA Modules:
  0.0 40.9 jit_solution(5371101833631536543)
XLA Ops:
  0.0 1.5 %join.1.refs_0_ = bf16[64,1024]{1,0:T(8,128)(2,1)} custom-call(bf16[64,512]{1,0:T(8,128)(2,1)} %k_hbm.1, bf16[64,512]{1,0:T(8,128)(2,1)} %v_hbm.1), custom_call_target="tpu_custom_call" | custom-call | tf_op jit(solution)/shard_map/join/pallas_call | solution.py:303
  1.5 3.1 %collective-permute-start = (bf16[64,1024]{1,0:T(8,128)(2,1)}, bf16[64,1024]{1,0:T(8,128)(2,1)}, u32[]{:S(2)}, u32[]{:S(2)}) collective-permute-start(bf16[64,1024]{1,0:T(8,128)(2,1)} %join.1.refs_0_), channel_id=1, source_target_pairs={{0,4},{1,5},{2,6},{3,7},{4,0},{5,1},{6,2},{7,3},{8,12},{9,13},{10,... | collective-permute-start | bytes 393224 | tf_op jit(solution)/shard_map/ppermute | solution.py:300
  4.6 2.6 %collective-permute-start.1 = (bf16[64,1024]{1,0:T(8,128)(2,1)}, bf16[64,1024]{1,0:T(8,128)(2,1)}, u32[]{:S(2)}, u32[]{:S(2)}) collective-permute-start(bf16[64,1024]{1,0:T(8,128)(2,1)} %join.1.refs_0_), channel_id=1, source_target_pairs={{0,8},{1,9},{2,10},{3,11},{4,12},{5,13},{6,14},{7,15},{8,0},{9,1},... | collective-permute-start | bytes 393224 | tf_op jit(solution)/shard_map/ppermute | solution.py:300
  7.2 0.0 collective-permute-start.2
  7.2 2.5 %pack.1 = bf16[16,16,1024]{2,1,0:T(8,128)(2,1)} custom-call(s32[8,128]{1,0:T(8,128)} %bitcast.1, bf16[64,4096]{1,0:T(8,128)(2,1)} %q_hbm.1), custom_call_target="tpu_custom_call" | custom-call | flops 33554432 | bytes 1048576 | tf_op jit(solution)/shard_map/pack/pallas_call | solution.py:318
  9.7 0.0 copy-start
  9.7 6.3 %all-to-all-start = ((bf16[16,16,1024]{2,1,0:T(8,128)(2,1)}), bf16[16,16,1024]{2,1,0:T(8,128)(2,1)S(1)}, u32[]{:S(2)}, u32[]{:S(2)}) async-start(bf16[16,16,1024]{2,1,0:T(8,128)(2,1)} %pack.1), calls=%async_computation | async-start | bytes 1048576 | tf_op jit(solution)/shard_map/all_to_all | solution.py:337
  16.0 0.0 collective-permute-done.refs_1_
  16.0 1.9 %collective-permute-done.1.refs_2_ = bf16[64,1024]{1,0:T(8,128)(2,1)} collective-permute-done((bf16[64,1024]{1,0:T(8,128)(2,1)}, bf16[64,1024]{1,0:T(8,128)(2,1)}, u32[]{:S(2)}, u32[]{:S(2)}) %collective-permute-start.1) | collective-permute-done | bytes 131104 | tf_op jit(solution)/shard_map/ppermute | solution.py:300
  17.9 0.0 collective-permute-done.2.refs_3_
  17.9 0.0 copy-done
  17.9 0.0 copy-start.1
  17.9 1.1 %heads.1 = (bf16[256,512]{1,0:T(8,128)(2,1)S(1)}, bf16[256,512]{1,0:T(8,128)(2,1)S(1)}) custom-call(bf16[64,1024]{1,0:T(8,128)(2,1)S(1)} %copy-done, bf16[64,1024]{1,0:T(8,128)(2,1)} %collective-permute-done.refs_1_, bf16[64,1024]{1,0:T(8,128)(2,1)} %collective-permute-done.1.refs_2_, bf16[64,1024]{1,0:T(8,128)(2,1)} %collective-permute-done.2.refs_3_), custom_call_target="tpu_custom_call" | custom-call | flops 20000000000 | bytes 67108864 | tf_op jit(solution)/shard_map/heads/pallas_call | solution.py:340
  19.0 0.0 copy-start.2
  19.0 0.1 collective-permute-start.3
  19.1 1.6 %collective-permute-start.4 = (bf16[256,512]{1,0:T(8,128)(2,1)S(1)}, bf16[256,512]{1,0:T(8,128)(2,1)S(1)}, u32[]{:S(2)}, u32[]{:S(2)}) collective-permute-start(bf16[256,512]{1,0:T(8,128)(2,1)S(1)} %get-tuple-element.15.refs_0_), channel_id=1, source_target_pairs={{0,2},{1,3},{2,0},{3,1},{4,6},{5,7},{6,4},{7,5},{8,10},{9,11},{10,... | collective-permute-start | bytes 786440 | tf_op jit(solution)/shard_map/ppermute | solution.py:300
  20.7 0.3 collective-permute-start.5
  21.0 0.0 copy-done.1
  21.0 0.0 copy-done.2
  21.0 1.6 %place.1 = (s32[128,128]{1,0:T(8,128)S(1)}, s32[128,128]{1,0:T(8,128)S(1)}, bf16[128,128]{1,0:T(8,128)(2,1)S(1)}) custom-call(s32[4]{0:T(128)S(1)} %copy-done.2, s32[8,128]{1,0:T(8,128)S(1)} %bitcast.2), custom_call_target="tpu_custom_call" | custom-call | tf_op jit(solution)/shard_map/place/pallas_call | solution.py:359
  22.6 0.0 collective-permute-done.3.refs_1_
  22.6 8.5 %collective-permute-done.4.refs_2_ = bf16[256,512]{1,0:T(8,128)(2,1)S(1)} collective-permute-done((bf16[256,512]{1,0:T(8,128)(2,1)S(1)}, bf16[256,512]{1,0:T(8,128)(2,1)S(1)}, u32[]{:S(2)}, u32[]{:S(2)}) %collective-permute-start.4) | collective-permute-done | bytes 262176 | tf_op jit(solution)/shard_map/ppermute | solution.py:300
  31.1 5.0 %collective-permute-done.5.refs_3_ = bf16[256,512]{1,0:T(8,128)(2,1)S(1)} collective-permute-done((bf16[256,512]{1,0:T(8,128)(2,1)S(1)}, bf16[256,512]{1,0:T(8,128)(2,1)S(1)}, u32[]{:S(2)}, u32[]{:S(2)}) %collective-permute-start.5) | collective-permute-done | bytes 262176 | tf_op jit(solution)/shard_map/ppermute | solution.py:300
  36.1 0.0 all-to-all-done.q_ref
  36.1 2.4 %attend.1 = (bf16[64,2048]{1,0:T(8,128)(2,1)S(1)}, bf16[64,2048]{1,0:T(8,128)(2,1)S(1)}) custom-call(bf16[16,16,1024]{2,1,0:T(8,128)(2,1)S(1)} %all-to-all-done.q_ref, s32[128,128]{1,0:T(8,128)S(1)} %get-tuple-element.12.pos_ref, s32[128,128]{1,0:T(8,128)S(1)} %get-tuple-element.13.start_ref, bf16[128,128]{1,0:T(8,128)(2,1)S(1)} %get-tuple-element.14.order_ref, ...), custom_call_target="tpu_custom_call" | custom-call | tf_op jit(solution)/shard_map/attend/pallas_call | solution.py:372
  38.5 0.2 collective-permute-start.6
  38.7 1.4 %collective-permute-done.6.refs_1_ = bf16[64,2048]{1,0:T(8,128)(2,1)S(1)} collective-permute-done((bf16[64,2048]{1,0:T(8,128)(2,1)S(1)}, bf16[64,2048]{1,0:T(8,128)(2,1)S(1)}, u32[]{:S(2)}, u32[]{:S(2)}) %collective-permute-start.6) | collective-permute-done | bytes 262176 | tf_op jit(solution)/shard_map/ppermute | solution.py:300
  40.1 0.8 %assemble.1 = bf16[64,4096]{1,0:T(8,128)(2,1)} custom-call(bf16[64,2048]{1,0:T(8,128)(2,1)S(1)} %get-tuple-element.17.refs_0_, bf16[64,2048]{1,0:T(8,128)(2,1)S(1)} %collective-permute-done.6.refs_1_), custom_call_target="tpu_custom_call" | custom-call | tf_op jit(solution)/shard_map/assemble/pallas_call | solution.py:386
Async XLA Ops:
  1.5 14.5 %collective-permute-start = (bf16[64,1024]{1,0:T(8,128)(2,1)}, bf16[64,1024]{1,0:T(8,128)(2,1)}, u32[]{:S(2)}, u32[]{:S(2)}) collective-permute-start(bf16[64,1024]{1,0:T(8,128)(2,1)} %join.1.refs_0_), channel_id=1, source_target_pairs={{0,4},{1,5},{2,6},{3,7},{4,0},{5,1},{6,2},{7,3},{8,12},{9,13},{10,... | collective-permute-start | bytes 393224 | tf_op jit(solution)/shard_map/ppermute | solution.py:300
  4.6 13.3 %collective-permute-start.1 = (bf16[64,1024]{1,0:T(8,128)(2,1)}, bf16[64,1024]{1,0:T(8,128)(2,1)}, u32[]{:S(2)}, u32[]{:S(2)}) collective-permute-start(bf16[64,1024]{1,0:T(8,128)(2,1)} %join.1.refs_0_), channel_id=1, source_target_pairs={{0,8},{1,9},{2,10},{3,11},{4,12},{5,13},{6,14},{7,15},{8,0},{9,1},... | collective-permute-start | bytes 393224 | tf_op jit(solution)/shard_map/ppermute | solution.py:300
  7.2 10.7 %collective-permute-start.2 = (bf16[64,1024]{1,0:T(8,128)(2,1)}, bf16[64,1024]{1,0:T(8,128)(2,1)}, u32[]{:S(2)}, u32[]{:S(2)}) collective-permute-start(bf16[64,1024]{1,0:T(8,128)(2,1)} %join.1.refs_0_), channel_id=1, source_target_pairs={{0,12},{1,13},{2,14},{3,15},{4,8},{5,9},{6,10},{7,11},{8,4},{9,5},... | collective-permute-start | bytes 393224 | tf_op jit(solution)/shard_map/ppermute | solution.py:300
  9.7 8.2 %copy-start = (bf16[64,1024]{1,0:T(8,128)(2,1)S(1)}, bf16[64,1024]{1,0:T(8,128)(2,1)}, u32[]{:S(2)}) copy-start(bf16[64,1024]{1,0:T(8,128)(2,1)} %join.1.refs_0_) | copy-start | bytes 393220
  9.7 26.4 %all-to-all-start = ((bf16[16,16,1024]{2,1,0:T(8,128)(2,1)}), bf16[16,16,1024]{2,1,0:T(8,128)(2,1)S(1)}, u32[]{:S(2)}, u32[]{:S(2)}) async-start(bf16[16,16,1024]{2,1,0:T(8,128)(2,1)} %pack.1), calls=%async_computation | async-start | bytes 1048576 | tf_op jit(solution)/shard_map/all_to_all | solution.py:337
  17.9 3.1 %copy-start.1 = (s32[1024]{0:T(1024)S(1)}, s32[1024]{0:T(1024)}, u32[]{:S(2)}) copy-start(s32[1024]{0:T(1024)} %param.8) | copy-start | bytes 12292
  19.0 2.0 %copy-start.2 = (s32[4]{0:T(128)S(1)}, s32[4]{0:T(128)}, u32[]{:S(2)}) copy-start(s32[4]{0:T(128)} %lengths_ref.1) | copy-start | bytes 52
  19.0 3.5 %collective-permute-start.3 = (bf16[256,512]{1,0:T(8,128)(2,1)S(1)}, bf16[256,512]{1,0:T(8,128)(2,1)S(1)}, u32[]{:S(2)}, u32[]{:S(2)}) collective-permute-start(bf16[256,512]{1,0:T(8,128)(2,1)S(1)} %get-tuple-element.16), channel_id=1, source_target_pairs={{0,1},{1,0},{2,3},{3,2},{4,5},{5,4},{6,7},{7,6},{8,9},{9,8},{10,11... | collective-permute-start | bytes 786440 | tf_op jit(solution)/shard_map/ppermute | solution.py:300
  19.1 12.0 %collective-permute-start.4 = (bf16[256,512]{1,0:T(8,128)(2,1)S(1)}, bf16[256,512]{1,0:T(8,128)(2,1)S(1)}, u32[]{:S(2)}, u32[]{:S(2)}) collective-permute-start(bf16[256,512]{1,0:T(8,128)(2,1)S(1)} %get-tuple-element.15.refs_0_), channel_id=1, source_target_pairs={{0,2},{1,3},{2,0},{3,1},{4,6},{5,7},{6,4},{7,5},{8,10},{9,11},{10,... | collective-permute-start | bytes 786440 | tf_op jit(solution)/shard_map/ppermute | solution.py:300
  20.7 15.4 %collective-permute-start.5 = (bf16[256,512]{1,0:T(8,128)(2,1)S(1)}, bf16[256,512]{1,0:T(8,128)(2,1)S(1)}, u32[]{:S(2)}, u32[]{:S(2)}) collective-permute-start(bf16[256,512]{1,0:T(8,128)(2,1)S(1)} %get-tuple-element.16), channel_id=1, source_target_pairs={{0,3},{1,2},{2,1},{3,0},{4,7},{5,6},{6,5},{7,4},{8,11},{9,10},{10,... | collective-permute-start | bytes 786440 | tf_op jit(solution)/shard_map/ppermute | solution.py:300
  38.5 1.6 %collective-permute-start.6 = (bf16[64,2048]{1,0:T(8,128)(2,1)S(1)}, bf16[64,2048]{1,0:T(8,128)(2,1)S(1)}, u32[]{:S(2)}, u32[]{:S(2)}) collective-permute-start(bf16[64,2048]{1,0:T(8,128)(2,1)S(1)} %get-tuple-element.18), channel_id=1, source_target_pairs={{0,1},{1,0},{2,3},{3,2},{4,5},{5,4},{6,7},{7,6},{8,9},{9,8},{10,11... | collective-permute-start | bytes 786440 | tf_op jit(solution)/shard_map/ppermute | solution.py:300

commit v4 on v3

--- a/solution.py
+++ b/solution.py
@@ -97,6 +97,10 @@
         copy.wait()
 
 
+def block_offsets(nodes):
+    return [0, CORES] + list(range(2 * CORES, nodes, 2 * CORES))
+
+
 def join_kernel(k_hbm, v_hbm, out_ref, sems):
     width = k_hbm.shape[1]
     copies = [
@@ -110,17 +114,19 @@
 
 
 def heads_kernel(*refs):
-    lanes, outs = refs[:-CORES], refs[-CORES:]
+    lanes, near, far = refs[: -2 * CORES], refs[-2 * CORES : -CORES], refs[-CORES:]
     core = lax.axis_index("ctx") % CORES
     rows = lanes[0].shape[0]
     width = HEADS * HD
     for index in range(CORES):
         col = jnp.bitwise_xor(core, index) * width
         for lane, ref in enumerate(lanes):
-            here = slice(lane * rows, (lane + 1) * rows)
             for half in range(2):
-                side = pl.ds(pl.multiple_of(col + half * KVH * HD, width), width)
-                outs[index][here, half * width : (half + 1) * width] = ref[:, side]
+                block = ref[:, pl.ds(pl.multiple_of(col + half * KVH * HD, width), width)]
+                side = slice(half * width, (half + 1) * width)
+                near[index][lane * rows : (lane + 1) * rows, side] = block
+                if lane >= 2:
+                    far[index][(lane - 2) * rows : (lane - 1) * rows, side] = block
 
 
 def place_kernel(per_chip, lengths_ref, owner_ref, pos_ref, start_ref, order_ref):
@@ -192,10 +198,12 @@
 
 def unpack_pieces(pieces, tokens, k_all, v_all):
     me = lax.axis_index("ctx")
+    offsets = block_offsets(k_all.shape[0] // tokens)
     width = HEADS * HD
     for index, ref in enumerate(pieces):
-        for lane in range(ref.shape[0] // tokens):
-            node = jnp.bitwise_xor(me, index ^ (lane * len(pieces)))
+        held = offsets if index < CORES else offsets[2:]
+        for lane, offset in enumerate(held):
+            node = jnp.bitwise_xor(me, index ^ offset)
             row = pl.ds(pl.multiple_of(node * tokens, tokens), tokens)
             here = slice(lane * tokens, (lane + 1) * tokens)
             k_all[row, :] = ref[here, :width]
@@ -293,8 +301,7 @@
     table = owner.reshape(total // LANES, LANES)
     whole = pl.BlockSpec(memory_space=pltpu.VMEM)
     hbm = pl.BlockSpec(memory_space=pltpu.HBM)
-    near = 4
-    apart = nodes == 4 * near
+    apart = nodes == 16
 
     def swap(array, offset):
         return lax.ppermute(array, "ctx", [(node, node ^ offset) for node in range(nodes)])
@@ -309,7 +316,8 @@
             compiler_params=ALL_VMEM,
             name="join",
         )(keys, values)
-        lanes = [joined] + [swap(joined, offset) for offset in range(near, nodes, near)]
+        offsets = block_offsets(nodes)
+        lanes = [joined] + [swap(joined, offset) for offset in offsets[1:]]
 
     kv_rows = 0 if apart else rows // 2
     message = (nodes, Q_ROWS + kv_rows, WIDE)
@@ -337,18 +345,22 @@
     moved = lax.all_to_all(packed, "ctx", split_axis=0, concat_axis=0, tiled=True)
 
     if apart:
-        mine, others = pl.pallas_call(
+        near, far = len(lanes) * rows, (len(lanes) - 2) * rows
+        pieces = pl.pallas_call(
             heads_kernel,
-            out_shape=(jax.ShapeDtypeStruct((near * rows, 2 * HEADS * HD), jnp.bfloat16),) * CORES,
+            out_shape=[
+                jax.ShapeDtypeStruct((count, 2 * HEADS * HD), jnp.bfloat16)
+                for count in (near, near, far, far)
+            ],
             in_specs=[whole] * len(lanes),
-            out_specs=(whole,) * CORES,
+            out_specs=[whole] * (2 * CORES),
             compiler_params=VMEM,
             cost_estimate=pl.CostEstimate(
                 flops=2 * 10**10, bytes_accessed=64 * 2**20, transcendentals=0
             ),
             name="heads",
         )(*lanes)
-        kv_parts = [mine, swap(others, 1), swap(mine, 2), swap(others, 3)]
+        kv_parts = [swap(piece, index) if index else piece for index, piece in enumerate(pieces)]
         q_part = moved
     else:
         kv_parts = [moved]

time: 41.2 us -> 38.7 us (0.939)
  waiting for transfers between devices: 16.8 us -> 13.6 us
  starting transfers between devices: 14.1 us -> 14.7 us
    ppermute x7 -> x8, waiting for transfers between devices: 16.8 us -> 13.6 us  [swap(): lax.ppermute(array, 'ctx', [(node, node ^ offset) for node in range(nodes)])]
    ppermute x7 -> x8, starting transfers between devices: 7.83 us -> 9.56 us  [swap(): lax.ppermute(array, 'ctx', [(node, node ^ offset) for node in range(nodes)])]
    all_to_all x1, starting transfers between devices: 6.3 us -> 5.13 us  [on_device(): lax.all_to_all(packed, 'ctx', split_axis=0, concat_axis=0, tiled=True)]
  transfers between devices with their start and end apart: 8 -> 9, of which waited for: 4 -> 4; matrix products, arithmetic and copies ran while one was open for 0% -> 0% of each run, Pallas kernels for 13% -> 14%
where the time goes in v4:
time: 38.7 us; the launch traced here: 38.4 us
  starting transfers between devices  14.7 us (38%)
  waiting for transfers between devices  13.6 us (35%)
  Pallas kernels  10 us (26%)
    ppermute x8, waiting for transfers between devices, swap(): lax.ppermute(array, 'ctx', [(node, node ^ offset) for node in range(nodes)])  13.6 us
    ppermute x8, starting transfers between devices, swap(): lax.ppermute(array, 'ctx', [(node, node ^ offset) for node in range(nodes)])  9.56 us
    all_to_all x1, starting transfers between devices, on_device(): lax.all_to_all(packed, 'ctx', split_axis=0, concat_axis=0, tiled=True)  5.13 us
    pallas_call x1, Pallas kernels, on_device(): pl.pallas_call(functools.partial(pack_kernel, chips), out_shape=jax.Shape...  2.46 us
    pallas_call x1, Pallas kernels, on_device(): pl.pallas_call(attend_kernel, out_shape=(jax.ShapeDtypeStruct((rows, HEAD...  2.4 us
    pallas_call x1, Pallas kernels, on_device(): pl.pallas_call(functools.partial(place_kernel, per_chip), out_shape=(jax....  1.57 us
    pallas_call x1, Pallas kernels, on_device(): pl.pallas_call(join_kernel, out_shape=jax.ShapeDtypeStruct((rows, 2 * KVH...  1.54 us
    pallas_call x1, Pallas kernels, on_device(): pl.pallas_call(heads_kernel, out_shape=[jax.ShapeDtypeStruct((count, 2 *...  1.18 us
  transfers between devices with their start and end apart: 9, of which 4 were waited for; matrix products, arithmetic and copies ran while one was open for 0% of the time, Pallas kernels for 14%

profile of v4, /device:TPU:0, one launch (start us, length us, event | category | flops | bytes accessed | tf_op | source)
XLA Modules:
  0.0 38.4 jit_solution(2173890843838832542)
XLA Ops:
  0.0 1.5 %join.1.refs_0_ = bf16[64,1024]{1,0:T(8,128)(2,1)} custom-call(bf16[64,512]{1,0:T(8,128)(2,1)} %k_hbm.1, bf16[64,512]{1,0:T(8,128)(2,1)} %v_hbm.1), custom_call_target="tpu_custom_call" | custom-call | tf_op jit(solution)/shard_map/join/pallas_call | solution.py:310
  1.6 5.1 %collective-permute-start.3 = (bf16[64,1024]{1,0:T(8,128)(2,1)}, bf16[64,1024]{1,0:T(8,128)(2,1)}, u32[]{:S(2)}, u32[]{:S(2)}) collective-permute-start(bf16[64,1024]{1,0:T(8,128)(2,1)} %join.1.refs_0_), channel_id=1, source_target_pairs={{0,12},{1,13},{2,14},{3,15},{4,8},{5,9},{6,10},{7,11},{8,4},{9,5},... | collective-permute-start | bytes 393224 | tf_op jit(solution)/shard_map/ppermute | solution.py:307
  6.7 0.0 collective-permute-start.2
  6.7 0.6 %collective-permute-start.1 = (bf16[64,1024]{1,0:T(8,128)(2,1)}, bf16[64,1024]{1,0:T(8,128)(2,1)}, u32[]{:S(2)}, u32[]{:S(2)}) collective-permute-start(bf16[64,1024]{1,0:T(8,128)(2,1)} %join.1.refs_0_), channel_id=1, source_target_pairs={{0,4},{1,5},{2,6},{3,7},{4,0},{5,1},{6,2},{7,3},{8,12},{9,13},{10,... | collective-permute-start | bytes 393224 | tf_op jit(solution)/shard_map/ppermute | solution.py:307
  7.3 1.7 %collective-permute-start = (bf16[64,1024]{1,0:T(8,128)(2,1)}, bf16[64,1024]{1,0:T(8,128)(2,1)}, u32[]{:S(2)}, u32[]{:S(2)}) collective-permute-start(bf16[64,1024]{1,0:T(8,128)(2,1)} %join.1.refs_0_), channel_id=1, source_target_pairs={{0,2},{1,3},{2,0},{3,1},{4,6},{5,7},{6,4},{7,5},{8,10},{9,11},{10,... | collective-permute-start | bytes 393224 | tf_op jit(solution)/shard_map/ppermute | solution.py:307
  9.0 2.5 %pack.1 = bf16[16,16,1024]{2,1,0:T(8,128)(2,1)} custom-call(s32[8,128]{1,0:T(8,128)} %bitcast.1, bf16[64,4096]{1,0:T(8,128)(2,1)} %q_hbm.1), custom_call_target="tpu_custom_call" | custom-call | flops 33554432 | bytes 1048576 | tf_op jit(solution)/shard_map/pack/pallas_call | solution.py:326
  11.4 0.0 copy-start
  11.5 5.1 %all-to-all-start = ((bf16[16,16,1024]{2,1,0:T(8,128)(2,1)}), bf16[16,16,1024]{2,1,0:T(8,128)(2,1)S(1)}, u32[]{:S(2)}, u32[]{:S(2)}) async-start(bf16[16,16,1024]{2,1,0:T(8,128)(2,1)} %pack.1), calls=%async_computation | async-start | bytes 1048576 | tf_op jit(solution)/shard_map/all_to_all | solution.py:345
  16.6 0.0 collective-permute-done.3.refs_4_
  16.6 1.5 %collective-permute-done.2.refs_3_ = bf16[64,1024]{1,0:T(8,128)(2,1)} collective-permute-done((bf16[64,1024]{1,0:T(8,128)(2,1)}, bf16[64,1024]{1,0:T(8,128)(2,1)}, u32[]{:S(2)}, u32[]{:S(2)}) %collective-permute-start.2) | collective-permute-done | bytes 131104 | tf_op jit(solution)/shard_map/ppermute | solution.py:307
  18.1 0.0 collective-permute-done.1.refs_2_
  18.1 0.0 collective-permute-done.refs_1_
  18.1 0.0 copy-done
  18.1 1.2 %heads.1 = (bf16[320,512]{1,0:T(8,128)(2,1)S(1)}, bf16[320,512]{1,0:T(8,128)(2,1)S(1)}, bf16[192,512]{1,0:T(8,128)(2,1)S(1)}, bf16[192,512]{1,0:T(8,128)(2,1)S(1)}) custom-call(bf16[64,1024]{1,0:T(8,128)(2,1)S(1)} %copy-done, bf16[64,1024]{1,0:T(8,128)(2,1)} %collective-permute-done.refs_1_, bf16[64,1024]{1,0:T(8,128)(2,1)} %collective-permute-done.1.refs_2_, ...), custom_call_target="tpu_custom_call" | custom-call | flops 20000000000 | bytes 67108864 | tf_op jit(solution)/shard_map/heads/pallas_call | solution.py:349
  19.3 0.0 copy-start.1
  19.3 0.1 collective-permute-start.4
  19.3 0.0 copy-start.2
  19.4 1.6 %collective-permute-start.5 = (bf16[192,512]{1,0:T(8,128)(2,1)S(1)}, bf16[192,512]{1,0:T(8,128)(2,1)S(1)}, u32[]{:S(2)}, u32[]{:S(2)}) collective-permute-start(bf16[192,512]{1,0:T(8,128)(2,1)S(1)} %get-tuple-element.19), channel_id=1, source_target_pairs={{0,2},{1,3},{2,0},{3,1},{4,6},{5,7},{6,4},{7,5},{8,10},{9,11},{10,... | collective-permute-start | bytes 589832 | tf_op jit(solution)/shard_map/ppermute | solution.py:307
  20.9 0.3 collective-permute-start.6
  21.2 0.0 copy-done.1
  21.2 0.0 copy-done.2
  21.2 1.6 %place.1 = (s32[128,128]{1,0:T(8,128)S(1)}, s32[128,128]{1,0:T(8,128)S(1)}, bf16[128,128]{1,0:T(8,128)(2,1)S(1)}) custom-call(s32[4]{0:T(128)S(1)} %copy-done.2, s32[8,128]{1,0:T(8,128)S(1)} %bitcast.2), custom_call_target="tpu_custom_call" | custom-call | tf_op jit(solution)/shard_map/place/pallas_call | solution.py:371
  22.8 6.0 %collective-permute-done.5.refs_2_ = bf16[192,512]{1,0:T(8,128)(2,1)S(1)} collective-permute-done((bf16[192,512]{1,0:T(8,128)(2,1)S(1)}, bf16[192,512]{1,0:T(8,128)(2,1)S(1)}, u32[]{:S(2)}, u32[]{:S(2)}) %collective-permute-start.5) | collective-permute-done | bytes 196640 | tf_op jit(solution)/shard_map/ppermute | solution.py:307
  28.7 4.8 %collective-permute-done.6.refs_3_ = bf16[192,512]{1,0:T(8,128)(2,1)S(1)} collective-permute-done((bf16[192,512]{1,0:T(8,128)(2,1)S(1)}, bf16[192,512]{1,0:T(8,128)(2,1)S(1)}, u32[]{:S(2)}, u32[]{:S(2)}) %collective-permute-start.6) | collective-permute-done | bytes 196640 | tf_op jit(solution)/shard_map/ppermute | solution.py:307
  33.6 0.0 collective-permute-done.4.refs_1_
  33.6 0.0 all-to-all-done.q_ref
  33.6 2.4 %attend.1 = (bf16[64,2048]{1,0:T(8,128)(2,1)S(1)}, bf16[64,2048]{1,0:T(8,128)(2,1)S(1)}) custom-call(bf16[16,16,1024]{2,1,0:T(8,128)(2,1)S(1)} %all-to-all-done.q_ref, s32[128,128]{1,0:T(8,128)S(1)} %get-tuple-element.14.pos_ref, s32[128,128]{1,0:T(8,128)S(1)} %get-tuple-element.15.start_ref, bf16[128,128]{1,0:T(8,128)(2,1)S(1)} %get-tuple-element.16.order_ref, ...), custom_call_target="tpu_custom_call" | custom-call | tf_op jit(solution)/shard_map/attend/pallas_call | solution.py:384
  36.0 0.2 collective-permute-start.7
  36.2 1.4 %collective-permute-done.7.refs_1_ = bf16[64,2048]{1,0:T(8,128)(2,1)S(1)} collective-permute-done((bf16[64,2048]{1,0:T(8,128)(2,1)S(1)}, bf16[64,2048]{1,0:T(8,128)(2,1)S(1)}, u32[]{:S(2)}, u32[]{:S(2)}) %collective-permute-start.7) | collective-permute-done | bytes 262176 | tf_op jit(solution)/shard_map/ppermute | solution.py:307
  37.6 0.8 %assemble.1 = bf16[64,4096]{1,0:T(8,128)(2,1)} custom-call(bf16[64,2048]{1,0:T(8,128)(2,1)S(1)} %get-tuple-element.21.refs_0_, bf16[64,2048]{1,0:T(8,128)(2,1)S(1)} %collective-permute-done.7.refs_1_), custom_call_target="tpu_custom_call" | custom-call | tf_op jit(solution)/shard_map/assemble/pallas_call | solution.py:398
Async XLA Ops:
  1.6 15.0 %collective-permute-start.3 = (bf16[64,1024]{1,0:T(8,128)(2,1)}, bf16[64,1024]{1,0:T(8,128)(2,1)}, u32[]{:S(2)}, u32[]{:S(2)}) collective-permute-start(bf16[64,1024]{1,0:T(8,128)(2,1)} %join.1.refs_0_), channel_id=1, source_target_pairs={{0,12},{1,13},{2,14},{3,15},{4,8},{5,9},{6,10},{7,11},{8,4},{9,5},... | collective-permute-start | bytes 393224 | tf_op jit(solution)/shard_map/ppermute | solution.py:307
  6.7 11.4 %collective-permute-start.2 = (bf16[64,1024]{1,0:T(8,128)(2,1)}, bf16[64,1024]{1,0:T(8,128)(2,1)}, u32[]{:S(2)}, u32[]{:S(2)}) collective-permute-start(bf16[64,1024]{1,0:T(8,128)(2,1)} %join.1.refs_0_), channel_id=1, source_target_pairs={{0,8},{1,9},{2,10},{3,11},{4,12},{5,13},{6,14},{7,15},{8,0},{9,1},... | collective-permute-start | bytes 393224 | tf_op jit(solution)/shard_map/ppermute | solution.py:307
  6.7 11.4 %collective-permute-start.1 = (bf16[64,1024]{1,0:T(8,128)(2,1)}, bf16[64,1024]{1,0:T(8,128)(2,1)}, u32[]{:S(2)}, u32[]{:S(2)}) collective-permute-start(bf16[64,1024]{1,0:T(8,128)(2,1)} %join.1.refs_0_), channel_id=1, source_target_pairs={{0,4},{1,5},{2,6},{3,7},{4,0},{5,1},{6,2},{7,3},{8,12},{9,13},{10,... | collective-permute-start | bytes 393224 | tf_op jit(solution)/shard_map/ppermute | solution.py:307
  7.3 10.8 %collective-permute-start = (bf16[64,1024]{1,0:T(8,128)(2,1)}, bf16[64,1024]{1,0:T(8,128)(2,1)}, u32[]{:S(2)}, u32[]{:S(2)}) collective-permute-start(bf16[64,1024]{1,0:T(8,128)(2,1)} %join.1.refs_0_), channel_id=1, source_target_pairs={{0,2},{1,3},{2,0},{3,1},{4,6},{5,7},{6,4},{7,5},{8,10},{9,11},{10,... | collective-permute-start | bytes 393224 | tf_op jit(solution)/shard_map/ppermute | solution.py:307
  11.4 6.6 %copy-start = (bf16[64,1024]{1,0:T(8,128)(2,1)S(1)}, bf16[64,1024]{1,0:T(8,128)(2,1)}, u32[]{:S(2)}) copy-start(bf16[64,1024]{1,0:T(8,128)(2,1)} %join.1.refs_0_) | copy-start | bytes 393220
  11.5 22.1 %all-to-all-start = ((bf16[16,16,1024]{2,1,0:T(8,128)(2,1)}), bf16[16,16,1024]{2,1,0:T(8,128)(2,1)S(1)}, u32[]{:S(2)}, u32[]{:S(2)}) async-start(bf16[16,16,1024]{2,1,0:T(8,128)(2,1)} %pack.1), calls=%async_computation | async-start | bytes 1048576 | tf_op jit(solution)/shard_map/all_to_all | solution.py:345
  19.3 2.0 %copy-start.1 = (s32[1024]{0:T(1024)S(1)}, s32[1024]{0:T(1024)}, u32[]{:S(2)}) copy-start(s32[1024]{0:T(1024)} %param.8) | copy-start | bytes 12292
  19.3 14.3 %collective-permute-start.4 = (bf16[320,512]{1,0:T(8,128)(2,1)S(1)}, bf16[320,512]{1,0:T(8,128)(2,1)S(1)}, u32[]{:S(2)}, u32[]{:S(2)}) collective-permute-start(bf16[320,512]{1,0:T(8,128)(2,1)S(1)} %get-tuple-element.18), channel_id=1, source_target_pairs={{0,1},{1,0},{2,3},{3,2},{4,5},{5,4},{6,7},{7,6},{8,9},{9,8},{10,11... | collective-permute-start | bytes 983048 | tf_op jit(solution)/shard_map/ppermute | solution.py:307
  19.3 1.9 %copy-start.2 = (s32[4]{0:T(128)S(1)}, s32[4]{0:T(128)}, u32[]{:S(2)}) copy-start(s32[4]{0:T(128)} %lengths_ref.1) | copy-start | bytes 52
  19.4 9.4 %collective-permute-start.5 = (bf16[192,512]{1,0:T(8,128)(2,1)S(1)}, bf16[192,512]{1,0:T(8,128)(2,1)S(1)}, u32[]{:S(2)}, u32[]{:S(2)}) collective-permute-start(bf16[192,512]{1,0:T(8,128)(2,1)S(1)} %get-tuple-element.19), channel_id=1, source_target_pairs={{0,2},{1,3},{2,0},{3,1},{4,6},{5,7},{6,4},{7,5},{8,10},{9,11},{10,... | collective-permute-start | bytes 589832 | tf_op jit(solution)/shard_map/ppermute | solution.py:307
  20.9 12.6 %collective-permute-start.6 = (bf16[192,512]{1,0:T(8,128)(2,1)S(1)}, bf16[192,512]{1,0:T(8,128)(2,1)S(1)}, u32[]{:S(2)}, u32[]{:S(2)}) collective-permute-start(bf16[192,512]{1,0:T(8,128)(2,1)S(1)} %get-tuple-element.20), channel_id=1, source_target_pairs={{0,3},{1,2},{2,1},{3,0},{4,7},{5,6},{6,5},{7,4},{8,11},{9,10},{10,... | collective-permute-start | bytes 589832 | tf_op jit(solution)/shard_map/ppermute | solution.py:307
  36.0 1.6 %collective-permute-start.7 = (bf16[64,2048]{1,0:T(8,128)(2,1)S(1)}, bf16[64,2048]{1,0:T(8,128)(2,1)S(1)}, u32[]{:S(2)}, u32[]{:S(2)}) collective-permute-start(bf16[64,2048]{1,0:T(8,128)(2,1)S(1)} %get-tuple-element.22), channel_id=1, source_target_pairs={{0,1},{1,0},{2,3},{3,2},{4,5},{5,4},{6,7},{7,6},{8,9},{9,8},{10,11... | collective-permute-start | bytes 786440 | tf_op jit(solution)/shard_map/ppermute | solution.py:307

commit v5 on v4

--- a/solution.py
+++ b/solution.py
@@ -37,25 +37,11 @@
     return jnp.sum(jnp.where(here == there, column, 0), axis=0, keepdims=True)
 
 
-def pack_kernel(chips, owner_hbm, q_hbm, *refs):
-    with_kv = len(refs) > 6
-    kv_hbm, refs = (refs[:2], refs[2:]) if with_kv else ((), refs)
-    out_hbm, owner_ref, q_ref, out_ref, in_sems, out_sems = refs[:6]
-    kv_refs = refs[6:]
+def pack_kernel(chips, owner_ref, q_ref, *refs):
+    kv_refs, out_ref = refs[:-1], refs[-1]
     me = lax.axis_index("ctx")
     rows = q_ref.shape[0]
     per_chip = rows // chips
-    first = pltpu.make_async_copy(owner_hbm, owner_ref, in_sems.at[KVH])
-    queries = []
-    for head in range(KVH):
-        wide = pl.ds(head * WIDE, WIDE)
-        queries.append(pltpu.make_async_copy(q_hbm.at[:, wide], q_ref.at[:, wide], in_sems.at[head]))
-    arrivals = []
-    for index, (source, target) in enumerate(zip(kv_hbm, kv_refs)):
-        arrivals.append(pltpu.make_async_copy(source, target, in_sems.at[KVH + 1 + index]))
-    for copy in [first] + queries + arrivals:
-        copy.start()
-    first.wait()
     both = owner_ref[pl.ds(me // 2, 1), :]
     swapped = jnp.concatenate((both[:, rows:], both[:, :rows]), axis=1)
     own = jnp.where(me % 2 == 1, swapped, both)[:, :rows]
@@ -64,13 +50,9 @@
     rank = jnp.sum((row_to_column(key_row) < key_row).astype(jnp.int32), axis=0, keepdims=True)
     place = lax.broadcasted_iota(jnp.int32, (rows, rows), 0)
     order = (place == rank).astype(jnp.float32).astype(jnp.bfloat16)
-    for copy in arrivals:
-        copy.wait()
-    departures = []
     for core in range(CORES):
         sorted_q = []
         for head in range(core * HEADS, (core + 1) * HEADS):
-            queries[head].wait()
             wide = slice(head * WIDE, (head + 1) * WIDE)
             sorted_q.append(jnp.dot(order, q_ref[:, wide], preferred_element_type=jnp.float32))
         for chip in range(chips):
@@ -81,7 +63,7 @@
                 if per_chip < SUB:
                     parts.append(jnp.zeros((SUB - per_chip, WIDE), jnp.float32))
             out_ref[dest, :Q_ROWS, :] = jnp.concatenate(parts, axis=0).astype(jnp.bfloat16)
-            if with_kv:
+            if kv_refs:
                 width = HEADS * HD
                 side = slice(core * width, (core + 1) * width)
                 half = rows // 2
@@ -90,15 +72,10 @@
                     for index in range(2):
                         col = (2 * part + index) * width
                         out_ref[dest, Q_ROWS:, col : col + width] = kv_refs[index][here, side]
-            copy = pltpu.make_async_copy(out_ref.at[dest], out_hbm.at[dest], out_sems.at[dest])
-            copy.start()
-            departures.append(copy)
-    for copy in departures:
-        copy.wait()
 
 
 def block_offsets(nodes):
-    return [0, CORES] + list(range(2 * CORES, nodes, 2 * CORES))
+    return [0, CORES, 2 * CORES, 3 * CORES] + list(range(4 * CORES, nodes, 2 * CORES))
 
 
 def join_kernel(k_hbm, v_hbm, out_ref, sems):
@@ -125,8 +102,8 @@
                 block = ref[:, pl.ds(pl.multiple_of(col + half * KVH * HD, width), width)]
                 side = slice(half * width, (half + 1) * width)
                 near[index][lane * rows : (lane + 1) * rows, side] = block
-                if lane >= 2:
-                    far[index][(lane - 2) * rows : (lane - 1) * rows, side] = block
+                if lane >= 4:
+                    far[index][(lane - 4) * rows : (lane - 3) * rows, side] = block
 
 
 def place_kernel(per_chip, lengths_ref, owner_ref, pos_ref, start_ref, order_ref):
@@ -201,7 +178,7 @@
     offsets = block_offsets(k_all.shape[0] // tokens)
     width = HEADS * HD
     for index, ref in enumerate(pieces):
-        held = offsets if index < CORES else offsets[2:]
+        held = offsets if index < CORES else offsets[4:]
         for lane, offset in enumerate(held):
             node = jnp.bitwise_xor(me, index ^ offset)
             row = pl.ds(pl.multiple_of(node * tokens, tokens), tokens)
@@ -321,22 +298,13 @@
 
     kv_rows = 0 if apart else rows // 2
     message = (nodes, Q_ROWS + kv_rows, WIDE)
-    kv_scratch = [pltpu.VMEM(keys.shape, jnp.bfloat16), pltpu.VMEM(values.shape, jnp.bfloat16)]
     operands = (table, queries) if apart else (table, queries, keys, values)
     packed = pl.pallas_call(
         functools.partial(pack_kernel, chips),
         out_shape=jax.ShapeDtypeStruct(message, jnp.bfloat16),
-        in_specs=[hbm] * len(operands),
-        out_specs=hbm,
-        scratch_shapes=[
-            pltpu.VMEM(table.shape, jnp.int32),
-            pltpu.VMEM(queries.shape, jnp.bfloat16),
-            pltpu.VMEM(message, jnp.bfloat16),
-            pltpu.SemaphoreType.DMA((KVH + 3,)),
-            pltpu.SemaphoreType.DMA((nodes,)),
-        ]
-        + ([] if apart else kv_scratch),
-        compiler_params=ALL_VMEM,
+        in_specs=[whole] * len(operands),
+        out_specs=whole,
+        compiler_params=VMEM,
         cost_estimate=pl.CostEstimate(
             flops=2 * rows * rows * H * HD, bytes_accessed=4 * rows * H * HD, transcendentals=0
         ),
@@ -345,7 +313,7 @@
     moved = lax.all_to_all(packed, "ctx", split_axis=0, concat_axis=0, tiled=True)
 
     if apart:
-        near, far = len(lanes) * rows, (len(lanes) - 2) * rows
+        near, far = len(lanes) * rows, (len(lanes) - 4) * rows
         pieces = pl.pallas_call(
             heads_kernel,
             out_shape=[

time: 38.7 us -> 37.5 us (0.969)
  Pallas kernels: 10 us -> 7.73 us
  starting transfers between devices: 14.7 us -> 16 us
  waiting for transfers between devices: 13.6 us -> 12.3 us
  local copies, waits for them, and re-layouts: 0.02 us -> 1.06 us
    ppermute x8 -> x9, waiting for transfers between devices: 13.6 us -> 10.8 us  [swap(): lax.ppermute(array, 'ctx', [(node, node ^ offset) for node in range(nodes)])]
    all_to_all x1, waiting for transfers between devices: 0.01 us -> 1.49 us  [on_device(): lax.all_to_all(packed, 'ctx', split_axis=0, concat_axis=0, tiled=True)]
    pallas_call x1, Pallas kernels: 2.46 us -> 1.26 us  [on_device(): pl.pallas_call(functools.partial(pack_kernel, chips), out_shape=jax.Shape...]
    pallas_call x1, Pallas kernels: 1.18 us -> 0.1 us  [on_device(): pl.pallas_call(heads_kernel, out_shape=[jax.ShapeDtypeStruct((count, 2 *...]
    ppermute x8 -> x9, starting transfers between devices: 9.56 us -> 10.6 us  [swap(): lax.ppermute(array, 'ctx', [(node, node ^ offset) for node in range(nodes)])]
    unnamed x6 -> x8, local copies, waits for them, and re-layouts: 0.02 us -> 1.06 us
  transfers between devices with their start and end apart: 9 -> 10, of which waited for: 4 -> 6; matrix products, arithmetic and copies ran while one was open for 0% -> 0% of each run, Pallas kernels for 14% -> 8%
where the time goes in v5:
time: 37.5 us; the launch traced here: 37.2 us
  starting transfers between devices  16 us (43%)
  waiting for transfers between devices  12.3 us (33%)
  Pallas kernels  7.73 us (21%)
  local copies, waits for them, and re-layouts  1.06 us (3%)
    ppermute x9, waiting for transfers between devices, swap(): lax.ppermute(array, 'ctx', [(node, node ^ offset) for node in range(nodes)])  10.8 us
    ppermute x9, starting transfers between devices, swap(): lax.ppermute(array, 'ctx', [(node, node ^ offset) for node in range(nodes)])  10.6 us
    all_to_all x1, starting transfers between devices, on_device(): lax.all_to_all(packed, 'ctx', split_axis=0, concat_axis=0, tiled=True)  5.38 us
    pallas_call x1, Pallas kernels, on_device(): pl.pallas_call(attend_kernel, out_shape=(jax.ShapeDtypeStruct((rows, HEAD...  2.4 us
    pallas_call x1, Pallas kernels, on_device(): pl.pallas_call(functools.partial(place_kernel, per_chip), out_shape=(jax....  1.57 us
    pallas_call x1, Pallas kernels, on_device(): pl.pallas_call(join_kernel, out_shape=jax.ShapeDtypeStruct((rows, 2 * KVH...  1.55 us
    all_to_all x1, waiting for transfers between devices, on_device(): lax.all_to_all(packed, 'ctx', split_axis=0, concat_axis=0, tiled=True)  1.49 us
    pallas_call x1, Pallas kernels, on_device(): pl.pallas_call(functools.partial(pack_kernel, chips), out_shape=jax.Shape...  1.26 us
  transfers between devices with their start and end apart: 10, of which 6 were waited for; matrix products, arithmetic and copies ran while one was open for 0% of the time, Pallas kernels for 8%

profile of v5, /device:TPU:0, one launch (start us, length us, event | category | flops | bytes accessed | tf_op | source)
XLA Modules:
  0.0 37.2 jit_solution(17201568701014867635)
XLA Ops:
  0.0 0.0 copy-start.2
  0.0 1.6 %join.1.refs_0_ = bf16[64,1024]{1,0:T(8,128)(2,1)} custom-call(bf16[64,512]{1,0:T(8,128)(2,1)} %k_hbm.1, bf16[64,512]{1,0:T(8,128)(2,1)} %v_hbm.1), custom_call_target="tpu_custom_call" | custom-call | tf_op jit(solution)/shard_map/join/pallas_call | solution.py:287
  1.6 5.1 %collective-permute-start.4 = (bf16[64,1024]{1,0:T(8,128)(2,1)}, bf16[64,1024]{1,0:T(8,128)(2,1)S(1)}, u32[]{:S(2)}, u32[]{:S(2)}) collective-permute-start(bf16[64,1024]{1,0:T(8,128)(2,1)} %join.1.refs_0_), channel_id=1, source_target_pairs={{0,12},{1,13},{2,14},{3,15},{4,8},{5,9},{6,10},{7,11},{8,4},{9,5},... | collective-permute-start | bytes 393224 | tf_op jit(solution)/shard_map/ppermute | solution.py:284
  6.7 0.0 collective-permute-start.3
  6.7 1.7 %collective-permute-start.2 = (bf16[64,1024]{1,0:T(8,128)(2,1)}, bf16[64,1024]{1,0:T(8,128)(2,1)S(1)}, u32[]{:S(2)}, u32[]{:S(2)}) collective-permute-start(bf16[64,1024]{1,0:T(8,128)(2,1)} %join.1.refs_0_), channel_id=1, source_target_pairs={{0,6},{1,7},{2,4},{3,5},{4,2},{5,3},{6,0},{7,1},{8,14},{9,15},{10,... | collective-permute-start | bytes 393224 | tf_op jit(solution)/shard_map/ppermute | solution.py:284
  8.4 1.2 %collective-permute-start.1 = (bf16[64,1024]{1,0:T(8,128)(2,1)}, bf16[64,1024]{1,0:T(8,128)(2,1)S(1)}, u32[]{:S(2)}, u32[]{:S(2)}) collective-permute-start(bf16[64,1024]{1,0:T(8,128)(2,1)} %join.1.refs_0_), channel_id=1, source_target_pairs={{0,4},{1,5},{2,6},{3,7},{4,0},{5,1},{6,2},{7,3},{8,12},{9,13},{10,... | collective-permute-start | bytes 393224 | tf_op jit(solution)/shard_map/ppermute | solution.py:284
  9.7 0.5 %collective-permute-start = (bf16[64,1024]{1,0:T(8,128)(2,1)}, bf16[64,1024]{1,0:T(8,128)(2,1)S(1)}, u32[]{:S(2)}, u32[]{:S(2)}) collective-permute-start(bf16[64,1024]{1,0:T(8,128)(2,1)} %join.1.refs_0_), channel_id=1, source_target_pairs={{0,2},{1,3},{2,0},{3,1},{4,6},{5,7},{6,4},{7,5},{8,10},{9,11},{10,... | collective-permute-start | bytes 393224 | tf_op jit(solution)/shard_map/ppermute | solution.py:284
  10.2 0.0 copy-done.2
  10.2 0.0 copy-start
  10.2 1.0 %copy-done = bf16[64,4096]{1,0:T(8,128)(2,1)S(1)} copy-done((bf16[64,4096]{1,0:T(8,128)(2,1)S(1)}, bf16[64,4096]{1,0:T(8,128)(2,1)}, u32[]{:S(2)}) %copy-start) | copy-done | bytes 524312
  11.2 1.3 %pack.1 = bf16[16,16,1024]{2,1,0:T(8,128)(2,1)} custom-call(s32[8,128]{1,0:T(8,128)S(1)} %bitcast.1, bf16[64,4096]{1,0:T(8,128)(2,1)S(1)} %copy-done), custom_call_target="tpu_custom_call" | custom-call | flops 33554432 | bytes 1048576 | tf_op jit(solution)/shard_map/pack/pallas_call | solution.py:302
  12.5 0.0 copy-start.1
  12.5 5.4 %all-to-all-start = ((bf16[16,16,1024]{2,1,0:T(8,128)(2,1)}), bf16[16,16,1024]{2,1,0:T(8,128)(2,1)S(1)}, u32[]{:S(2)}, u32[]{:S(2)}) async-start(bf16[16,16,1024]{2,1,0:T(8,128)(2,1)} %pack.1), calls=%async_computation | async-start | bytes 1048576 | tf_op jit(solution)/shard_map/all_to_all | solution.py:313
  17.9 0.0 collective-permute-done.4.refs_5_
  17.9 0.2 collective-permute-done.3.refs_4_
  18.1 0.0 collective-permute-done.2.refs_3_
  18.1 1.0 %collective-permute-done.1.refs_2_ = bf16[64,1024]{1,0:T(8,128)(2,1)S(1)} collective-permute-done((bf16[64,1024]{1,0:T(8,128)(2,1)}, bf16[64,1024]{1,0:T(8,128)(2,1)S(1)}, u32[]{:S(2)}, u32[]{:S(2)}) %collective-permute-start.1) | collective-permute-done | bytes 131104 | tf_op jit(solution)/shard_map/ppermute | solution.py:284
  19.1 0.0 collective-permute-done.refs_1_
  19.1 0.0 copy-done.1
  19.1 0.1 heads.1
  19.2 0.1 collective-permute-start.5
  19.3 0.0 copy-start.3
  19.3 1.4 %collective-permute-start.6 = (bf16[128,512]{1,0:T(8,128)(2,1)S(1)}, bf16[128,512]{1,0:T(8,128)(2,1)S(1)}, u32[]{:S(2)}, u32[]{:S(2)}) collective-permute-start(bf16[128,512]{1,0:T(8,128)(2,1)S(1)} %get-tuple-element.19), channel_id=1, source_target_pairs={{0,2},{1,3},{2,0},{3,1},{4,6},{5,7},{6,4},{7,5},{8,10},{9,11},{10,... | collective-permute-start | bytes 393224 | tf_op jit(solution)/shard_map/ppermute | solution.py:284
  20.8 0.4 %collective-permute-start.7 = (bf16[128,512]{1,0:T(8,128)(2,1)S(1)}, bf16[128,512]{1,0:T(8,128)(2,1)S(1)}, u32[]{:S(2)}, u32[]{:S(2)}) collective-permute-start(bf16[128,512]{1,0:T(8,128)(2,1)S(1)} %get-tuple-element.20), channel_id=1, source_target_pairs={{0,3},{1,2},{2,1},{3,0},{4,7},{5,6},{6,5},{7,4},{8,11},{9,10},{10,... | collective-permute-start | bytes 393224 | tf_op jit(solution)/shard_map/ppermute | solution.py:284
  21.2 0.0 copy-done.3
  21.2 1.6 %place.1 = (s32[128,128]{1,0:T(8,128)S(1)}, s32[128,128]{1,0:T(8,128)S(1)}, bf16[128,128]{1,0:T(8,128)(2,1)S(1)}) custom-call(s32[4]{0:T(128)S(1)} %copy-done.3, s32[8,128]{1,0:T(8,128)S(1)} %bitcast.2), custom_call_target="tpu_custom_call" | custom-call | tf_op jit(solution)/shard_map/place/pallas_call | solution.py:339
  22.8 5.5 %collective-permute-done.6.refs_2_ = bf16[128,512]{1,0:T(8,128)(2,1)S(1)} collective-permute-done((bf16[128,512]{1,0:T(8,128)(2,1)S(1)}, bf16[128,512]{1,0:T(8,128)(2,1)S(1)}, u32[]{:S(2)}, u32[]{:S(2)}) %collective-permute-start.6) | collective-permute-done | bytes 131104 | tf_op jit(solution)/shard_map/ppermute | solution.py:284
  28.3 2.6 %collective-permute-done.7.refs_3_ = bf16[128,512]{1,0:T(8,128)(2,1)S(1)} collective-permute-done((bf16[128,512]{1,0:T(8,128)(2,1)S(1)}, bf16[128,512]{1,0:T(8,128)(2,1)S(1)}, u32[]{:S(2)}, u32[]{:S(2)}) %collective-permute-start.7) | collective-permute-done | bytes 131104 | tf_op jit(solution)/shard_map/ppermute | solution.py:284
  30.8 0.0 collective-permute-done.5.refs_1_
  30.8 1.5 %all-to-all-done.q_ref = bf16[16,16,1024]{2,1,0:T(8,128)(2,1)S(1)} async-done(((bf16[16,16,1024]{2,1,0:T(8,128)(2,1)}), bf16[16,16,1024]{2,1,0:T(8,128)(2,1)S(1)}, u32[]{:S(2)}, u32[]{:S(2)}) %all-to-all-start) | async-done | bytes 524320 | tf_op jit(solution)/shard_map/all_to_all | solution.py:313
  32.3 2.4 %attend.1 = (bf16[64,2048]{1,0:T(8,128)(2,1)S(1)}, bf16[64,2048]{1,0:T(8,128)(2,1)S(1)}) custom-call(bf16[16,16,1024]{2,1,0:T(8,128)(2,1)S(1)} %all-to-all-done.q_ref, s32[128,128]{1,0:T(8,128)S(1)} %get-tuple-element.14.pos_ref, s32[128,128]{1,0:T(8,128)S(1)} %get-tuple-element.15.start_ref, bf16[128,128]{1,0:T(8,128)(2,1)S(1)} %get-tuple-element.16.order_ref, ...), custom_call_target="tpu_custom_call" | custom-call | tf_op jit(solution)/shard_map/attend/pallas_call | solution.py:352
  34.7 0.1 collective-permute-start.8
  34.8 1.5 %collective-permute-done.8.refs_1_ = bf16[64,2048]{1,0:T(8,128)(2,1)S(1)} collective-permute-done((bf16[64,2048]{1,0:T(8,128)(2,1)S(1)}, bf16[64,2048]{1,0:T(8,128)(2,1)S(1)}, u32[]{:S(2)}, u32[]{:S(2)}) %collective-permute-start.8) | collective-permute-done | bytes 262176 | tf_op jit(solution)/shard_map/ppermute | solution.py:284
  36.3 0.8 %assemble.1 = bf16[64,4096]{1,0:T(8,128)(2,1)} custom-call(bf16[64,2048]{1,0:T(8,128)(2,1)S(1)} %get-tuple-element.21.refs_0_, bf16[64,2048]{1,0:T(8,128)(2,1)S(1)} %collective-permute-done.8.refs_1_), custom_call_target="tpu_custom_call" | custom-call | tf_op jit(solution)/shard_map/assemble/pallas_call | solution.py:366
Async XLA Ops:
  0.0 10.2 %copy-start.2 = (s32[1024]{0:T(1024)S(1)}, s32[1024]{0:T(1024)}, u32[]{:S(2)}) copy-start(s32[1024]{0:T(1024)} %param.8) | copy-start | bytes 12292
  1.6 16.3 %collective-permute-start.4 = (bf16[64,1024]{1,0:T(8,128)(2,1)}, bf16[64,1024]{1,0:T(8,128)(2,1)S(1)}, u32[]{:S(2)}, u32[]{:S(2)}) collective-permute-start(bf16[64,1024]{1,0:T(8,128)(2,1)} %join.1.refs_0_), channel_id=1, source_target_pairs={{0,12},{1,13},{2,14},{3,15},{4,8},{5,9},{6,10},{7,11},{8,4},{9,5},... | collective-permute-start | bytes 393224 | tf_op jit(solution)/shard_map/ppermute | solution.py:284
  6.7 11.4 %collective-permute-start.3 = (bf16[64,1024]{1,0:T(8,128)(2,1)}, bf16[64,1024]{1,0:T(8,128)(2,1)S(1)}, u32[]{:S(2)}, u32[]{:S(2)}) collective-permute-start(bf16[64,1024]{1,0:T(8,128)(2,1)} %join.1.refs_0_), channel_id=1, source_target_pairs={{0,8},{1,9},{2,10},{3,11},{4,12},{5,13},{6,14},{7,15},{8,0},{9,1},... | collective-permute-start | bytes 393224 | tf_op jit(solution)/shard_map/ppermute | solution.py:284
  6.7 11.4 %collective-permute-start.2 = (bf16[64,1024]{1,0:T(8,128)(2,1)}, bf16[64,1024]{1,0:T(8,128)(2,1)S(1)}, u32[]{:S(2)}, u32[]{:S(2)}) collective-permute-start(bf16[64,1024]{1,0:T(8,128)(2,1)} %join.1.refs_0_), channel_id=1, source_target_pairs={{0,6},{1,7},{2,4},{3,5},{4,2},{5,3},{6,0},{7,1},{8,14},{9,15},{10,... | collective-permute-start | bytes 393224 | tf_op jit(solution)/shard_map/ppermute | solution.py:284
  8.4 10.7 %collective-permute-start.1 = (bf16[64,1024]{1,0:T(8,128)(2,1)}, bf16[64,1024]{1,0:T(8,128)(2,1)S(1)}, u32[]{:S(2)}, u32[]{:S(2)}) collective-permute-start(bf16[64,1024]{1,0:T(8,128)(2,1)} %join.1.refs_0_), channel_id=1, source_target_pairs={{0,4},{1,5},{2,6},{3,7},{4,0},{5,1},{6,2},{7,3},{8,12},{9,13},{10,... | collective-permute-start | bytes 393224 | tf_op jit(solution)/shard_map/ppermute | solution.py:284
  9.7 9.5 %collective-permute-start = (bf16[64,1024]{1,0:T(8,128)(2,1)}, bf16[64,1024]{1,0:T(8,128)(2,1)S(1)}, u32[]{:S(2)}, u32[]{:S(2)}) collective-permute-start(bf16[64,1024]{1,0:T(8,128)(2,1)} %join.1.refs_0_), channel_id=1, source_target_pairs={{0,2},{1,3},{2,0},{3,1},{4,6},{5,7},{6,4},{7,5},{8,10},{9,11},{10,... | collective-permute-start | bytes 393224 | tf_op jit(solution)/shard_map/ppermute | solution.py:284
  10.2 1.0 %copy-start = (bf16[64,4096]{1,0:T(8,128)(2,1)S(1)}, bf16[64,4096]{1,0:T(8,128)(2,1)}, u32[]{:S(2)}) copy-start(bf16[64,4096]{1,0:T(8,128)(2,1)} %q_ref.1) | copy-start | bytes 1572868
  12.5 6.7 %copy-start.1 = (bf16[64,1024]{1,0:T(8,128)(2,1)S(1)}, bf16[64,1024]{1,0:T(8,128)(2,1)}, u32[]{:S(2)}) copy-start(bf16[64,1024]{1,0:T(8,128)(2,1)} %join.1.refs_0_) | copy-start | bytes 393220
  12.5 19.9 %all-to-all-start = ((bf16[16,16,1024]{2,1,0:T(8,128)(2,1)}), bf16[16,16,1024]{2,1,0:T(8,128)(2,1)S(1)}, u32[]{:S(2)}, u32[]{:S(2)}) async-start(bf16[16,16,1024]{2,1,0:T(8,128)(2,1)} %pack.1), calls=%async_computation | async-start | bytes 1048576 | tf_op jit(solution)/shard_map/all_to_all | solution.py:313
  19.2 11.6 %collective-permute-start.5 = (bf16[384,512]{1,0:T(8,128)(2,1)S(1)}, bf16[384,512]{1,0:T(8,128)(2,1)S(1)}, u32[]{:S(2)}, u32[]{:S(2)}) collective-permute-start(bf16[384,512]{1,0:T(8,128)(2,1)S(1)} %get-tuple-element.18), channel_id=1, source_target_pairs={{0,1},{1,0},{2,3},{3,2},{4,5},{5,4},{6,7},{7,6},{8,9},{9,8},{10,11... | collective-permute-start | bytes 1179656 | tf_op jit(solution)/shard_map/ppermute | solution.py:284
  19.3 1.9 %copy-start.3 = (s32[4]{0:T(128)S(1)}, s32[4]{0:T(128)}, u32[]{:S(2)}) copy-start(s32[4]{0:T(128)} %lengths_ref.1) | copy-start | bytes 52
  19.3 8.9 %collective-permute-start.6 = (bf16[128,512]{1,0:T(8,128)(2,1)S(1)}, bf16[128,512]{1,0:T(8,128)(2,1)S(1)}, u32[]{:S(2)}, u32[]{:S(2)}) collective-permute-start(bf16[128,512]{1,0:T(8,128)(2,1)S(1)} %get-tuple-element.19), channel_id=1, source_target_pairs={{0,2},{1,3},{2,0},{3,1},{4,6},{5,7},{6,4},{7,5},{8,10},{9,11},{10,... | collective-permute-start | bytes 393224 | tf_op jit(solution)/shard_map/ppermute | solution.py:284
  20.8 10.1 %collective-permute-start.7 = (bf16[128,512]{1,0:T(8,128)(2,1)S(1)}, bf16[128,512]{1,0:T(8,128)(2,1)S(1)}, u32[]{:S(2)}, u32[]{:S(2)}) collective-permute-start(bf16[128,512]{1,0:T(8,128)(2,1)S(1)} %get-tuple-element.20), channel_id=1, source_target_pairs={{0,3},{1,2},{2,1},{3,0},{4,7},{5,6},{6,5},{7,4},{8,11},{9,10},{10,... | collective-permute-start | bytes 393224 | tf_op jit(solution)/shard_map/ppermute | solution.py:284
  34.7 1.6 %collective-permute-start.8 = (bf16[64,2048]{1,0:T(8,128)(2,1)S(1)}, bf16[64,2048]{1,0:T(8,128)(2,1)S(1)}, u32[]{:S(2)}, u32[]{:S(2)}) collective-permute-start(bf16[64,2048]{1,0:T(8,128)(2,1)S(1)} %get-tuple-element.22), channel_id=1, source_target_pairs={{0,1},{1,0},{2,3},{3,2},{4,5},{5,4},{6,7},{7,6},{8,9},{9,8},{10,11... | collective-permute-start | bytes 786440 | tf_op jit(solution)/shard_map/ppermute | solution.py:284

commit v6 on v5

--- a/solution.py
+++ b/solution.py
@@ -74,20 +74,21 @@
                         out_ref[dest, Q_ROWS:, col : col + width] = kv_refs[index][here, side]
 
 
-def block_offsets(nodes):
-    return [0, CORES, 2 * CORES, 3 * CORES] + list(range(4 * CORES, nodes, 2 * CORES))
-
-
-def join_kernel(k_hbm, v_hbm, out_ref, sems):
+def fetch_kernel(q_hbm, k_hbm, v_hbm, q_ref, kv_ref, sems):
     width = k_hbm.shape[1]
     copies = [
-        pltpu.make_async_copy(k_hbm, out_ref.at[:, pl.ds(0, width)], sems.at[0]),
-        pltpu.make_async_copy(v_hbm, out_ref.at[:, pl.ds(width, width)], sems.at[1]),
+        pltpu.make_async_copy(k_hbm, kv_ref.at[:, pl.ds(0, width)], sems.at[0]),
+        pltpu.make_async_copy(v_hbm, kv_ref.at[:, pl.ds(width, width)], sems.at[1]),
+        pltpu.make_async_copy(q_hbm, q_ref, sems.at[2]),
     ]
     for copy in copies:
         copy.start()
     for copy in copies:
         copy.wait()
+
+
+def block_offsets(nodes):
+    return list(range(nodes - 2 * CORES, 3 * CORES, -2 * CORES)) + [3 * CORES, 2 * CORES, CORES, 0]
 
 
 def heads_kernel(*refs):
@@ -102,8 +103,8 @@
                 block = ref[:, pl.ds(pl.multiple_of(col + half * KVH * HD, width), width)]
                 side = slice(half * width, (half + 1) * width)
                 near[index][lane * rows : (lane + 1) * rows, side] = block
-                if lane >= 4:
-                    far[index][(lane - 4) * rows : (lane - 3) * rows, side] = block
+                if lane < len(lanes) - 4:
+                    far[index][lane * rows : (lane + 1) * rows, side] = block
 
 
 def place_kernel(per_chip, lengths_ref, owner_ref, pos_ref, start_ref, order_ref):
@@ -178,7 +179,7 @@
     offsets = block_offsets(k_all.shape[0] // tokens)
     width = HEADS * HD
     for index, ref in enumerate(pieces):
-        held = offsets if index < CORES else offsets[4:]
+        held = offsets if index < CORES else offsets[:-4]
         for lane, offset in enumerate(held):
             node = jnp.bitwise_xor(me, index ^ offset)
             row = pl.ds(pl.multiple_of(node * tokens, tokens), tokens)
@@ -283,25 +284,24 @@
     def swap(array, offset):
         return lax.ppermute(array, "ctx", [(node, node ^ offset) for node in range(nodes)])
 
+    kv_rows = 0 if apart else rows // 2
+    message = jax.ShapeDtypeStruct((nodes, Q_ROWS + kv_rows, WIDE), jnp.bfloat16)
+    joined = jax.ShapeDtypeStruct((rows, 2 * KVH * HD), jnp.bfloat16)
     if apart:
-        joined = pl.pallas_call(
-            join_kernel,
-            out_shape=jax.ShapeDtypeStruct((rows, 2 * KVH * HD), jnp.bfloat16),
-            in_specs=[hbm] * 2,
-            out_specs=whole,
-            scratch_shapes=[pltpu.SemaphoreType.DMA((2,))],
-            compiler_params=ALL_VMEM,
-            name="join",
-        )(keys, values)
-        offsets = block_offsets(nodes)
-        lanes = [joined] + [swap(joined, offset) for offset in offsets[1:]]
-
-    kv_rows = 0 if apart else rows // 2
-    message = (nodes, Q_ROWS + kv_rows, WIDE)
-    operands = (table, queries) if apart else (table, queries, keys, values)
+        q_near, kv_near = pl.pallas_call(
+            fetch_kernel,
+            out_shape=[jax.ShapeDtypeStruct(queries.shape, jnp.bfloat16), joined],
+            in_specs=[hbm] * 3,
+            out_specs=[whole] * 2,
+            scratch_shapes=[pltpu.SemaphoreType.DMA((3,))],
+            compiler_params=VMEM,
+            name="fetch",
+        )(pltpu.with_memory_space_constraint(queries, pltpu.HBM), pltpu.with_memory_space_constraint(keys, pltpu.HBM), pltpu.with_memory_space_constraint(values, pltpu.HBM))
+        lanes = [kv_near]
+    operands = (table, q_near) if apart else (table, queries, keys, values)
     packed = pl.pallas_call(
         functools.partial(pack_kernel, chips),
-        out_shape=jax.ShapeDtypeStruct(message, jnp.bfloat16),
+        out_shape=message,
         in_specs=[whole] * len(operands),
         out_specs=whole,
         compiler_params=VMEM,
@@ -310,6 +310,9 @@
         ),
         name="pack",
     )(*operands)
+    if apart:
+        lanes = [swap(lanes[0], offset) if offset else lanes[0] for offset in block_offsets(nodes)]
+
     moved = lax.all_to_all(packed, "ctx", split_axis=0, concat_axis=0, tiled=True)
 
     if apart:

time: 37.5 us -> 35.8 us (0.955)
  local copies, waits for them, and re-layouts: 1.06 us -> 0.01 us
  Pallas kernels: 7.73 us -> 7.32 us
    unnamed x8 -> x4, local copies, waits for them, and re-layouts: 1.06 us -> 0.01 us
    ppermute x9, waiting for transfers between devices: 10.8 us -> 11.4 us  [swap(): lax.ppermute(array, 'ctx', [(node, node ^ offset) for node in range(nodes)])]
    all_to_all x1, waiting for transfers between devices: 1.49 us -> 0.91 us  [on_device(): lax.all_to_all(packed, 'ctx', split_axis=0, concat_axis=0, tiled=True)]
    pallas_call x2, Pallas kernels: 2.81 us -> 2.41 us  [the longest x1 1.26 us: on_device(): pl.pallas_call(functools.partial(pack_kernel, chips), out_shape=message,...]
where the time goes in v6:
time: 35.8 us; the launch traced here: 35.6 us
  starting transfers between devices  15.9 us (44%)
  waiting for transfers between devices  12.3 us (34%)
  Pallas kernels  7.32 us (20%)
    ppermute x9, waiting for transfers between devices, swap(): lax.ppermute(array, 'ctx', [(node, node ^ offset) for node in range(nodes)])  11.4 us
    ppermute x9, starting transfers between devices, swap(): lax.ppermute(array, 'ctx', [(node, node ^ offset) for node in range(nodes)])  10.6 us
    all_to_all x1, starting transfers between devices, on_device(): lax.all_to_all(packed, 'ctx', split_axis=0, concat_axis=0, tiled=True)  5.24 us
    pallas_call x1, Pallas kernels, on_device(): pl.pallas_call(attend_kernel, out_shape=(jax.ShapeDtypeStruct((rows, HEAD...  2.4 us
    pallas_call x1, Pallas kernels, on_device(): pl.pallas_call(functools.partial(place_kernel, per_chip), out_shape=(jax....  1.57 us
    pallas_call x1, Pallas kernels, on_device(): pl.pallas_call(functools.partial(pack_kernel, chips), out_shape=message,...  1.26 us
    pallas_call x1, Pallas kernels, on_device(): pl.pallas_call(fetch_kernel, out_shape=[jax.ShapeDtypeStruct(queries.shap...  1.14 us
    all_to_all x1, waiting for transfers between devices, on_device(): lax.all_to_all(packed, 'ctx', split_axis=0, concat_axis=0, tiled=True)  0.91 us
  transfers between devices with their start and end apart: 10, of which 6 were waited for; matrix products, arithmetic and copies ran while one was open for 0% of the time, Pallas kernels for 8%

profile of v6, /device:TPU:0, one launch (start us, length us, event | category | flops | bytes accessed | tf_op | source)
XLA Modules:
  0.0 35.6 jit_solution(11010147584422084124)
XLA Ops:
  0.0 1.1 %fetch.1 = (bf16[64,4096]{1,0:T(8,128)(2,1)S(1)}, bf16[64,1024]{1,0:T(8,128)(2,1)S(1)}) custom-call(bf16[64,4096]{1,0:T(8,128)(2,1)} %q_hbm.1, bf16[64,512]{1,0:T(8,128)(2,1)} %k_hbm.1, bf16[64,512]{1,0:T(8,128)(2,1)} %v_hbm.1), custom_call_target="tpu_custom_call" | custom-call | tf_op jit(solution)/shard_map/fetch/pallas_call | solution.py:291
  1.2 0.0 copy-start
  1.2 5.1 %collective-permute-start = (bf16[64,1024]{1,0:T(8,128)(2,1)S(1)}, bf16[64,1024]{1,0:T(8,128)(2,1)S(1)}, u32[]{:S(2)}, u32[]{:S(2)}) collective-permute-start(bf16[64,1024]{1,0:T(8,128)(2,1)S(1)} %get-tuple-element.20.refs_5_), channel_id=1, source_target_pairs={{0,12},{1,13},{2,14},{3,15},{4,8},{5,9},{6,10},{7,11},{8,4},{9,5},... | collective-permute-start | bytes 393224 | tf_op jit(solution)/shard_map/ppermute | solution.py:285
  6.3 0.0 collective-permute-start.1
  6.3 1.7 %collective-permute-start.2 = (bf16[64,1024]{1,0:T(8,128)(2,1)S(1)}, bf16[64,1024]{1,0:T(8,128)(2,1)S(1)}, u32[]{:S(2)}, u32[]{:S(2)}) collective-permute-start(bf16[64,1024]{1,0:T(8,128)(2,1)S(1)} %get-tuple-element.20.refs_5_), channel_id=1, source_target_pairs={{0,6},{1,7},{2,4},{3,5},{4,2},{5,3},{6,0},{7,1},{8,14},{9,15},{10,... | collective-permute-start | bytes 393224 | tf_op jit(solution)/shard_map/ppermute | solution.py:285
  8.0 1.2 %collective-permute-start.3 = (bf16[64,1024]{1,0:T(8,128)(2,1)S(1)}, bf16[64,1024]{1,0:T(8,128)(2,1)S(1)}, u32[]{:S(2)}, u32[]{:S(2)}) collective-permute-start(bf16[64,1024]{1,0:T(8,128)(2,1)S(1)} %get-tuple-element.20.refs_5_), channel_id=1, source_target_pairs={{0,4},{1,5},{2,6},{3,7},{4,0},{5,1},{6,2},{7,3},{8,12},{9,13},{10,... | collective-permute-start | bytes 393224 | tf_op jit(solution)/shard_map/ppermute | solution.py:285
  9.3 0.5 %collective-permute-start.4 = (bf16[64,1024]{1,0:T(8,128)(2,1)S(1)}, bf16[64,1024]{1,0:T(8,128)(2,1)S(1)}, u32[]{:S(2)}, u32[]{:S(2)}) collective-permute-start(bf16[64,1024]{1,0:T(8,128)(2,1)S(1)} %get-tuple-element.20.refs_5_), channel_id=1, source_target_pairs={{0,2},{1,3},{2,0},{3,1},{4,6},{5,7},{6,4},{7,5},{8,10},{9,11},{10,... | collective-permute-start | bytes 393224 | tf_op jit(solution)/shard_map/ppermute | solution.py:285
  9.8 0.0 copy-done
  9.8 1.3 %pack.1 = bf16[16,16,1024]{2,1,0:T(8,128)(2,1)} custom-call(s32[8,128]{1,0:T(8,128)S(1)} %bitcast.1, bf16[64,4096]{1,0:T(8,128)(2,1)S(1)} %get-tuple-element.16.q_ref), custom_call_target="tpu_custom_call" | custom-call | flops 33554432 | bytes 1048576 | tf_op jit(solution)/shard_map/pack/pallas_call | solution.py:302
  11.0 5.2 %all-to-all-start = ((bf16[16,16,1024]{2,1,0:T(8,128)(2,1)}), bf16[16,16,1024]{2,1,0:T(8,128)(2,1)S(1)}, u32[]{:S(2)}, u32[]{:S(2)}) async-start(bf16[16,16,1024]{2,1,0:T(8,128)(2,1)} %pack.1), calls=%async_computation | async-start | bytes 1048576 | tf_op jit(solution)/shard_map/all_to_all | solution.py:316
  16.3 0.0 collective-permute-done.refs_0_
  16.3 1.2 %collective-permute-done.1.refs_1_ = bf16[64,1024]{1,0:T(8,128)(2,1)S(1)} collective-permute-done((bf16[64,1024]{1,0:T(8,128)(2,1)S(1)}, bf16[64,1024]{1,0:T(8,128)(2,1)S(1)}, u32[]{:S(2)}, u32[]{:S(2)}) %collective-permute-start.1) | collective-permute-done | bytes 131104 | tf_op jit(solution)/shard_map/ppermute | solution.py:285
  17.5 0.0 collective-permute-done.2.refs_2_
  17.5 1.0 %collective-permute-done.3.refs_3_ = bf16[64,1024]{1,0:T(8,128)(2,1)S(1)} collective-permute-done((bf16[64,1024]{1,0:T(8,128)(2,1)S(1)}, bf16[64,1024]{1,0:T(8,128)(2,1)S(1)}, u32[]{:S(2)}, u32[]{:S(2)}) %collective-permute-start.3) | collective-permute-done | bytes 131104 | tf_op jit(solution)/shard_map/ppermute | solution.py:285
  18.5 0.0 collective-permute-done.4.refs_4_
  18.5 0.1 heads.1
  18.6 0.1 collective-permute-start.5
  18.7 0.0 copy-start.1
  18.7 1.4 %collective-permute-start.6 = (bf16[128,512]{1,0:T(8,128)(2,1)S(1)}, bf16[128,512]{1,0:T(8,128)(2,1)S(1)}, u32[]{:S(2)}, u32[]{:S(2)}) collective-permute-start(bf16[128,512]{1,0:T(8,128)(2,1)S(1)} %get-tuple-element.23), channel_id=1, source_target_pairs={{0,2},{1,3},{2,0},{3,1},{4,6},{5,7},{6,4},{7,5},{8,10},{9,11},{10,... | collective-permute-start | bytes 393224 | tf_op jit(solution)/shard_map/ppermute | solution.py:285
  20.1 0.4 %collective-permute-start.7 = (bf16[128,512]{1,0:T(8,128)(2,1)S(1)}, bf16[128,512]{1,0:T(8,128)(2,1)S(1)}, u32[]{:S(2)}, u32[]{:S(2)}) collective-permute-start(bf16[128,512]{1,0:T(8,128)(2,1)S(1)} %get-tuple-element.24), channel_id=1, source_target_pairs={{0,3},{1,2},{2,1},{3,0},{4,7},{5,6},{6,5},{7,4},{8,11},{9,10},{10,... | collective-permute-start | bytes 393224 | tf_op jit(solution)/shard_map/ppermute | solution.py:285
  20.6 0.0 copy-done.1
  20.6 1.6 %place.1 = (s32[128,128]{1,0:T(8,128)S(1)}, s32[128,128]{1,0:T(8,128)S(1)}, bf16[128,128]{1,0:T(8,128)(2,1)S(1)}) custom-call(s32[4]{0:T(128)S(1)} %copy-done.1, s32[8,128]{1,0:T(8,128)S(1)} %bitcast.2), custom_call_target="tpu_custom_call" | custom-call | tf_op jit(solution)/shard_map/place/pallas_call | solution.py:342
  22.2 4.4 %collective-permute-done.6.refs_2_ = bf16[128,512]{1,0:T(8,128)(2,1)S(1)} collective-permute-done((bf16[128,512]{1,0:T(8,128)(2,1)S(1)}, bf16[128,512]{1,0:T(8,128)(2,1)S(1)}, u32[]{:S(2)}, u32[]{:S(2)}) %collective-permute-start.6) | collective-permute-done | bytes 131104 | tf_op jit(solution)/shard_map/ppermute | solution.py:285
  26.5 3.3 %collective-permute-done.7.refs_3_ = bf16[128,512]{1,0:T(8,128)(2,1)S(1)} collective-permute-done((bf16[128,512]{1,0:T(8,128)(2,1)S(1)}, bf16[128,512]{1,0:T(8,128)(2,1)S(1)}, u32[]{:S(2)}, u32[]{:S(2)}) %collective-permute-start.7) | collective-permute-done | bytes 131104 | tf_op jit(solution)/shard_map/ppermute | solution.py:285
  29.8 0.0 collective-permute-done.5.refs_1_
  29.9 0.9 %all-to-all-done.q_ref = bf16[16,16,1024]{2,1,0:T(8,128)(2,1)S(1)} async-done(((bf16[16,16,1024]{2,1,0:T(8,128)(2,1)}), bf16[16,16,1024]{2,1,0:T(8,128)(2,1)S(1)}, u32[]{:S(2)}, u32[]{:S(2)}) %all-to-all-start) | async-done | bytes 524320 | tf_op jit(solution)/shard_map/all_to_all | solution.py:316
  30.8 2.4 %attend.1 = (bf16[64,2048]{1,0:T(8,128)(2,1)S(1)}, bf16[64,2048]{1,0:T(8,128)(2,1)S(1)}) custom-call(bf16[16,16,1024]{2,1,0:T(8,128)(2,1)S(1)} %all-to-all-done.q_ref, s32[128,128]{1,0:T(8,128)S(1)} %get-tuple-element.17.pos_ref, s32[128,128]{1,0:T(8,128)S(1)} %get-tuple-element.18.start_ref, bf16[128,128]{1,0:T(8,128)(2,1)S(1)} %get-tuple-element.19.order_ref, ...), custom_call_target="tpu_custom_call" | custom-call | tf_op jit(solution)/shard_map/attend/pallas_call | solution.py:355
  33.2 0.1 collective-permute-start.8
  33.2 1.5 %collective-permute-done.8.refs_1_ = bf16[64,2048]{1,0:T(8,128)(2,1)S(1)} collective-permute-done((bf16[64,2048]{1,0:T(8,128)(2,1)S(1)}, bf16[64,2048]{1,0:T(8,128)(2,1)S(1)}, u32[]{:S(2)}, u32[]{:S(2)}) %collective-permute-start.8) | collective-permute-done | bytes 262176 | tf_op jit(solution)/shard_map/ppermute | solution.py:285
  34.8 0.8 %assemble.1 = bf16[64,4096]{1,0:T(8,128)(2,1)} custom-call(bf16[64,2048]{1,0:T(8,128)(2,1)S(1)} %get-tuple-element.25.refs_0_, bf16[64,2048]{1,0:T(8,128)(2,1)S(1)} %collective-permute-done.8.refs_1_), custom_call_target="tpu_custom_call" | custom-call | tf_op jit(solution)/shard_map/assemble/pallas_call | solution.py:369
Async XLA Ops:
  1.2 8.6 %copy-start = (s32[1024]{0:T(1024)S(1)}, s32[1024]{0:T(1024)}, u32[]{:S(2)}) copy-start(s32[1024]{0:T(1024)} %param.8) | copy-start | bytes 12292
  1.2 15.1 %collective-permute-start = (bf16[64,1024]{1,0:T(8,128)(2,1)S(1)}, bf16[64,1024]{1,0:T(8,128)(2,1)S(1)}, u32[]{:S(2)}, u32[]{:S(2)}) collective-permute-start(bf16[64,1024]{1,0:T(8,128)(2,1)S(1)} %get-tuple-element.20.refs_5_), channel_id=1, source_target_pairs={{0,12},{1,13},{2,14},{3,15},{4,8},{5,9},{6,10},{7,11},{8,4},{9,5},... | collective-permute-start | bytes 393224 | tf_op jit(solution)/shard_map/ppermute | solution.py:285
  6.3 11.2 %collective-permute-start.1 = (bf16[64,1024]{1,0:T(8,128)(2,1)S(1)}, bf16[64,1024]{1,0:T(8,128)(2,1)S(1)}, u32[]{:S(2)}, u32[]{:S(2)}) collective-permute-start(bf16[64,1024]{1,0:T(8,128)(2,1)S(1)} %get-tuple-element.20.refs_5_), channel_id=1, source_target_pairs={{0,8},{1,9},{2,10},{3,11},{4,12},{5,13},{6,14},{7,15},{8,0},{9,1},... | collective-permute-start | bytes 393224 | tf_op jit(solution)/shard_map/ppermute | solution.py:285
  6.3 11.2 %collective-permute-start.2 = (bf16[64,1024]{1,0:T(8,128)(2,1)S(1)}, bf16[64,1024]{1,0:T(8,128)(2,1)S(1)}, u32[]{:S(2)}, u32[]{:S(2)}) collective-permute-start(bf16[64,1024]{1,0:T(8,128)(2,1)S(1)} %get-tuple-element.20.refs_5_), channel_id=1, source_target_pairs={{0,6},{1,7},{2,4},{3,5},{4,2},{5,3},{6,0},{7,1},{8,14},{9,15},{10,... | collective-permute-start | bytes 393224 | tf_op jit(solution)/shard_map/ppermute | solution.py:285
  8.0 10.5 %collective-permute-start.3 = (bf16[64,1024]{1,0:T(8,128)(2,1)S(1)}, bf16[64,1024]{1,0:T(8,128)(2,1)S(1)}, u32[]{:S(2)}, u32[]{:S(2)}) collective-permute-start(bf16[64,1024]{1,0:T(8,128)(2,1)S(1)} %get-tuple-element.20.refs_5_), channel_id=1, source_target_pairs={{0,4},{1,5},{2,6},{3,7},{4,0},{5,1},{6,2},{7,3},{8,12},{9,13},{10,... | collective-permute-start | bytes 393224 | tf_op jit(solution)/shard_map/ppermute | solution.py:285
  9.3 9.3 %collective-permute-start.4 = (bf16[64,1024]{1,0:T(8,128)(2,1)S(1)}, bf16[64,1024]{1,0:T(8,128)(2,1)S(1)}, u32[]{:S(2)}, u32[]{:S(2)}) collective-permute-start(bf16[64,1024]{1,0:T(8,128)(2,1)S(1)} %get-tuple-element.20.refs_5_), channel_id=1, source_target_pairs={{0,2},{1,3},{2,0},{3,1},{4,6},{5,7},{6,4},{7,5},{8,10},{9,11},{10,... | collective-permute-start | bytes 393224 | tf_op jit(solution)/shard_map/ppermute | solution.py:285
  11.0 19.7 %all-to-all-start = ((bf16[16,16,1024]{2,1,0:T(8,128)(2,1)}), bf16[16,16,1024]{2,1,0:T(8,128)(2,1)S(1)}, u32[]{:S(2)}, u32[]{:S(2)}) async-start(bf16[16,16,1024]{2,1,0:T(8,128)(2,1)} %pack.1), calls=%async_computation | async-start | bytes 1048576 | tf_op jit(solution)/shard_map/all_to_all | solution.py:316
  18.6 11.2 %collective-permute-start.5 = (bf16[384,512]{1,0:T(8,128)(2,1)S(1)}, bf16[384,512]{1,0:T(8,128)(2,1)S(1)}, u32[]{:S(2)}, u32[]{:S(2)}) collective-permute-start(bf16[384,512]{1,0:T(8,128)(2,1)S(1)} %get-tuple-element.22), channel_id=1, source_target_pairs={{0,1},{1,0},{2,3},{3,2},{4,5},{5,4},{6,7},{7,6},{8,9},{9,8},{10,11... | collective-permute-start | bytes 1179656 | tf_op jit(solution)/shard_map/ppermute | solution.py:285
  18.7 1.9 %copy-start.1 = (s32[4]{0:T(128)S(1)}, s32[4]{0:T(128)}, u32[]{:S(2)}) copy-start(s32[4]{0:T(128)} %lengths_ref.1) | copy-start | bytes 52
  18.7 7.8 %collective-permute-start.6 = (bf16[128,512]{1,0:T(8,128)(2,1)S(1)}, bf16[128,512]{1,0:T(8,128)(2,1)S(1)}, u32[]{:S(2)}, u32[]{:S(2)}) collective-permute-start(bf16[128,512]{1,0:T(8,128)(2,1)S(1)} %get-tuple-element.23), channel_id=1, source_target_pairs={{0,2},{1,3},{2,0},{3,1},{4,6},{5,7},{6,4},{7,5},{8,10},{9,11},{10,... | collective-permute-start | bytes 393224 | tf_op jit(solution)/shard_map/ppermute | solution.py:285
  20.1 9.7 %collective-permute-start.7 = (bf16[128,512]{1,0:T(8,128)(2,1)S(1)}, bf16[128,512]{1,0:T(8,128)(2,1)S(1)}, u32[]{:S(2)}, u32[]{:S(2)}) collective-permute-start(bf16[128,512]{1,0:T(8,128)(2,1)S(1)} %get-tuple-element.24), channel_id=1, source_target_pairs={{0,3},{1,2},{2,1},{3,0},{4,7},{5,6},{6,5},{7,4},{8,11},{9,10},{10,... | collective-permute-start | bytes 393224 | tf_op jit(solution)/shard_map/ppermute | solution.py:285
  33.2 1.6 %collective-permute-start.8 = (bf16[64,2048]{1,0:T(8,128)(2,1)S(1)}, bf16[64,2048]{1,0:T(8,128)(2,1)S(1)}, u32[]{:S(2)}, u32[]{:S(2)}) collective-permute-start(bf16[64,2048]{1,0:T(8,128)(2,1)S(1)} %get-tuple-element.26), channel_id=1, source_target_pairs={{0,1},{1,0},{2,3},{3,2},{4,5},{5,4},{6,7},{7,6},{8,9},{9,8},{10,11... | collective-permute-start | bytes 786440 | tf_op jit(solution)/shard_map/ppermute | solution.py:285

commit v7 on v6

--- a/solution.py
+++ b/solution.py
@@ -20,7 +20,6 @@
 SUB = 8
 Q_ROWS = HEADS * SUB
 VMEM = pltpu.CompilerParams(vmem_limit_bytes=40 * 2**20)
-ALL_VMEM = pltpu.CompilerParams(vmem_limit_bytes=64 * 2**20 - 2**17)
 
 
 def row_to_column(row):
@@ -37,11 +36,18 @@
     return jnp.sum(jnp.where(here == there, column, 0), axis=0, keepdims=True)
 
 
-def pack_kernel(chips, owner_ref, q_ref, *refs):
-    kv_refs, out_ref = refs[:-1], refs[-1]
+def fetch_kernel(owner_hbm, q_hbm, k_hbm, v_hbm, order_ref, q_ref, kv_ref, owner_ref, sems):
     me = lax.axis_index("ctx")
-    rows = q_ref.shape[0]
-    per_chip = rows // chips
+    rows, width = k_hbm.shape
+    copies = [
+        pltpu.make_async_copy(owner_hbm, owner_ref, sems.at[0]),
+        pltpu.make_async_copy(k_hbm, kv_ref.at[:, pl.ds(0, width)], sems.at[1]),
+        pltpu.make_async_copy(v_hbm, kv_ref.at[:, pl.ds(width, width)], sems.at[2]),
+        pltpu.make_async_copy(q_hbm, q_ref, sems.at[3]),
+    ]
+    for copy in copies:
+        copy.start()
+    copies[0].wait()
     both = owner_ref[pl.ds(me // 2, 1), :]
     swapped = jnp.concatenate((both[:, rows:], both[:, :rows]), axis=1)
     own = jnp.where(me % 2 == 1, swapped, both)[:, :rows]
@@ -49,7 +55,16 @@
     key_row = own * rows + token
     rank = jnp.sum((row_to_column(key_row) < key_row).astype(jnp.int32), axis=0, keepdims=True)
     place = lax.broadcasted_iota(jnp.int32, (rows, rows), 0)
-    order = (place == rank).astype(jnp.float32).astype(jnp.bfloat16)
+    order_ref[...] = (place == rank).astype(jnp.float32).astype(jnp.bfloat16)
+    for copy in copies[1:]:
+        copy.wait()
+
+
+def pack_kernel(chips, order_ref, q_ref, *refs):
+    kv_refs, out_ref = refs[:-1], refs[-1]
+    rows = q_ref.shape[0]
+    per_chip = rows // chips
+    order = order_ref[...]
     for core in range(CORES):
         sorted_q = []
         for head in range(core * HEADS, (core + 1) * HEADS):
@@ -65,26 +80,14 @@
             out_ref[dest, :Q_ROWS, :] = jnp.concatenate(parts, axis=0).astype(jnp.bfloat16)
             if kv_refs:
                 width = HEADS * HD
-                side = slice(core * width, (core + 1) * width)
                 half = rows // 2
                 for part in range(2):
                     here = slice(part * half, (part + 1) * half)
                     for index in range(2):
                         col = (2 * part + index) * width
-                        out_ref[dest, Q_ROWS:, col : col + width] = kv_refs[index][here, side]
-
-
-def fetch_kernel(q_hbm, k_hbm, v_hbm, q_ref, kv_ref, sems):
-    width = k_hbm.shape[1]
-    copies = [
-        pltpu.make_async_copy(k_hbm, kv_ref.at[:, pl.ds(0, width)], sems.at[0]),
-        pltpu.make_async_copy(v_hbm, kv_ref.at[:, pl.ds(width, width)], sems.at[1]),
-        pltpu.make_async_copy(q_hbm, q_ref, sems.at[2]),
-    ]
-    for copy in copies:
-        copy.start()
-    for copy in copies:
-        copy.wait()
+                        side = index * KVH * HD + core * width
+                        block = kv_refs[0][here, side : side + width]
+                        out_ref[dest, Q_ROWS:, col : col + width] = block
 
 
 def block_offsets(nodes):
@@ -207,53 +210,75 @@
     else:
         unpack_pieces(kv_refs, held // CORES, k_all, v_all)
 
-    for block in range(blocks):
-        here = slice(block * block_rows, (block + 1) * block_rows)
+    def rows_of(block):
+        return slice(block * block_rows, (block + 1) * block_rows)
+
+    def scores_of(block, head, keys):
         parts = block_rows // SUB
-        messages = [q_ref[block * parts + part].astype(jnp.float32) for part in range(parts)]
-        pos = pos_ref[here, :1]
-        start = start_ref[here, :1]
-        low, high = max(0, block - blocks // 2) * span, (block + 1) * span
-        chunk = min(high - low, 1024)
-        for head in range(HEADS):
-            pieces = []
-            for group in range(GROUP):
-                for message in messages:
-                    rows = slice(head * SUB, (head + 1) * SUB)
-                    pieces.append(message[rows, group * HD : (group + 1) * HD])
-            queries = jnp.concatenate(pieces, axis=0).astype(jnp.bfloat16)
-            peak, acc = None, None
-            for lower in range(low, high, chunk):
-                keys = slice(lower, lower + chunk)
-                scores = lax.dot_general(
-                    queries,
-                    k_all[keys, head * HD : (head + 1) * HD],
-                    (((1,), (1,)), ((), ())),
-                    preferred_element_type=jnp.float32,
-                )
-                at = lower + lax.broadcasted_iota(jnp.int32, (block_rows, chunk), 1)
-                seen = (at <= pos) & (at >= start)
-                bias = jnp.where(seen, 0.0, NEGATIVE)
-                scores = scores.reshape(GROUP, block_rows, chunk) + bias[None]
-                scores = scores.reshape(GROUP * block_rows, chunk)
-                top = jnp.max(scores, axis=1, keepdims=True)
-                if peak is not None:
-                    top = jnp.maximum(peak, top)
-                probs = jnp.exp2((scores - top) * scale)
-                if chunk != high - low:
-                    probs = probs.reshape(GROUP, block_rows, chunk)
-                    probs = jnp.where(seen[None], probs, 0.0).reshape(GROUP * block_rows, chunk)
-                new = jnp.dot(
-                    probs.astype(jnp.bfloat16),
-                    v_all[keys, 2 * head * HD : (2 * head + 2) * HD],
-                    preferred_element_type=jnp.float32,
-                )
-                acc = new if acc is None else acc * jnp.exp2((peak - top) * scale) + new
+        mine = slice(head * SUB, (head + 1) * SUB)
+        messages = [q_ref[block * parts + part].astype(jnp.float32)[mine] for part in range(parts)]
+        pieces = []
+        for group in range(GROUP):
+            for message in messages:
+                pieces.append(message[:, group * HD : (group + 1) * HD])
+        return lax.dot_general(
+            jnp.concatenate(pieces, axis=0).astype(jnp.bfloat16),
+            k_all[keys, head * HD : (head + 1) * HD],
+            (((1,), (1,)), ((), ())),
+            preferred_element_type=jnp.float32,
+        )
+
+    def weights_of(block, keys, scores, peak=None):
+        count = keys.stop - keys.start
+        at = keys.start + lax.broadcasted_iota(jnp.int32, (block_rows, count), 1)
+        seen = (at <= pos_ref[rows_of(block), :1]) & (at >= start_ref[rows_of(block), :1])
+        scores = scores.reshape(GROUP, block_rows, count) + jnp.where(seen, 0.0, NEGATIVE)[None]
+        scores = scores.reshape(GROUP * block_rows, count)
+        top = jnp.max(scores, axis=1, keepdims=True)
+        if peak is None:
+            return top, jnp.exp2((scores - top) * scale).astype(jnp.bfloat16)
+        top = jnp.maximum(peak, top)
+        weights = jnp.exp2((scores - top) * scale).reshape(GROUP, block_rows, count)
+        weights = jnp.where(seen[None], weights, 0.0).reshape(GROUP * block_rows, count)
+        return top, weights.astype(jnp.bfloat16)
+
+    def sums_of(head, keys, weights):
+        values = v_all[keys, 2 * head * HD : (2 * head + 2) * HD]
+        return jnp.dot(weights, values, preferred_element_type=jnp.float32)
+
+    def store(block, head, sums):
+        result = (sums[:, :HD] / sums[:, HD:]).astype(jnp.bfloat16)
+        for group in range(GROUP):
+            col = head * WIDE + group * HD
+            part = result[group * block_rows : (group + 1) * block_rows]
+            context[rows_of(block), col : col + HD] = part
+
+    tasks = [
+        (block, head, slice(max(0, block - blocks // 2) * span, (block + 1) * span))
+        for block in reversed(range(blocks))
+        for head in range(HEADS)
+    ]
+    most = 1024
+    if max(keys.stop - keys.start for _, _, keys in tasks) <= most:
+        scores, last = scores_of(*tasks[0]), None
+        for index, (block, head, keys) in enumerate(tasks):
+            later = scores_of(*tasks[index + 1]) if index + 1 < len(tasks) else None
+            _, weights = weights_of(block, keys, scores)
+            if last is not None:
+                store(*last[:2], sums_of(*last[1:]))
+            scores, last = later, (block, head, keys, weights)
+        store(*last[:2], sums_of(*last[1:]))
+    else:
+        for block, head, keys in tasks:
+            peak = jnp.full((GROUP * block_rows, 1), NEGATIVE, jnp.float32)
+            sums = jnp.zeros((GROUP * block_rows, 2 * HD), jnp.float32)
+            for lower in range(keys.start, keys.stop, most):
+                part = slice(lower, min(lower + most, keys.stop))
+                top, weights = weights_of(block, part, scores_of(block, head, part), peak)
+                sums = sums * jnp.exp2((peak - top) * scale) + sums_of(head, part, weights)
                 peak = top
-            result = (acc[:, :HD] / acc[:, HD:]).astype(jnp.bfloat16)
-            for group in range(GROUP):
-                col = head * WIDE + group * HD
-                context[here, col : col + HD] = result[group * block_rows : (group + 1) * block_rows]
+            store(block, head, sums)
+
     rows = held // CORES
     for core in range(CORES):
         order = order_ref[core * rows : (core + 1) * rows, :]
@@ -261,12 +286,14 @@
         out_refs[core][...] = moved.astype(jnp.bfloat16)
 
 
-def assemble_kernel(*refs):
-    core = lax.axis_index("ctx") % CORES
+def write_kernel(other, heads_ref, *refs):
+    out_hbm, sem = refs[-2:]
+    core = jnp.bitwise_xor(lax.axis_index("ctx") % CORES, other)
     width = HEADS * WIDE
-    for index in range(CORES):
-        col = pl.multiple_of(jnp.bitwise_xor(core, index) * width, width)
-        refs[CORES][:, pl.ds(col, width)] = refs[index][...]
+    side = pl.ds(pl.multiple_of(core * width, width), width)
+    copy = pltpu.make_async_copy(heads_ref, out_hbm.at[:, side], sem)
+    copy.start()
+    copy.wait()
 
 
 def on_device(queries, keys, values, owner, rollout_lengths):
@@ -286,19 +313,20 @@
 
     kv_rows = 0 if apart else rows // 2
     message = jax.ShapeDtypeStruct((nodes, Q_ROWS + kv_rows, WIDE), jnp.bfloat16)
-    joined = jax.ShapeDtypeStruct((rows, 2 * KVH * HD), jnp.bfloat16)
-    if apart:
-        q_near, kv_near = pl.pallas_call(
-            fetch_kernel,
-            out_shape=[jax.ShapeDtypeStruct(queries.shape, jnp.bfloat16), joined],
-            in_specs=[hbm] * 3,
-            out_specs=[whole] * 2,
-            scratch_shapes=[pltpu.SemaphoreType.DMA((3,))],
-            compiler_params=VMEM,
-            name="fetch",
-        )(pltpu.with_memory_space_constraint(queries, pltpu.HBM), pltpu.with_memory_space_constraint(keys, pltpu.HBM), pltpu.with_memory_space_constraint(values, pltpu.HBM))
-        lanes = [kv_near]
-    operands = (table, q_near) if apart else (table, queries, keys, values)
+    order_in, q_near, kv_near = pl.pallas_call(
+        fetch_kernel,
+        out_shape=[
+            jax.ShapeDtypeStruct((rows, rows), jnp.bfloat16),
+            jax.ShapeDtypeStruct(queries.shape, jnp.bfloat16),
+            jax.ShapeDtypeStruct((rows, 2 * KVH * HD), jnp.bfloat16),
+        ],
+        in_specs=[hbm] * 4,
+        out_specs=[whole] * 3,
+        scratch_shapes=[pltpu.VMEM(table.shape, jnp.int32), pltpu.SemaphoreType.DMA((4,))],
+        compiler_params=VMEM,
+        name="fetch",
+    )(*(pltpu.with_memory_space_constraint(x, pltpu.HBM) for x in (table, queries, keys, values)))
+    operands = (order_in, q_near) if apart else (order_in, q_near, kv_near)
     packed = pl.pallas_call(
         functools.partial(pack_kernel, chips),
         out_shape=message,
@@ -311,7 +339,7 @@
         name="pack",
     )(*operands)
     if apart:
-        lanes = [swap(lanes[0], offset) if offset else lanes[0] for offset in block_offsets(nodes)]
+        lanes = [swap(kv_near, offset) if offset else kv_near for offset in block_offsets(nodes)]
 
     moved = lax.all_to_all(packed, "ctx", split_axis=0, concat_axis=0, tiled=True)
 
@@ -366,14 +394,26 @@
         name="attend",
     )(q_part, pos, start, order, *kv_parts)
 
+    result = jax.ShapeDtypeStruct((rows, H * HD), jnp.bfloat16)
+    half = pl.pallas_call(
+        functools.partial(write_kernel, 0),
+        out_shape=result,
+        in_specs=[whole],
+        out_specs=hbm,
+        scratch_shapes=[pltpu.SemaphoreType.DMA],
+        compiler_params=VMEM,
+        name="write_own",
+    )(own)
     return pl.pallas_call(
-        assemble_kernel,
-        out_shape=jax.ShapeDtypeStruct((rows, H * HD), jnp.bfloat16),
-        in_specs=[whole] * CORES,
-        out_specs=whole,
-        compiler_params=VMEM,
-        name="assemble",
-    )(own, swap(other, 1))
+        functools.partial(write_kernel, 1),
+        out_shape=result,
+        in_specs=[whole, hbm],
+        out_specs=hbm,
+        scratch_shapes=[pltpu.SemaphoreType.DMA],
+        input_output_aliases={1: 0},
+        compiler_params=VMEM,
+        name="write_received",
+    )(swap(other, 1), half)
 
 
 def solution(mesh):

time: 35.8 us -> 35.2 us (0.983)
  waiting for transfers between devices: 12.3 us -> 11.6 us
    ppermute x9, waiting for transfers between devices: 11.4 us -> 10.7 us  [swap(): lax.ppermute(array, 'ctx', [(node, node ^ offset) for node in range(nodes)])]
    pallas_call x2 -> x3, Pallas kernels: 1.98 us -> 2.6 us  [the longest x1 1.17 us: on_device(): pl.pallas_call(fetch_kernel, out_shape=[jax.ShapeDtypeStruct((rows, rows)...]
  transfers between devices with their start and end apart: 10 -> 10, of which waited for: 6 -> 6; matrix products, arithmetic and copies ran while one was open for 0% -> 0% of each run, Pallas kernels for 8% -> 10%
where the time goes in v7:
time: 35.2 us; the launch traced here: 35 us
  starting transfers between devices  15.9 us (45%)
  waiting for transfers between devices  11.6 us (33%)
  Pallas kernels  7.42 us (21%)
    ppermute x9, waiting for transfers between devices, swap(): lax.ppermute(array, 'ctx', [(node, node ^ offset) for node in range(nodes)])  10.7 us
    ppermute x9, starting transfers between devices, swap(): lax.ppermute(array, 'ctx', [(node, node ^ offset) for node in range(nodes)])  10.6 us
    all_to_all x1, starting transfers between devices, on_device(): lax.all_to_all(packed, 'ctx', split_axis=0, concat_axis=0, tiled=True)  5.26 us
    pallas_call x1, Pallas kernels, on_device(): pl.pallas_call(attend_kernel, out_shape=(jax.ShapeDtypeStruct((rows, HEAD...  2.07 us
    pallas_call x1, Pallas kernels, on_device(): pl.pallas_call(functools.partial(place_kernel, per_chip), out_shape=(jax....  1.57 us
    pallas_call x1, Pallas kernels, on_device(): pl.pallas_call(fetch_kernel, out_shape=[jax.ShapeDtypeStruct((rows, rows)...  1.17 us
    pallas_call x1, Pallas kernels, on_device(): pl.pallas_call(functools.partial(pack_kernel, chips), out_shape=message,...  1.07 us
    all_to_all x1, waiting for transfers between devices, on_device(): lax.all_to_all(packed, 'ctx', split_axis=0, concat_axis=0, tiled=True)  0.87 us
  transfers between devices with their start and end apart: 10, of which 6 were waited for; matrix products, arithmetic and copies ran while one was open for 0% of the time, Pallas kernels for 10%

profile of v7, /device:TPU:0, one launch (start us, length us, event | category | flops | bytes accessed | tf_op | source)
XLA Modules:
  0.0 35.0 jit_solution(12208481896348261599)
XLA Ops:
  0.0 1.2 %fetch.1 = (bf16[64,64]{1,0:T(8,128)(2,1)S(1)}, bf16[64,4096]{1,0:T(8,128)(2,1)S(1)}, bf16[64,1024]{1,0:T(8,128)(2,1)S(1)}) custom-call(s32[8,128]{1,0:T(8,128)} %bitcast.1, bf16[64,4096]{1,0:T(8,128)(2,1)} %q_hbm.1, bf16[64,512]{1,0:T(8,128)(2,1)} %k_hbm.1, bf16[64,512]{1,0:T(8,128)(2,1)} %v_hbm.1), custom_call_target="tpu_custom_call" | custom-call | tf_op jit(solution)/shard_map/fetch/pallas_call | solution.py:316
  1.2 5.1 %collective-permute-start = (bf16[64,1024]{1,0:T(8,128)(2,1)S(1)}, bf16[64,1024]{1,0:T(8,128)(2,1)S(1)}, u32[]{:S(2)}, u32[]{:S(2)}) collective-permute-start(bf16[64,1024]{1,0:T(8,128)(2,1)S(1)} %get-tuple-element.22.refs_5_), channel_id=1, source_target_pairs={{0,12},{1,13},{2,14},{3,15},{4,8},{5,9},{6,10},{7,11},{8,4},{9,5},... | collective-permute-start | bytes 393224 | tf_op jit(solution)/shard_map/ppermute | solution.py:312
  6.3 0.0 collective-permute-start.1
  6.3 1.7 %collective-permute-start.2 = (bf16[64,1024]{1,0:T(8,128)(2,1)S(1)}, bf16[64,1024]{1,0:T(8,128)(2,1)S(1)}, u32[]{:S(2)}, u32[]{:S(2)}) collective-permute-start(bf16[64,1024]{1,0:T(8,128)(2,1)S(1)} %get-tuple-element.22.refs_5_), channel_id=1, source_target_pairs={{0,6},{1,7},{2,4},{3,5},{4,2},{5,3},{6,0},{7,1},{8,14},{9,15},{10,... | collective-permute-start | bytes 393224 | tf_op jit(solution)/shard_map/ppermute | solution.py:312
  8.0 1.2 %collective-permute-start.3 = (bf16[64,1024]{1,0:T(8,128)(2,1)S(1)}, bf16[64,1024]{1,0:T(8,128)(2,1)S(1)}, u32[]{:S(2)}, u32[]{:S(2)}) collective-permute-start(bf16[64,1024]{1,0:T(8,128)(2,1)S(1)} %get-tuple-element.22.refs_5_), channel_id=1, source_target_pairs={{0,4},{1,5},{2,6},{3,7},{4,0},{5,1},{6,2},{7,3},{8,12},{9,13},{10,... | collective-permute-start | bytes 393224 | tf_op jit(solution)/shard_map/ppermute | solution.py:312
  9.3 0.5 %collective-permute-start.4 = (bf16[64,1024]{1,0:T(8,128)(2,1)S(1)}, bf16[64,1024]{1,0:T(8,128)(2,1)S(1)}, u32[]{:S(2)}, u32[]{:S(2)}) collective-permute-start(bf16[64,1024]{1,0:T(8,128)(2,1)S(1)} %get-tuple-element.22.refs_5_), channel_id=1, source_target_pairs={{0,2},{1,3},{2,0},{3,1},{4,6},{5,7},{6,4},{7,5},{8,10},{9,11},{10,... | collective-permute-start | bytes 393224 | tf_op jit(solution)/shard_map/ppermute | solution.py:312
  9.8 1.1 %pack.1 = bf16[16,16,1024]{2,1,0:T(8,128)(2,1)} custom-call(bf16[64,64]{1,0:T(8,128)(2,1)S(1)} %get-tuple-element.17.order_ref, bf16[64,4096]{1,0:T(8,128)(2,1)S(1)} %get-tuple-element.18.q_ref), custom_call_target="tpu_custom_call" | custom-call | flops 33554432 | bytes 1048576 | tf_op jit(solution)/shard_map/pack/pallas_call | solution.py:330
  10.9 5.3 %all-to-all-start = ((bf16[16,16,1024]{2,1,0:T(8,128)(2,1)}), bf16[16,16,1024]{2,1,0:T(8,128)(2,1)S(1)}, u32[]{:S(2)}, u32[]{:S(2)}) async-start(bf16[16,16,1024]{2,1,0:T(8,128)(2,1)} %pack.1), calls=%async_computation | async-start | bytes 1048576 | tf_op jit(solution)/shard_map/all_to_all | solution.py:344
  16.1 0.0 collective-permute-done.refs_0_
  16.1 1.3 %collective-permute-done.1.refs_1_ = bf16[64,1024]{1,0:T(8,128)(2,1)S(1)} collective-permute-done((bf16[64,1024]{1,0:T(8,128)(2,1)S(1)}, bf16[64,1024]{1,0:T(8,128)(2,1)S(1)}, u32[]{:S(2)}, u32[]{:S(2)}) %collective-permute-start.1) | collective-permute-done | bytes 131104 | tf_op jit(solution)/shard_map/ppermute | solution.py:312
  17.5 0.0 collective-permute-done.2.refs_2_
  17.5 1.0 %collective-permute-done.3.refs_3_ = bf16[64,1024]{1,0:T(8,128)(2,1)S(1)} collective-permute-done((bf16[64,1024]{1,0:T(8,128)(2,1)S(1)}, bf16[64,1024]{1,0:T(8,128)(2,1)S(1)}, u32[]{:S(2)}, u32[]{:S(2)}) %collective-permute-start.3) | collective-permute-done | bytes 131104 | tf_op jit(solution)/shard_map/ppermute | solution.py:312
  18.5 0.0 collective-permute-done.4.refs_4_
  18.5 0.1 heads.1
  18.6 0.0 copy-start
  18.7 0.1 collective-permute-start.5
  18.7 0.0 copy-start.1
  18.7 1.4 %collective-permute-start.6 = (bf16[128,512]{1,0:T(8,128)(2,1)S(1)}, bf16[128,512]{1,0:T(8,128)(2,1)S(1)}, u32[]{:S(2)}, u32[]{:S(2)}) collective-permute-start(bf16[128,512]{1,0:T(8,128)(2,1)S(1)} %get-tuple-element.25), channel_id=1, source_target_pairs={{0,2},{1,3},{2,0},{3,1},{4,6},{5,7},{6,4},{7,5},{8,10},{9,11},{10,... | collective-permute-start | bytes 393224 | tf_op jit(solution)/shard_map/ppermute | solution.py:312
  20.2 0.4 %collective-permute-start.7 = (bf16[128,512]{1,0:T(8,128)(2,1)S(1)}, bf16[128,512]{1,0:T(8,128)(2,1)S(1)}, u32[]{:S(2)}, u32[]{:S(2)}) collective-permute-start(bf16[128,512]{1,0:T(8,128)(2,1)S(1)} %get-tuple-element.26), channel_id=1, source_target_pairs={{0,3},{1,2},{2,1},{3,0},{4,7},{5,6},{6,5},{7,4},{8,11},{9,10},{10,... | collective-permute-start | bytes 393224 | tf_op jit(solution)/shard_map/ppermute | solution.py:312
  20.6 0.0 copy-done
  20.6 0.0 copy-done.1
  20.6 1.6 %place.1 = (s32[128,128]{1,0:T(8,128)S(1)}, s32[128,128]{1,0:T(8,128)S(1)}, bf16[128,128]{1,0:T(8,128)(2,1)S(1)}) custom-call(s32[4]{0:T(128)S(1)} %copy-done.1, s32[8,128]{1,0:T(8,128)S(1)} %bitcast.2), custom_call_target="tpu_custom_call" | custom-call | tf_op jit(solution)/shard_map/place/pallas_call | solution.py:370
  22.2 4.4 %collective-permute-done.6.refs_2_ = bf16[128,512]{1,0:T(8,128)(2,1)S(1)} collective-permute-done((bf16[128,512]{1,0:T(8,128)(2,1)S(1)}, bf16[128,512]{1,0:T(8,128)(2,1)S(1)}, u32[]{:S(2)}, u32[]{:S(2)}) %collective-permute-start.6) | collective-permute-done | bytes 131104 | tf_op jit(solution)/shard_map/ppermute | solution.py:312
  26.6 3.1 %collective-permute-done.7.refs_3_ = bf16[128,512]{1,0:T(8,128)(2,1)S(1)} collective-permute-done((bf16[128,512]{1,0:T(8,128)(2,1)S(1)}, bf16[128,512]{1,0:T(8,128)(2,1)S(1)}, u32[]{:S(2)}, u32[]{:S(2)}) %collective-permute-start.7) | collective-permute-done | bytes 131104 | tf_op jit(solution)/shard_map/ppermute | solution.py:312
  29.7 0.0 collective-permute-done.5.refs_1_
  29.7 0.9 %all-to-all-done.q_ref = bf16[16,16,1024]{2,1,0:T(8,128)(2,1)S(1)} async-done(((bf16[16,16,1024]{2,1,0:T(8,128)(2,1)}), bf16[16,16,1024]{2,1,0:T(8,128)(2,1)S(1)}, u32[]{:S(2)}, u32[]{:S(2)}) %all-to-all-start) | async-done | bytes 524320 | tf_op jit(solution)/shard_map/all_to_all | solution.py:344
  30.6 2.1 %attend.1 = (bf16[64,2048]{1,0:T(8,128)(2,1)S(1)}, bf16[64,2048]{1,0:T(8,128)(2,1)S(1)}) custom-call(bf16[16,16,1024]{2,1,0:T(8,128)(2,1)S(1)} %all-to-all-done.q_ref, s32[128,128]{1,0:T(8,128)S(1)} %get-tuple-element.19.pos_ref, s32[128,128]{1,0:T(8,128)S(1)} %get-tuple-element.20.start_ref, bf16[128,128]{1,0:T(8,128)(2,1)S(1)} %get-tuple-element.21.order_ref, ...), custom_call_target="tpu_custom_call" | custom-call | tf_op jit(solution)/shard_map/attend/pallas_call | solution.py:383
  32.7 0.1 collective-permute-start.8
  32.8 0.7 %write_own.1.refs_0_ = bf16[64,4096]{1,0:T(8,128)(2,1)} custom-call(bf16[64,2048]{1,0:T(8,128)(2,1)S(1)} %get-tuple-element.28.heads_ref), custom_call_target="tpu_custom_call" | custom-call | tf_op jit(solution)/shard_map/write_own/pallas_call | solution.py:398
  33.5 0.8 %collective-permute-done.8.heads_ref = bf16[64,2048]{1,0:T(8,128)(2,1)S(1)} collective-permute-done((bf16[64,2048]{1,0:T(8,128)(2,1)S(1)}, bf16[64,2048]{1,0:T(8,128)(2,1)S(1)}, u32[]{:S(2)}, u32[]{:S(2)}) %collective-permute-start.8) | collective-permute-done | bytes 262176 | tf_op jit(solution)/shard_map/ppermute | solution.py:312
  34.3 0.7 %write_received.1 = bf16[64,4096]{1,0:T(8,128)(2,1)} custom-call(bf16[64,2048]{1,0:T(8,128)(2,1)S(1)} %collective-permute-done.8.heads_ref, bf16[64,4096]{1,0:T(8,128)(2,1)} %write_own.1.refs_0_), custom_call_target="tpu_custom_call", output_to_operand_aliasing={{}: (1, {})} | custom-call | tf_op jit(solution)/shard_map/write_received/pallas_call | solution.py:407
Async XLA Ops:
  1.2 14.9 %collective-permute-start = (bf16[64,1024]{1,0:T(8,128)(2,1)S(1)}, bf16[64,1024]{1,0:T(8,128)(2,1)S(1)}, u32[]{:S(2)}, u32[]{:S(2)}) collective-permute-start(bf16[64,1024]{1,0:T(8,128)(2,1)S(1)} %get-tuple-element.22.refs_5_), channel_id=1, source_target_pairs={{0,12},{1,13},{2,14},{3,15},{4,8},{5,9},{6,10},{7,11},{8,4},{9,5},... | collective-permute-start | bytes 393224 | tf_op jit(solution)/shard_map/ppermute | solution.py:312
  6.3 11.2 %collective-permute-start.1 = (bf16[64,1024]{1,0:T(8,128)(2,1)S(1)}, bf16[64,1024]{1,0:T(8,128)(2,1)S(1)}, u32[]{:S(2)}, u32[]{:S(2)}) collective-permute-start(bf16[64,1024]{1,0:T(8,128)(2,1)S(1)} %get-tuple-element.22.refs_5_), channel_id=1, source_target_pairs={{0,8},{1,9},{2,10},{3,11},{4,12},{5,13},{6,14},{7,15},{8,0},{9,1},... | collective-permute-start | bytes 393224 | tf_op jit(solution)/shard_map/ppermute | solution.py:312
  6.3 11.2 %collective-permute-start.2 = (bf16[64,1024]{1,0:T(8,128)(2,1)S(1)}, bf16[64,1024]{1,0:T(8,128)(2,1)S(1)}, u32[]{:S(2)}, u32[]{:S(2)}) collective-permute-start(bf16[64,1024]{1,0:T(8,128)(2,1)S(1)} %get-tuple-element.22.refs_5_), channel_id=1, source_target_pairs={{0,6},{1,7},{2,4},{3,5},{4,2},{5,3},{6,0},{7,1},{8,14},{9,15},{10,... | collective-permute-start | bytes 393224 | tf_op jit(solution)/shard_map/ppermute | solution.py:312
  8.0 10.5 %collective-permute-start.3 = (bf16[64,1024]{1,0:T(8,128)(2,1)S(1)}, bf16[64,1024]{1,0:T(8,128)(2,1)S(1)}, u32[]{:S(2)}, u32[]{:S(2)}) collective-permute-start(bf16[64,1024]{1,0:T(8,128)(2,1)S(1)} %get-tuple-element.22.refs_5_), channel_id=1, source_target_pairs={{0,4},{1,5},{2,6},{3,7},{4,0},{5,1},{6,2},{7,3},{8,12},{9,13},{10,... | collective-permute-start | bytes 393224 | tf_op jit(solution)/shard_map/ppermute | solution.py:312
  9.3 9.3 %collective-permute-start.4 = (bf16[64,1024]{1,0:T(8,128)(2,1)S(1)}, bf16[64,1024]{1,0:T(8,128)(2,1)S(1)}, u32[]{:S(2)}, u32[]{:S(2)}) collective-permute-start(bf16[64,1024]{1,0:T(8,128)(2,1)S(1)} %get-tuple-element.22.refs_5_), channel_id=1, source_target_pairs={{0,2},{1,3},{2,0},{3,1},{4,6},{5,7},{6,4},{7,5},{8,10},{9,11},{10,... | collective-permute-start | bytes 393224 | tf_op jit(solution)/shard_map/ppermute | solution.py:312
  10.9 19.7 %all-to-all-start = ((bf16[16,16,1024]{2,1,0:T(8,128)(2,1)}), bf16[16,16,1024]{2,1,0:T(8,128)(2,1)S(1)}, u32[]{:S(2)}, u32[]{:S(2)}) async-start(bf16[16,16,1024]{2,1,0:T(8,128)(2,1)} %pack.1), calls=%async_computation | async-start | bytes 1048576 | tf_op jit(solution)/shard_map/all_to_all | solution.py:344
  18.6 2.0 %copy-start = (s32[1024]{0:T(1024)S(1)}, s32[1024]{0:T(1024)}, u32[]{:S(2)}) copy-start(s32[1024]{0:T(1024)} %param.8) | copy-start | bytes 12292
  18.7 11.1 %collective-permute-start.5 = (bf16[384,512]{1,0:T(8,128)(2,1)S(1)}, bf16[384,512]{1,0:T(8,128)(2,1)S(1)}, u32[]{:S(2)}, u32[]{:S(2)}) collective-permute-start(bf16[384,512]{1,0:T(8,128)(2,1)S(1)} %get-tuple-element.24), channel_id=1, source_target_pairs={{0,1},{1,0},{2,3},{3,2},{4,5},{5,4},{6,7},{7,6},{8,9},{9,8},{10,11... | collective-permute-start | bytes 1179656 | tf_op jit(solution)/shard_map/ppermute | solution.py:312
  18.7 1.9 %copy-start.1 = (s32[4]{0:T(128)S(1)}, s32[4]{0:T(128)}, u32[]{:S(2)}) copy-start(s32[4]{0:T(128)} %lengths_ref.1) | copy-start | bytes 52
  18.7 7.9 %collective-permute-start.6 = (bf16[128,512]{1,0:T(8,128)(2,1)S(1)}, bf16[128,512]{1,0:T(8,128)(2,1)S(1)}, u32[]{:S(2)}, u32[]{:S(2)}) collective-permute-start(bf16[128,512]{1,0:T(8,128)(2,1)S(1)} %get-tuple-element.25), channel_id=1, source_target_pairs={{0,2},{1,3},{2,0},{3,1},{4,6},{5,7},{6,4},{7,5},{8,10},{9,11},{10,... | collective-permute-start | bytes 393224 | tf_op jit(solution)/shard_map/ppermute | solution.py:312
  20.2 9.6 %collective-permute-start.7 = (bf16[128,512]{1,0:T(8,128)(2,1)S(1)}, bf16[128,512]{1,0:T(8,128)(2,1)S(1)}, u32[]{:S(2)}, u32[]{:S(2)}) collective-permute-start(bf16[128,512]{1,0:T(8,128)(2,1)S(1)} %get-tuple-element.26), channel_id=1, source_target_pairs={{0,3},{1,2},{2,1},{3,0},{4,7},{5,6},{6,5},{7,4},{8,11},{9,10},{10,... | collective-permute-start | bytes 393224 | tf_op jit(solution)/shard_map/ppermute | solution.py:312
  32.7 1.6 %collective-permute-start.8 = (bf16[64,2048]{1,0:T(8,128)(2,1)S(1)}, bf16[64,2048]{1,0:T(8,128)(2,1)S(1)}, u32[]{:S(2)}, u32[]{:S(2)}) collective-permute-start(bf16[64,2048]{1,0:T(8,128)(2,1)S(1)} %get-tuple-element.27), channel_id=1, source_target_pairs={{0,1},{1,0},{2,3},{3,2},{4,5},{5,4},{6,7},{7,6},{8,9},{9,8},{10,11... | collective-permute-start | bytes 786440 | tf_op jit(solution)/shard_map/ppermute | solution.py:312

commit v8 on v7

--- a/solution.py
+++ b/solution.py
@@ -90,24 +90,24 @@
                         out_ref[dest, Q_ROWS:, col : col + width] = block
 
 
-def block_offsets(nodes):
-    return list(range(nodes - 2 * CORES, 3 * CORES, -2 * CORES)) + [3 * CORES, 2 * CORES, CORES, 0]
+WHOLE = ((12, 8), (6, 4), (2, 0))
+HALVES = ((0, WHOLE[0]), (1, WHOLE[0]), (2, WHOLE[0]), (3, WHOLE[0])) + tuple(
+    (core, pair) for pair in WHOLE[1:] for core in range(CORES)
+)
 
 
 def heads_kernel(*refs):
-    lanes, near, far = refs[: -2 * CORES], refs[-2 * CORES : -CORES], refs[-CORES:]
+    lanes, outs = refs[:-CORES], refs[-CORES:]
     core = lax.axis_index("ctx") % CORES
     rows = lanes[0].shape[0]
     width = HEADS * HD
     for index in range(CORES):
         col = jnp.bitwise_xor(core, index) * width
         for lane, ref in enumerate(lanes):
+            here = slice(lane * rows, (lane + 1) * rows)
             for half in range(2):
-                block = ref[:, pl.ds(pl.multiple_of(col + half * KVH * HD, width), width)]
-                side = slice(half * width, (half + 1) * width)
-                near[index][lane * rows : (lane + 1) * rows, side] = block
-                if lane < len(lanes) - 4:
-                    far[index][lane * rows : (lane + 1) * rows, side] = block
+                side = pl.ds(pl.multiple_of(col + half * KVH * HD, width), width)
+                outs[index][here, half * width : (half + 1) * width] = ref[:, side]
 
 
 def place_kernel(per_chip, lengths_ref, owner_ref, pos_ref, start_ref, order_ref):
@@ -179,36 +179,37 @@
 
 def unpack_pieces(pieces, tokens, k_all, v_all):
     me = lax.axis_index("ctx")
-    offsets = block_offsets(k_all.shape[0] // tokens)
     width = HEADS * HD
-    for index, ref in enumerate(pieces):
-        held = offsets if index < CORES else offsets[:-4]
-        for lane, offset in enumerate(held):
-            node = jnp.bitwise_xor(me, index ^ offset)
+    for ref, (sender, blocks) in zip(pieces, HALVES):
+        for place, offset in enumerate(blocks):
+            node = jnp.bitwise_xor(me, sender ^ offset)
             row = pl.ds(pl.multiple_of(node * tokens, tokens), tokens)
-            here = slice(lane * tokens, (lane + 1) * tokens)
+            here = slice(place * tokens, (place + 1) * tokens)
             k_all[row, :] = ref[here, :width]
             for head in range(HEADS):
                 at = width + head * HD
                 v_all[row, 2 * head * HD : (2 * head + 1) * HD] = ref[here, at : at + HD]
 
 
-def attend_kernel(q_ref, pos_ref, start_ref, order_ref, *refs):
-    kv_refs, refs = refs[: -CORES - 3], refs[-CORES - 3 :]
-    out_refs, (k_all, v_all, context) = refs[:CORES], refs[CORES:]
+def unpack_kernel(tokens, *refs):
+    kv_refs, (k_all, v_all) = refs[:-2], refs[-2:]
+    for head in range(HEADS):
+        ones = jnp.ones((v_all.shape[0], HD), jnp.bfloat16)
+        v_all[:, (2 * head + 1) * HD : (2 * head + 2) * HD] = ones
+    if len(kv_refs) == 1:
+        unpack_moved(kv_refs[0], k_all, v_all)
+    else:
+        unpack_pieces(kv_refs, tokens, k_all, v_all)
+
+
+def attend_kernel(q_ref, pos_ref, start_ref, order_ref, k_all, v_all, *refs):
+    out_refs, context = refs[:CORES], refs[CORES]
     total = k_all.shape[0]
     held = context.shape[0]
     block_rows = 32
     blocks = held // block_rows
     span = total // blocks
     scale = math.log2(math.e) / math.sqrt(HD)
-
-    for head in range(HEADS):
-        v_all[:, (2 * head + 1) * HD : (2 * head + 2) * HD] = jnp.ones((total, HD), jnp.bfloat16)
-    if len(kv_refs) == 1:
-        unpack_moved(kv_refs[0], k_all, v_all)
-    else:
-        unpack_pieces(kv_refs, held // CORES, k_all, v_all)
 
     def rows_of(block):
         return slice(block * block_rows, (block + 1) * block_rows)
@@ -339,27 +340,26 @@
         name="pack",
     )(*operands)
     if apart:
-        lanes = [swap(kv_near, offset) if offset else kv_near for offset in block_offsets(nodes)]
+        lanes = {offset: swap(kv_near, offset) if offset else kv_near for pair in WHOLE for offset in pair}
 
     moved = lax.all_to_all(packed, "ctx", split_axis=0, concat_axis=0, tiled=True)
 
     if apart:
-        near, far = len(lanes) * rows, (len(lanes) - 4) * rows
-        pieces = pl.pallas_call(
-            heads_kernel,
-            out_shape=[
-                jax.ShapeDtypeStruct((count, 2 * HEADS * HD), jnp.bfloat16)
-                for count in (near, near, far, far)
-            ],
-            in_specs=[whole] * len(lanes),
-            out_specs=[whole] * (2 * CORES),
-            compiler_params=VMEM,
-            cost_estimate=pl.CostEstimate(
-                flops=2 * 10**10, bytes_accessed=64 * 2**20, transcendentals=0
-            ),
-            name="heads",
-        )(*lanes)
-        kv_parts = [swap(piece, index) if index else piece for index, piece in enumerate(pieces)]
+        halves = {}
+        for pair, flops in zip(WHOLE, (2 * 10**10, 2 * 10**10, 2 * 10**10)):
+            halves[pair] = pl.pallas_call(
+                heads_kernel,
+                out_shape=[jax.ShapeDtypeStruct((2 * rows, 2 * HEADS * HD), jnp.bfloat16)] * CORES,
+                in_specs=[whole] * 2,
+                out_specs=[whole] * CORES,
+                compiler_params=VMEM,
+                cost_estimate=pl.CostEstimate(flops=flops, bytes_accessed=2**20, transcendentals=0),
+                name="heads",
+            )(*(lanes[offset] for offset in pair))
+        kv_parts = []
+        for sender, pair in HALVES:
+            part = halves[pair][sender % CORES]
+            kv_parts.append(swap(part, sender) if sender else part)
         q_part = moved
     else:
         kv_parts = [moved]
@@ -380,19 +380,26 @@
         name="place",
     )(rollout_lengths, table)
 
+    k_all, v_all = pl.pallas_call(
+        functools.partial(unpack_kernel, rows),
+        out_shape=[
+            jax.ShapeDtypeStruct((total, HEADS * HD), jnp.bfloat16),
+            jax.ShapeDtypeStruct((total, HEADS * 2 * HD), jnp.bfloat16),
+        ],
+        in_specs=[whole] * len(kv_parts),
+        out_specs=[whole] * 2,
+        compiler_params=VMEM,
+        name="unpack",
+    )(*kv_parts)
     own, other = pl.pallas_call(
         attend_kernel,
         out_shape=(jax.ShapeDtypeStruct((rows, HEADS * WIDE), jnp.bfloat16),) * CORES,
-        in_specs=[whole] * (4 + len(kv_parts)),
+        in_specs=[whole] * 6,
         out_specs=(whole,) * CORES,
-        scratch_shapes=[
-            pltpu.VMEM((total, HEADS * HD), jnp.bfloat16),
-            pltpu.VMEM((total, HEADS * 2 * HD), jnp.bfloat16),
-            pltpu.VMEM((held, HEADS * WIDE), jnp.bfloat16),
-        ],
+        scratch_shapes=[pltpu.VMEM((held, HEADS * WIDE), jnp.bfloat16)],
         compiler_params=VMEM,
         name="attend",
-    )(q_part, pos, start, order, *kv_parts)
+    )(q_part, pos, start, order, k_all, v_all)
 
     result = jax.ShapeDtypeStruct((rows, H * HD), jnp.bfloat16)
     half = pl.pallas_call(

time: 35.2 us -> 35.1 us (level)
  waiting for transfers between devices: 11.6 us -> 10.3 us
  starting transfers between devices: 15.9 us -> 16.8 us
    ppermute x9 -> x11, waiting for transfers between devices: 10.7 us -> 9.83 us  [swap(): lax.ppermute(array, 'ctx', [(node, node ^ offset) for node in range(nodes)])]
    ppermute x9 -> x11, starting transfers between devices: 10.6 us -> 11.5 us  [swap(): lax.ppermute(array, 'ctx', [(node, node ^ offset) for node in range(nodes)])]
    all_to_all x1, waiting for transfers between devices: 0.87 us -> 0.51 us  [on_device(): lax.all_to_all(packed, 'ctx', split_axis=0, concat_axis=0, tiled=True)]
  transfers between devices with their start and end apart: 10 -> 12, of which waited for: 6 -> 4; matrix products, arithmetic and copies ran while one was open for 0% -> 0% of each run, Pallas kernels for 10% -> 11%
where the time goes in v8:
time: 35.1 us; the launch traced here: 34.8 us
  starting transfers between devices  16.8 us (48%)
  waiting for transfers between devices  10.3 us (29%)
  Pallas kernels  7.45 us (21%)
    ppermute x11, starting transfers between devices, swap(): lax.ppermute(array, 'ctx', [(node, node ^ offset) for node in range(nodes)])  11.5 us
    ppermute x11, waiting for transfers between devices, swap(): lax.ppermute(array, 'ctx', [(node, node ^ offset) for node in range(nodes)])  9.83 us
    all_to_all x1, starting transfers between devices, on_device(): lax.all_to_all(packed, 'ctx', split_axis=0, concat_axis=0, tiled=True)  5.26 us
    pallas_call x1, Pallas kernels, on_device(): pl.pallas_call(attend_kernel, out_shape=(jax.ShapeDtypeStruct((rows, HEAD...  1.9 us
    pallas_call x1, Pallas kernels, on_device(): pl.pallas_call(functools.partial(place_kernel, per_chip), out_shape=(jax....  1.57 us
    pallas_call x1, Pallas kernels, on_device(): pl.pallas_call(fetch_kernel, out_shape=[jax.ShapeDtypeStruct((rows, rows)...  1.17 us
    pallas_call x1, Pallas kernels, on_device(): pl.pallas_call(functools.partial(pack_kernel, chips), out_shape=message,...  1.07 us
    pallas_call x1, Pallas kernels, on_device(): pl.pallas_call(functools.partial(write_kernel, 0), out_shape=result, in_s...  0.72 us
  transfers between devices with their start and end apart: 12, of which 4 were waited for; matrix products, arithmetic and copies ran while one was open for 0% of the time, Pallas kernels for 11%

profile of v8, /device:TPU:0, one launch (start us, length us, event | category | flops | bytes accessed | tf_op | source)
XLA Modules:
  0.0 34.8 jit_solution(360502362197902206)
XLA Ops:
  0.0 1.2 %fetch.1 = (bf16[64,64]{1,0:T(8,128)(2,1)S(1)}, bf16[64,4096]{1,0:T(8,128)(2,1)S(1)}, bf16[64,1024]{1,0:T(8,128)(2,1)S(1)}) custom-call(s32[8,128]{1,0:T(8,128)} %bitcast.1, bf16[64,4096]{1,0:T(8,128)(2,1)} %q_hbm.1, bf16[64,512]{1,0:T(8,128)(2,1)} %k_hbm.1, bf16[64,512]{1,0:T(8,128)(2,1)} %v_hbm.1), custom_call_target="tpu_custom_call" | custom-call | tf_op jit(solution)/shard_map/fetch/pallas_call | solution.py:317
  1.2 5.1 %collective-permute-start = (bf16[64,1024]{1,0:T(8,128)(2,1)S(1)}, bf16[64,1024]{1,0:T(8,128)(2,1)S(1)}, u32[]{:S(2)}, u32[]{:S(2)}) collective-permute-start(bf16[64,1024]{1,0:T(8,128)(2,1)S(1)} %get-tuple-element.26.refs_1_), channel_id=1, source_target_pairs={{0,12},{1,13},{2,14},{3,15},{4,8},{5,9},{6,10},{7,11},{8,4},{9,5},... | collective-permute-start | bytes 393224 | tf_op jit(solution)/shard_map/ppermute | solution.py:313
  6.3 0.0 collective-permute-start.1
  6.3 1.7 %collective-permute-start.5 = (bf16[64,1024]{1,0:T(8,128)(2,1)S(1)}, bf16[64,1024]{1,0:T(8,128)(2,1)S(1)}, u32[]{:S(2)}, u32[]{:S(2)}) collective-permute-start(bf16[64,1024]{1,0:T(8,128)(2,1)S(1)} %get-tuple-element.26.refs_1_), channel_id=1, source_target_pairs={{0,6},{1,7},{2,4},{3,5},{4,2},{5,3},{6,0},{7,1},{8,14},{9,15},{10,... | collective-permute-start | bytes 393224 | tf_op jit(solution)/shard_map/ppermute | solution.py:313
  8.0 1.2 %collective-permute-start.6 = (bf16[64,1024]{1,0:T(8,128)(2,1)S(1)}, bf16[64,1024]{1,0:T(8,128)(2,1)S(1)}, u32[]{:S(2)}, u32[]{:S(2)}) collective-permute-start(bf16[64,1024]{1,0:T(8,128)(2,1)S(1)} %get-tuple-element.26.refs_1_), channel_id=1, source_target_pairs={{0,4},{1,5},{2,6},{3,7},{4,0},{5,1},{6,2},{7,3},{8,12},{9,13},{10,... | collective-permute-start | bytes 393224 | tf_op jit(solution)/shard_map/ppermute | solution.py:313
  9.3 0.5 %collective-permute-start.8 = (bf16[64,1024]{1,0:T(8,128)(2,1)S(1)}, bf16[64,1024]{1,0:T(8,128)(2,1)S(1)}, u32[]{:S(2)}, u32[]{:S(2)}) collective-permute-start(bf16[64,1024]{1,0:T(8,128)(2,1)S(1)} %get-tuple-element.26.refs_1_), channel_id=1, source_target_pairs={{0,2},{1,3},{2,0},{3,1},{4,6},{5,7},{6,4},{7,5},{8,10},{9,11},{10,... | collective-permute-start | bytes 393224 | tf_op jit(solution)/shard_map/ppermute | solution.py:313
  9.8 1.1 %pack.1 = bf16[16,16,1024]{2,1,0:T(8,128)(2,1)} custom-call(bf16[64,64]{1,0:T(8,128)(2,1)S(1)} %get-tuple-element.21.order_ref, bf16[64,4096]{1,0:T(8,128)(2,1)S(1)} %get-tuple-element.22.q_ref), custom_call_target="tpu_custom_call" | custom-call | flops 33554432 | bytes 1048576 | tf_op jit(solution)/shard_map/pack/pallas_call | solution.py:331
  10.9 5.3 %all-to-all-start = ((bf16[16,16,1024]{2,1,0:T(8,128)(2,1)}), bf16[16,16,1024]{2,1,0:T(8,128)(2,1)S(1)}, u32[]{:S(2)}, u32[]{:S(2)}) async-start(bf16[16,16,1024]{2,1,0:T(8,128)(2,1)} %pack.1), calls=%async_computation | async-start | bytes 1048576 | tf_op jit(solution)/shard_map/all_to_all | solution.py:345
  16.1 0.0 collective-permute-done.refs_0_
  16.1 1.3 %collective-permute-done.1.refs_1_ = bf16[64,1024]{1,0:T(8,128)(2,1)S(1)} collective-permute-done((bf16[64,1024]{1,0:T(8,128)(2,1)S(1)}, bf16[64,1024]{1,0:T(8,128)(2,1)S(1)}, u32[]{:S(2)}, u32[]{:S(2)}) %collective-permute-start.1) | collective-permute-done | bytes 131104 | tf_op jit(solution)/shard_map/ppermute | solution.py:313
  17.5 0.1 collective-permute-start.2
  17.6 1.6 %collective-permute-start.4 = (bf16[128,512]{1,0:T(8,128)(2,1)S(1)}, bf16[128,512]{1,0:T(8,128)(2,1)S(1)}, u32[]{:S(2)}, u32[]{:S(2)}) collective-permute-start(bf16[128,512]{1,0:T(8,128)(2,1)S(1)} %get-tuple-element.28), channel_id=1, source_target_pairs={{0,3},{1,2},{2,1},{3,0},{4,7},{5,6},{6,5},{7,4},{8,11},{9,10},{10,... | collective-permute-start | bytes 393224 | tf_op jit(solution)/shard_map/ppermute | solution.py:313
  19.2 0.0 collective-permute-done.5.refs_0_
  19.2 0.5 %collective-permute-start.3 = (bf16[128,512]{1,0:T(8,128)(2,1)S(1)}, bf16[128,512]{1,0:T(8,128)(2,1)S(1)}, u32[]{:S(2)}, u32[]{:S(2)}) collective-permute-start(bf16[128,512]{1,0:T(8,128)(2,1)S(1)} %get-tuple-element.27.refs_0_), channel_id=1, source_target_pairs={{0,2},{1,3},{2,0},{3,1},{4,6},{5,7},{6,4},{7,5},{8,10},{9,11},{10,... | collective-permute-start | bytes 393224 | tf_op jit(solution)/shard_map/ppermute | solution.py:313
  19.7 0.0 collective-permute-done.6.refs_1_
  19.8 0.1 collective-permute-start.7
  19.9 0.0 collective-permute-done.8.refs_0_
  19.9 0.0 copy-start
  19.9 0.0 copy-start.1
  20.0 0.5 %collective-permute-start.9 = (bf16[128,512]{1,0:T(8,128)(2,1)S(1)}, bf16[128,512]{1,0:T(8,128)(2,1)S(1)}, u32[]{:S(2)}, u32[]{:S(2)}) collective-permute-start(bf16[128,512]{1,0:T(8,128)(2,1)S(1)} %get-tuple-element.32), channel_id=1, source_target_pairs={{0,1},{1,0},{2,3},{3,2},{4,5},{5,4},{6,7},{7,6},{8,9},{9,8},{10,11... | collective-permute-start | bytes 393224 | tf_op jit(solution)/shard_map/ppermute | solution.py:313
  20.5 0.1 copy-done
  20.6 0.0 copy-done.1
  20.6 1.6 %place.1 = (s32[128,128]{1,0:T(8,128)S(1)}, s32[128,128]{1,0:T(8,128)S(1)}, bf16[128,128]{1,0:T(8,128)(2,1)S(1)}) custom-call(s32[4]{0:T(128)S(1)} %copy-done.1, s32[8,128]{1,0:T(8,128)S(1)} %bitcast.2), custom_call_target="tpu_custom_call" | custom-call | tf_op jit(solution)/shard_map/place/pallas_call | solution.py:370
  22.2 0.0 collective-permute-done.2.refs_1_
  22.2 7.7 %collective-permute-done.3.refs_2_ = bf16[128,512]{1,0:T(8,128)(2,1)S(1)} collective-permute-done((bf16[128,512]{1,0:T(8,128)(2,1)S(1)}, bf16[128,512]{1,0:T(8,128)(2,1)S(1)}, u32[]{:S(2)}, u32[]{:S(2)}) %collective-permute-start.3) | collective-permute-done | bytes 131104 | tf_op jit(solution)/shard_map/ppermute | solution.py:313
  29.9 0.0 collective-permute-done.4.refs_3_
  29.9 0.0 collective-permute-done.7.refs_5_
  29.9 0.0 collective-permute-done.9.refs_7_
  29.9 0.2 unpack.1
  30.1 0.5 %all-to-all-done.q_ref = bf16[16,16,1024]{2,1,0:T(8,128)(2,1)S(1)} async-done(((bf16[16,16,1024]{2,1,0:T(8,128)(2,1)}), bf16[16,16,1024]{2,1,0:T(8,128)(2,1)S(1)}, u32[]{:S(2)}, u32[]{:S(2)}) %all-to-all-start) | async-done | bytes 524320 | tf_op jit(solution)/shard_map/all_to_all | solution.py:345
  30.6 1.9 %attend.1 = (bf16[64,2048]{1,0:T(8,128)(2,1)S(1)}, bf16[64,2048]{1,0:T(8,128)(2,1)S(1)}) custom-call(bf16[16,16,1024]{2,1,0:T(8,128)(2,1)S(1)} %all-to-all-done.q_ref, s32[128,128]{1,0:T(8,128)S(1)} %get-tuple-element.23.pos_ref, s32[128,128]{1,0:T(8,128)S(1)} %get-tuple-element.24.start_ref, bf16[128,128]{1,0:T(8,128)(2,1)S(1)} %get-tuple-element.25.order_ref, ...), custom_call_target="tpu_custom_call" | custom-call | tf_op jit(solution)/shard_map/attend/pallas_call | solution.py:394
  32.5 0.1 collective-permute-start.10
  32.6 0.7 %write_own.1.refs_0_ = bf16[64,4096]{1,0:T(8,128)(2,1)} custom-call(bf16[64,2048]{1,0:T(8,128)(2,1)S(1)} %get-tuple-element.36.heads_ref), custom_call_target="tpu_custom_call" | custom-call | tf_op jit(solution)/shard_map/write_own/pallas_call | solution.py:405
  33.3 0.8 %collective-permute-done.10.heads_ref = bf16[64,2048]{1,0:T(8,128)(2,1)S(1)} collective-permute-done((bf16[64,2048]{1,0:T(8,128)(2,1)S(1)}, bf16[64,2048]{1,0:T(8,128)(2,1)S(1)}, u32[]{:S(2)}, u32[]{:S(2)}) %collective-permute-start.10) | collective-permute-done | bytes 262176 | tf_op jit(solution)/shard_map/ppermute | solution.py:313
  34.1 0.7 %write_received.1 = bf16[64,4096]{1,0:T(8,128)(2,1)} custom-call(bf16[64,2048]{1,0:T(8,128)(2,1)S(1)} %collective-permute-done.10.heads_ref, bf16[64,4096]{1,0:T(8,128)(2,1)} %write_own.1.refs_0_), custom_call_target="tpu_custom_call", output_to_operand_aliasing={{}: (1, {})} | custom-call | tf_op jit(solution)/shard_map/write_received/pallas_call | solution.py:414
  (3 shorter events, 0.1 us)
Async XLA Ops:
  1.2 14.9 %collective-permute-start = (bf16[64,1024]{1,0:T(8,128)(2,1)S(1)}, bf16[64,1024]{1,0:T(8,128)(2,1)S(1)}, u32[]{:S(2)}, u32[]{:S(2)}) collective-permute-start(bf16[64,1024]{1,0:T(8,128)(2,1)S(1)} %get-tuple-element.26.refs_1_), channel_id=1, source_target_pairs={{0,12},{1,13},{2,14},{3,15},{4,8},{5,9},{6,10},{7,11},{8,4},{9,5},... | collective-permute-start | bytes 393224 | tf_op jit(solution)/shard_map/ppermute | solution.py:313
  6.3 11.2 %collective-permute-start.1 = (bf16[64,1024]{1,0:T(8,128)(2,1)S(1)}, bf16[64,1024]{1,0:T(8,128)(2,1)S(1)}, u32[]{:S(2)}, u32[]{:S(2)}) collective-permute-start(bf16[64,1024]{1,0:T(8,128)(2,1)S(1)} %get-tuple-element.26.refs_1_), channel_id=1, source_target_pairs={{0,8},{1,9},{2,10},{3,11},{4,12},{5,13},{6,14},{7,15},{8,0},{9,1},... | collective-permute-start | bytes 393224 | tf_op jit(solution)/shard_map/ppermute | solution.py:313
  6.3 12.9 %collective-permute-start.5 = (bf16[64,1024]{1,0:T(8,128)(2,1)S(1)}, bf16[64,1024]{1,0:T(8,128)(2,1)S(1)}, u32[]{:S(2)}, u32[]{:S(2)}) collective-permute-start(bf16[64,1024]{1,0:T(8,128)(2,1)S(1)} %get-tuple-element.26.refs_1_), channel_id=1, source_target_pairs={{0,6},{1,7},{2,4},{3,5},{4,2},{5,3},{6,0},{7,1},{8,14},{9,15},{10,... | collective-permute-start | bytes 393224 | tf_op jit(solution)/shard_map/ppermute | solution.py:313
  8.0 11.7 %collective-permute-start.6 = (bf16[64,1024]{1,0:T(8,128)(2,1)S(1)}, bf16[64,1024]{1,0:T(8,128)(2,1)S(1)}, u32[]{:S(2)}, u32[]{:S(2)}) collective-permute-start(bf16[64,1024]{1,0:T(8,128)(2,1)S(1)} %get-tuple-element.26.refs_1_), channel_id=1, source_target_pairs={{0,4},{1,5},{2,6},{3,7},{4,0},{5,1},{6,2},{7,3},{8,12},{9,13},{10,... | collective-permute-start | bytes 393224 | tf_op jit(solution)/shard_map/ppermute | solution.py:313
  9.3 10.6 %collective-permute-start.8 = (bf16[64,1024]{1,0:T(8,128)(2,1)S(1)}, bf16[64,1024]{1,0:T(8,128)(2,1)S(1)}, u32[]{:S(2)}, u32[]{:S(2)}) collective-permute-start(bf16[64,1024]{1,0:T(8,128)(2,1)S(1)} %get-tuple-element.26.refs_1_), channel_id=1, source_target_pairs={{0,2},{1,3},{2,0},{3,1},{4,6},{5,7},{6,4},{7,5},{8,10},{9,11},{10,... | collective-permute-start | bytes 393224 | tf_op jit(solution)/shard_map/ppermute | solution.py:313
  10.9 19.7 %all-to-all-start = ((bf16[16,16,1024]{2,1,0:T(8,128)(2,1)}), bf16[16,16,1024]{2,1,0:T(8,128)(2,1)S(1)}, u32[]{:S(2)}, u32[]{:S(2)}) async-start(bf16[16,16,1024]{2,1,0:T(8,128)(2,1)} %pack.1), calls=%async_computation | async-start | bytes 1048576 | tf_op jit(solution)/shard_map/all_to_all | solution.py:345
  17.5 4.7 %collective-permute-start.2 = (bf16[128,512]{1,0:T(8,128)(2,1)S(1)}, bf16[128,512]{1,0:T(8,128)(2,1)S(1)}, u32[]{:S(2)}, u32[]{:S(2)}) collective-permute-start(bf16[128,512]{1,0:T(8,128)(2,1)S(1)} %get-tuple-element.28), channel_id=1, source_target_pairs={{0,1},{1,0},{2,3},{3,2},{4,5},{5,4},{6,7},{7,6},{8,9},{9,8},{10,11... | collective-permute-start | bytes 393224 | tf_op jit(solution)/shard_map/ppermute | solution.py:313
  17.6 12.3 %collective-permute-start.4 = (bf16[128,512]{1,0:T(8,128)(2,1)S(1)}, bf16[128,512]{1,0:T(8,128)(2,1)S(1)}, u32[]{:S(2)}, u32[]{:S(2)}) collective-permute-start(bf16[128,512]{1,0:T(8,128)(2,1)S(1)} %get-tuple-element.28), channel_id=1, source_target_pairs={{0,3},{1,2},{2,1},{3,0},{4,7},{5,6},{6,5},{7,4},{8,11},{9,10},{10,... | collective-permute-start | bytes 393224 | tf_op jit(solution)/shard_map/ppermute | solution.py:313
  19.2 10.6 %collective-permute-start.3 = (bf16[128,512]{1,0:T(8,128)(2,1)S(1)}, bf16[128,512]{1,0:T(8,128)(2,1)S(1)}, u32[]{:S(2)}, u32[]{:S(2)}) collective-permute-start(bf16[128,512]{1,0:T(8,128)(2,1)S(1)} %get-tuple-element.27.refs_0_), channel_id=1, source_target_pairs={{0,2},{1,3},{2,0},{3,1},{4,6},{5,7},{6,4},{7,5},{8,10},{9,11},{10,... | collective-permute-start | bytes 393224 | tf_op jit(solution)/shard_map/ppermute | solution.py:313
  19.8 10.1 %collective-permute-start.7 = (bf16[128,512]{1,0:T(8,128)(2,1)S(1)}, bf16[128,512]{1,0:T(8,128)(2,1)S(1)}, u32[]{:S(2)}, u32[]{:S(2)}) collective-permute-start(bf16[128,512]{1,0:T(8,128)(2,1)S(1)} %get-tuple-element.30), channel_id=1, source_target_pairs={{0,1},{1,0},{2,3},{3,2},{4,5},{5,4},{6,7},{7,6},{8,9},{9,8},{10,11... | collective-permute-start | bytes 393224 | tf_op jit(solution)/shard_map/ppermute | solution.py:313
  19.9 0.7 %copy-start = (s32[1024]{0:T(1024)S(1)}, s32[1024]{0:T(1024)}, u32[]{:S(2)}) copy-start(s32[1024]{0:T(1024)} %param.8) | copy-start | bytes 12292
  19.9 0.7 %copy-start.1 = (s32[4]{0:T(128)S(1)}, s32[4]{0:T(128)}, u32[]{:S(2)}) copy-start(s32[4]{0:T(128)} %lengths_ref.1) | copy-start | bytes 52
  20.0 9.9 %collective-permute-start.9 = (bf16[128,512]{1,0:T(8,128)(2,1)S(1)}, bf16[128,512]{1,0:T(8,128)(2,1)S(1)}, u32[]{:S(2)}, u32[]{:S(2)}) collective-permute-start(bf16[128,512]{1,0:T(8,128)(2,1)S(1)} %get-tuple-element.32), channel_id=1, source_target_pairs={{0,1},{1,0},{2,3},{3,2},{4,5},{5,4},{6,7},{7,6},{8,9},{9,8},{10,11... | collective-permute-start | bytes 393224 | tf_op jit(solution)/shard_map/ppermute | solution.py:313
  32.5 1.6 %collective-permute-start.10 = (bf16[64,2048]{1,0:T(8,128)(2,1)S(1)}, bf16[64,2048]{1,0:T(8,128)(2,1)S(1)}, u32[]{:S(2)}, u32[]{:S(2)}) collective-permute-start(bf16[64,2048]{1,0:T(8,128)(2,1)S(1)} %get-tuple-element.35), channel_id=1, source_target_pairs={{0,1},{1,0},{2,3},{3,2},{4,5},{5,4},{6,7},{7,6},{8,9},{9,8},{10,11... | collective-permute-start | bytes 786440 | tf_op jit(solution)/shard_map/ppermute | solution.py:313

commit v9 on v8

--- a/solution.py
+++ b/solution.py
@@ -90,21 +90,28 @@
                         out_ref[dest, Q_ROWS:, col : col + width] = block
 
 
-WHOLE = ((12, 8), (6, 4), (2, 0))
-HALVES = ((0, WHOLE[0]), (1, WHOLE[0]), (2, WHOLE[0]), (3, WHOLE[0])) + tuple(
-    (core, pair) for pair in WHOLE[1:] for core in range(CORES)
-)
+FAR = (12, 8)
+DIAGONAL = 6
+ALONG, ACROSS = 4, 2
+
+
+def pair_kernel(mine_ref, other_ref, out_ref):
+    rows = mine_ref.shape[0]
+    core = lax.axis_index("ctx") % CORES
+    out_ref[pl.ds(pl.multiple_of(core * rows, rows), rows), :] = mine_ref[...]
+    out_ref[pl.ds(pl.multiple_of((1 - core) * rows, rows), rows), :] = other_ref[...]
 
 
 def heads_kernel(*refs):
-    lanes, outs = refs[:-CORES], refs[-CORES:]
+    outs = refs[-CORES:]
     core = lax.axis_index("ctx") % CORES
-    rows = lanes[0].shape[0]
     width = HEADS * HD
     for index in range(CORES):
         col = jnp.bitwise_xor(core, index) * width
-        for lane, ref in enumerate(lanes):
-            here = slice(lane * rows, (lane + 1) * rows)
+        first = 0
+        for ref in refs[:-CORES]:
+            here = slice(first, first + ref.shape[0])
+            first = here.stop
             for half in range(2):
                 side = pl.ds(pl.multiple_of(col + half * KVH * HD, width), width)
                 outs[index][here, half * width : (half + 1) * width] = ref[:, side]
@@ -180,9 +187,18 @@
 def unpack_pieces(pieces, tokens, k_all, v_all):
     me = lax.axis_index("ctx")
     width = HEADS * HD
-    for ref, (sender, blocks) in zip(pieces, HALVES):
-        for place, offset in enumerate(blocks):
-            node = jnp.bitwise_xor(me, sender ^ offset)
+
+    def chip_of(sender):
+        offset = jnp.where(sender % CORES == 0, ALONG, ACROSS)
+        chip = jnp.bitwise_xor(sender, offset) // CORES
+        return [chip * CORES + core for core in range(CORES)]
+
+    senders = [jnp.bitwise_xor(me, index) for index in range(2 * CORES)]
+    nodes = [[jnp.bitwise_xor(sender, offset) for offset in FAR] for sender in senders]
+    nodes += [[jnp.bitwise_xor(sender, DIAGONAL)] + chip_of(sender) for sender in senders[:CORES]]
+    nodes.append([me // CORES * CORES + core for core in range(CORES)])
+    for ref, held in zip(pieces, nodes):
+        for place, node in enumerate(held):
             row = pl.ds(pl.multiple_of(node * tokens, tokens), tokens)
             here = slice(place * tokens, (place + 1) * tokens)
             k_all[row, :] = ref[here, :width]
@@ -309,8 +325,9 @@
     hbm = pl.BlockSpec(memory_space=pltpu.HBM)
     apart = nodes == 16
 
-    def swap(array, offset):
-        return lax.ppermute(array, "ctx", [(node, node ^ offset) for node in range(nodes)])
+    def swap(array, *offsets):
+        pairs = [(node, node ^ offsets[node % len(offsets)]) for node in range(nodes)]
+        return lax.ppermute(array, "ctx", pairs)
 
     kv_rows = 0 if apart else rows // 2
     message = jax.ShapeDtypeStruct((nodes, Q_ROWS + kv_rows, WIDE), jnp.bfloat16)
@@ -327,6 +344,21 @@
         compiler_params=VMEM,
         name="fetch",
     )(*(pltpu.with_memory_space_constraint(x, pltpu.HBM) for x in (table, queries, keys, values)))
+    if apart:
+        other = swap(kv_near, 1)
+        far = [swap(kv_near, offset) for offset in FAR]
+        diagonal = swap(kv_near, DIAGONAL)
+        chip = pl.pallas_call(
+            pair_kernel,
+            out_shape=jax.ShapeDtypeStruct((CORES * rows, 2 * KVH * HD), jnp.bfloat16),
+            in_specs=[whole] * 2,
+            out_specs=whole,
+            compiler_params=VMEM,
+            name="pair",
+        )(kv_near, other)
+        next_chip = swap(chip, ALONG, ACROSS)
+        q_near, _ = lax.optimization_barrier((q_near, chip))
+
     operands = (order_in, q_near) if apart else (order_in, q_near, kv_near)
     packed = pl.pallas_call(
         functools.partial(pack_kernel, chips),
@@ -339,33 +371,7 @@
         ),
         name="pack",
     )(*operands)
-    if apart:
-        lanes = {offset: swap(kv_near, offset) if offset else kv_near for pair in WHOLE for offset in pair}
-
     moved = lax.all_to_all(packed, "ctx", split_axis=0, concat_axis=0, tiled=True)
-
-    if apart:
-        halves = {}
-        for pair, flops in zip(WHOLE, (2 * 10**10, 2 * 10**10, 2 * 10**10)):
-            halves[pair] = pl.pallas_call(
-                heads_kernel,
-                out_shape=[jax.ShapeDtypeStruct((2 * rows, 2 * HEADS * HD), jnp.bfloat16)] * CORES,
-                in_specs=[whole] * 2,
-                out_specs=[whole] * CORES,
-                compiler_params=VMEM,
-                cost_estimate=pl.CostEstimate(flops=flops, bytes_accessed=2**20, transcendentals=0),
-                name="heads",
-            )(*(lanes[offset] for offset in pair))
-        kv_parts = []
-        for sender, pair in HALVES:
-            part = halves[pair][sender % CORES]
-            kv_parts.append(swap(part, sender) if sender else part)
-        q_part = moved
-    else:
-        kv_parts = [moved]
-        groups = held // SUB
-        q_part = moved[:, :Q_ROWS].reshape(groups, nodes // groups, HEADS, SUB, WIDE)[:, :, :, :per_chip]
-        q_part = q_part.transpose(0, 2, 1, 3, 4).reshape(groups, Q_ROWS, WIDE)
 
     pos, start, order = pl.pallas_call(
         functools.partial(place_kernel, per_chip),
@@ -379,6 +385,36 @@
         compiler_params=VMEM,
         name="place",
     )(rollout_lengths, table)
+
+    if apart:
+
+        def heads_of(flops, *blocks):
+            count = sum(block.shape[0] for block in blocks)
+            return pl.pallas_call(
+                heads_kernel,
+                out_shape=[jax.ShapeDtypeStruct((count, 2 * HEADS * HD), jnp.bfloat16)] * CORES,
+                in_specs=[whole] * len(blocks),
+                out_specs=[whole] * CORES,
+                compiler_params=VMEM,
+                cost_estimate=pl.CostEstimate(flops=flops, bytes_accessed=2**20, transcendentals=0),
+                name="heads",
+            )(*blocks)
+
+        mine_far, other_far = heads_of(2 * 10**10, *far)
+        from_core, from_y, from_both = swap(other_far, 1), swap(mine_far, 2), swap(other_far, 3)
+        mine_chip, _ = heads_of(10**6, chip)
+        diagonal, next_chip, *_ = lax.optimization_barrier(
+            (diagonal, next_chip, from_core, from_y, from_both, mine_chip, order)
+        )
+        mine_near, other_near = heads_of(10**6, diagonal, next_chip)
+        kv_parts = [mine_far, from_core, from_y, from_both]
+        kv_parts += [mine_near, swap(other_near, 1), mine_chip]
+        q_part = moved
+    else:
+        kv_parts = [moved]
+        groups = held // SUB
+        q_part = moved[:, :Q_ROWS].reshape(groups, nodes // groups, HEADS, SUB, WIDE)[:, :, :, :per_chip]
+        q_part = q_part.transpose(0, 2, 1, 3, 4).reshape(groups, Q_ROWS, WIDE)
 
     k_all, v_all = pl.pallas_call(
         functools.partial(unpack_kernel, rows),

time: 35.1 us -> 34.5 us (0.983)
  Pallas kernels: 7.45 us -> 8.15 us
  starting transfers between devices: 16.8 us -> 16.2 us
  waiting for transfers between devices: 10.3 us -> 9.74 us
    all_to_all x1, starting transfers between devices: 5.26 us -> 3.86 us  [on_device(): lax.all_to_all(packed, 'ctx', split_axis=0, concat_axis=0, tiled=True)]
    ppermute x11 -> x10, starting transfers between devices: 11.5 us -> 12.4 us  [swap(): return lax.ppermute(array, 'ctx', pairs)]
    pallas_call x3 -> x4, Pallas kernels: 0.12 us -> 0.81 us  [the longest x3 0.78 us: heads_of(): pl.pallas_call(heads_kernel, out_shape=[jax.ShapeDtypeStruct((count, 2 *...]
    all_to_all x1, waiting for transfers between devices: 0.51 us -> 0.01 us  [on_device(): lax.all_to_all(packed, 'ctx', split_axis=0, concat_axis=0, tiled=True)]
    ppermute x11 -> x10, waiting for transfers between devices: 9.83 us -> 9.74 us  [swap(): return lax.ppermute(array, 'ctx', pairs)]
  transfers between devices with their start and end apart: 12 -> 11, of which waited for: 4 -> 5; matrix products, arithmetic and copies ran while one was open for 0% -> 0% of each run, Pallas kernels for 11% -> 13%
where the time goes in v9:
time: 34.5 us; the launch traced here: 34.2 us
  starting transfers between devices  16.2 us (47%)
  waiting for transfers between devices  9.74 us (28%)
  Pallas kernels  8.15 us (24%)
    ppermute x10, starting transfers between devices, swap(): return lax.ppermute(array, 'ctx', pairs)  12.4 us
    ppermute x10, waiting for transfers between devices, swap(): return lax.ppermute(array, 'ctx', pairs)  9.74 us
    all_to_all x1, starting transfers between devices, on_device(): lax.all_to_all(packed, 'ctx', split_axis=0, concat_axis=0, tiled=True)  3.86 us
    pallas_call x1, Pallas kernels, on_device(): pl.pallas_call(attend_kernel, out_shape=(jax.ShapeDtypeStruct((rows, HEAD...  1.91 us
    pallas_call x1, Pallas kernels, on_device(): pl.pallas_call(functools.partial(place_kernel, per_chip), out_shape=(jax....  1.57 us
    pallas_call x1, Pallas kernels, on_device(): pl.pallas_call(fetch_kernel, out_shape=[jax.ShapeDtypeStruct((rows, rows)...  1.17 us
    pallas_call x1, Pallas kernels, on_device(): pl.pallas_call(functools.partial(pack_kernel, chips), out_shape=message,...  1.07 us
    pallas_call x3, Pallas kernels, heads_of(): pl.pallas_call(heads_kernel, out_shape=[jax.ShapeDtypeStruct((count, 2 *...  0.78 us
  transfers between devices with their start and end apart: 11, of which 5 were waited for; matrix products, arithmetic and copies ran while one was open for 0% of the time, Pallas kernels for 13%

profile of v9, /device:TPU:0, one launch (start us, length us, event | category | flops | bytes accessed | tf_op | source)
XLA Modules:
  0.0 34.2 jit_solution(12280605680679188592)
XLA Ops:
  0.0 1.2 %fetch.1 = (bf16[64,64]{1,0:T(8,128)(2,1)S(1)}, bf16[64,4096]{1,0:T(8,128)(2,1)S(1)}, bf16[64,1024]{1,0:T(8,128)(2,1)S(1)}) custom-call(s32[8,128]{1,0:T(8,128)} %bitcast.1, bf16[64,4096]{1,0:T(8,128)(2,1)} %q_hbm.1, bf16[64,512]{1,0:T(8,128)(2,1)} %k_hbm.1, bf16[64,512]{1,0:T(8,128)(2,1)} %v_hbm.1), custom_call_target="tpu_custom_call" | custom-call | tf_op jit(solution)/shard_map/fetch/pallas_call | solution.py:334
  1.2 0.5 %collective-permute-start = (bf16[64,1024]{1,0:T(8,128)(2,1)S(1)}, bf16[64,1024]{1,0:T(8,128)(2,1)S(1)}, u32[]{:S(2)}, u32[]{:S(2)}) collective-permute-start(bf16[64,1024]{1,0:T(8,128)(2,1)S(1)} %get-tuple-element.25.mine_ref), channel_id=1, source_target_pairs={{0,1},{1,0},{2,3},{3,2},{4,5},{5,4},{6,7},{7,6},{8,9},{9,8},{10,11... | collective-permute-start | bytes 393224 | tf_op jit(solution)/shard_map/ppermute | solution.py:330
  1.7 3.7 %collective-permute-start.2 = (bf16[64,1024]{1,0:T(8,128)(2,1)S(1)}, bf16[64,1024]{1,0:T(8,128)(2,1)S(1)}, u32[]{:S(2)}, u32[]{:S(2)}) collective-permute-start(bf16[64,1024]{1,0:T(8,128)(2,1)S(1)} %get-tuple-element.25.mine_ref), channel_id=1, source_target_pairs={{0,8},{1,9},{2,10},{3,11},{4,12},{5,13},{6,14},{7,15},{8,0},{9,1},... | collective-permute-start | bytes 393224 | tf_op jit(solution)/shard_map/ppermute | solution.py:330
  5.4 1.3 %collective-permute-start.1 = (bf16[64,1024]{1,0:T(8,128)(2,1)S(1)}, bf16[64,1024]{1,0:T(8,128)(2,1)S(1)}, u32[]{:S(2)}, u32[]{:S(2)}) collective-permute-start(bf16[64,1024]{1,0:T(8,128)(2,1)S(1)} %get-tuple-element.25.mine_ref), channel_id=1, source_target_pairs={{0,12},{1,13},{2,14},{3,15},{4,8},{5,9},{6,10},{7,11},{8,4},{9,5},... | collective-permute-start | bytes 393224 | tf_op jit(solution)/shard_map/ppermute | solution.py:330
  6.7 1.2 %collective-permute-start.6 = (bf16[64,1024]{1,0:T(8,128)(2,1)S(1)}, bf16[64,1024]{1,0:T(8,128)(2,1)S(1)}, u32[]{:S(2)}, u32[]{:S(2)}) collective-permute-start(bf16[64,1024]{1,0:T(8,128)(2,1)S(1)} %get-tuple-element.25.mine_ref), channel_id=1, source_target_pairs={{0,6},{1,7},{2,4},{3,5},{4,2},{5,3},{6,0},{7,1},{8,14},{9,15},{10,... | collective-permute-start | bytes 393224 | tf_op jit(solution)/shard_map/ppermute | solution.py:330
  7.9 0.0 collective-permute-done.other_ref
  7.9 1.9 %collective-permute-start.7 = (bf16[128,1024]{1,0:T(8,128)(2,1)S(1)}, bf16[128,1024]{1,0:T(8,128)(2,1)S(1)}, u32[]{:S(2)}, u32[]{:S(2)}) collective-permute-start(bf16[128,1024]{1,0:T(8,128)(2,1)S(1)} %pair.1.refs_0_), channel_id=1, source_target_pairs={{0,4},{1,3},{2,6},{3,1},{4,0},{5,7},{6,2},{7,5},{8,12},{9,11},{10,... | collective-permute-start | bytes 786440 | tf_op jit(solution)/shard_map/ppermute | solution.py:330
  9.8 1.1 %pack.1 = bf16[16,16,1024]{2,1,0:T(8,128)(2,1)} custom-call(bf16[64,64]{1,0:T(8,128)(2,1)S(1)} %get-tuple-element.23.order_ref, bf16[64,4096]{1,0:T(8,128)(2,1)S(1)} %get-tuple-element.26.q_ref), custom_call_target="tpu_custom_call" | custom-call | flops 33554432 | bytes 1048576 | tf_op jit(solution)/shard_map/pack/pallas_call | solution.py:363
  10.9 3.9 %all-to-all-start = ((bf16[16,16,1024]{2,1,0:T(8,128)(2,1)}), bf16[16,16,1024]{2,1,0:T(8,128)(2,1)S(1)}, u32[]{:S(2)}, u32[]{:S(2)}) async-start(bf16[16,16,1024]{2,1,0:T(8,128)(2,1)} %pack.1), calls=%async_computation | async-start | bytes 1048576 | tf_op jit(solution)/shard_map/all_to_all | solution.py:374
  14.7 0.6 %collective-permute-done.2.refs_1_ = bf16[64,1024]{1,0:T(8,128)(2,1)S(1)} collective-permute-done((bf16[64,1024]{1,0:T(8,128)(2,1)S(1)}, bf16[64,1024]{1,0:T(8,128)(2,1)S(1)}, u32[]{:S(2)}, u32[]{:S(2)}) %collective-permute-start.2) | collective-permute-done | bytes 131104 | tf_op jit(solution)/shard_map/ppermute | solution.py:330
  15.4 0.0 collective-permute-done.1.refs_0_
  15.4 0.0 copy-start
  15.4 0.0 copy-start.1
  15.4 1.8 %collective-permute-start.4 = (bf16[128,512]{1,0:T(8,128)(2,1)S(1)}, bf16[128,512]{1,0:T(8,128)(2,1)S(1)}, u32[]{:S(2)}, u32[]{:S(2)}) collective-permute-start(bf16[128,512]{1,0:T(8,128)(2,1)S(1)} %get-tuple-element.30.refs_0_), channel_id=1, source_target_pairs={{0,2},{1,3},{2,0},{3,1},{4,6},{5,7},{6,4},{7,5},{8,10},{9,11},{10,... | collective-permute-start | bytes 393224 | tf_op jit(solution)/shard_map/ppermute | solution.py:330
  17.3 0.0 collective-permute-start.5
  17.3 0.4 %collective-permute-start.3 = (bf16[128,512]{1,0:T(8,128)(2,1)S(1)}, bf16[128,512]{1,0:T(8,128)(2,1)S(1)}, u32[]{:S(2)}, u32[]{:S(2)}) collective-permute-start(bf16[128,512]{1,0:T(8,128)(2,1)S(1)} %get-tuple-element.31), channel_id=1, source_target_pairs={{0,1},{1,0},{2,3},{3,2},{4,5},{5,4},{6,7},{7,6},{8,9},{9,8},{10,11... | collective-permute-start | bytes 393224 | tf_op jit(solution)/shard_map/ppermute | solution.py:330
  17.6 0.0 copy-done
  17.6 0.0 copy-done.1
  17.6 1.6 %place.1 = (s32[128,128]{1,0:T(8,128)S(1)}, s32[128,128]{1,0:T(8,128)S(1)}, bf16[128,128]{1,0:T(8,128)(2,1)S(1)}) custom-call(s32[4]{0:T(128)S(1)} %copy-done.1, s32[8,128]{1,0:T(8,128)S(1)} %bitcast.2), custom_call_target="tpu_custom_call" | custom-call | tf_op jit(solution)/shard_map/place/pallas_call | solution.py:376
  19.2 0.7 %heads.4 = (bf16[128,512]{1,0:T(8,128)(2,1)S(1)}, bf16[128,512]{1,0:T(8,128)(2,1)}) custom-call(bf16[128,1024]{1,0:T(8,128)(2,1)S(1)} %pair.1.refs_0_), custom_call_target="tpu_custom_call" | custom-call | flops 1000000 | bytes 1048576 | tf_op jit(solution)/shard_map/heads/pallas_call | solution.py:393
  19.9 0.0 collective-permute-done.6.refs_0_
  19.9 4.7 %collective-permute-done.4.refs_2_ = bf16[128,512]{1,0:T(8,128)(2,1)S(1)} collective-permute-done((bf16[128,512]{1,0:T(8,128)(2,1)S(1)}, bf16[128,512]{1,0:T(8,128)(2,1)S(1)}, u32[]{:S(2)}, u32[]{:S(2)}) %collective-permute-start.4) | collective-permute-done | bytes 131104 | tf_op jit(solution)/shard_map/ppermute | solution.py:330
  24.7 2.8 %collective-permute-done.5.refs_3_ = bf16[128,512]{1,0:T(8,128)(2,1)S(1)} collective-permute-done((bf16[128,512]{1,0:T(8,128)(2,1)S(1)}, bf16[128,512]{1,0:T(8,128)(2,1)S(1)}, u32[]{:S(2)}, u32[]{:S(2)}) %collective-permute-start.5) | collective-permute-done | bytes 131104 | tf_op jit(solution)/shard_map/ppermute | solution.py:330
  27.5 0.0 collective-permute-done.3.refs_1_
  27.5 0.0 collective-permute-done.7.refs_1_
  27.5 0.1 heads.5
  27.6 1.2 %collective-permute-start.8 = (bf16[192,512]{1,0:T(8,128)(2,1)S(1)}, bf16[192,512]{1,0:T(8,128)(2,1)S(1)}, u32[]{:S(2)}, u32[]{:S(2)}) collective-permute-start(bf16[192,512]{1,0:T(8,128)(2,1)S(1)} %get-tuple-element.36), channel_id=1, source_target_pairs={{0,1},{1,0},{2,3},{3,2},{4,5},{5,4},{6,7},{7,6},{8,9},{9,8},{10,11... | collective-permute-start | bytes 589832 | tf_op jit(solution)/shard_map/ppermute | solution.py:330
  28.7 1.1 %collective-permute-done.8.refs_5_ = bf16[192,512]{1,0:T(8,128)(2,1)S(1)} collective-permute-done((bf16[192,512]{1,0:T(8,128)(2,1)S(1)}, bf16[192,512]{1,0:T(8,128)(2,1)S(1)}, u32[]{:S(2)}, u32[]{:S(2)}) %collective-permute-start.8) | collective-permute-done | bytes 196640 | tf_op jit(solution)/shard_map/ppermute | solution.py:330
  29.8 0.2 unpack.1
  30.0 0.0 all-to-all-done.q_ref
  30.0 1.9 %attend.1 = (bf16[64,2048]{1,0:T(8,128)(2,1)S(1)}, bf16[64,2048]{1,0:T(8,128)(2,1)S(1)}) custom-call(bf16[16,16,1024]{2,1,0:T(8,128)(2,1)S(1)} %all-to-all-done.q_ref, s32[128,128]{1,0:T(8,128)S(1)} %get-tuple-element.27.pos_ref, s32[128,128]{1,0:T(8,128)S(1)} %get-tuple-element.28.start_ref, bf16[128,128]{1,0:T(8,128)(2,1)S(1)} %get-tuple-element.29.order_ref, ...), custom_call_target="tpu_custom_call" | custom-call | tf_op jit(solution)/shard_map/attend/pallas_call | solution.py:430
  31.9 0.4 %collective-permute-start.9 = (bf16[64,2048]{1,0:T(8,128)(2,1)S(1)}, bf16[64,2048]{1,0:T(8,128)(2,1)S(1)}, u32[]{:S(2)}, u32[]{:S(2)}) collective-permute-start(bf16[64,2048]{1,0:T(8,128)(2,1)S(1)} %get-tuple-element.39), channel_id=1, source_target_pairs={{0,1},{1,0},{2,3},{3,2},{4,5},{5,4},{6,7},{7,6},{8,9},{9,8},{10,11... | collective-permute-start | bytes 786440 | tf_op jit(solution)/shard_map/ppermute | solution.py:330
  32.4 0.7 %write_own.1.refs_0_ = bf16[64,4096]{1,0:T(8,128)(2,1)} custom-call(bf16[64,2048]{1,0:T(8,128)(2,1)S(1)} %get-tuple-element.40.heads_ref), custom_call_target="tpu_custom_call" | custom-call | tf_op jit(solution)/shard_map/write_own/pallas_call | solution.py:441
  33.1 0.4 %collective-permute-done.9.heads_ref = bf16[64,2048]{1,0:T(8,128)(2,1)S(1)} collective-permute-done((bf16[64,2048]{1,0:T(8,128)(2,1)S(1)}, bf16[64,2048]{1,0:T(8,128)(2,1)S(1)}, u32[]{:S(2)}, u32[]{:S(2)}) %collective-permute-start.9) | collective-permute-done | bytes 262176 | tf_op jit(solution)/shard_map/ppermute | solution.py:330
  33.5 0.7 %write_received.1 = bf16[64,4096]{1,0:T(8,128)(2,1)} custom-call(bf16[64,2048]{1,0:T(8,128)(2,1)S(1)} %collective-permute-done.9.heads_ref, bf16[64,4096]{1,0:T(8,128)(2,1)} %write_own.1.refs_0_), custom_call_target="tpu_custom_call", output_to_operand_aliasing={{}: (1, {})} | custom-call | tf_op jit(solution)/shard_map/write_received/pallas_call | solution.py:450
  (2 shorter events, 0.1 us)
Async XLA Ops:
  1.2 6.7 %collective-permute-start = (bf16[64,1024]{1,0:T(8,128)(2,1)S(1)}, bf16[64,1024]{1,0:T(8,128)(2,1)S(1)}, u32[]{:S(2)}, u32[]{:S(2)}) collective-permute-start(bf16[64,1024]{1,0:T(8,128)(2,1)S(1)} %get-tuple-element.25.mine_ref), channel_id=1, source_target_pairs={{0,1},{1,0},{2,3},{3,2},{4,5},{5,4},{6,7},{7,6},{8,9},{9,8},{10,11... | collective-permute-start | bytes 393224 | tf_op jit(solution)/shard_map/ppermute | solution.py:330
  1.7 13.7 %collective-permute-start.2 = (bf16[64,1024]{1,0:T(8,128)(2,1)S(1)}, bf16[64,1024]{1,0:T(8,128)(2,1)S(1)}, u32[]{:S(2)}, u32[]{:S(2)}) collective-permute-start(bf16[64,1024]{1,0:T(8,128)(2,1)S(1)} %get-tuple-element.25.mine_ref), channel_id=1, source_target_pairs={{0,8},{1,9},{2,10},{3,11},{4,12},{5,13},{6,14},{7,15},{8,0},{9,1},... | collective-permute-start | bytes 393224 | tf_op jit(solution)/shard_map/ppermute | solution.py:330
  5.4 10.0 %collective-permute-start.1 = (bf16[64,1024]{1,0:T(8,128)(2,1)S(1)}, bf16[64,1024]{1,0:T(8,128)(2,1)S(1)}, u32[]{:S(2)}, u32[]{:S(2)}) collective-permute-start(bf16[64,1024]{1,0:T(8,128)(2,1)S(1)} %get-tuple-element.25.mine_ref), channel_id=1, source_target_pairs={{0,12},{1,13},{2,14},{3,15},{4,8},{5,9},{6,10},{7,11},{8,4},{9,5},... | collective-permute-start | bytes 393224 | tf_op jit(solution)/shard_map/ppermute | solution.py:330
  6.7 13.2 %collective-permute-start.6 = (bf16[64,1024]{1,0:T(8,128)(2,1)S(1)}, bf16[64,1024]{1,0:T(8,128)(2,1)S(1)}, u32[]{:S(2)}, u32[]{:S(2)}) collective-permute-start(bf16[64,1024]{1,0:T(8,128)(2,1)S(1)} %get-tuple-element.25.mine_ref), channel_id=1, source_target_pairs={{0,6},{1,7},{2,4},{3,5},{4,2},{5,3},{6,0},{7,1},{8,14},{9,15},{10,... | collective-permute-start | bytes 393224 | tf_op jit(solution)/shard_map/ppermute | solution.py:330
  7.9 19.6 %collective-permute-start.7 = (bf16[128,1024]{1,0:T(8,128)(2,1)S(1)}, bf16[128,1024]{1,0:T(8,128)(2,1)S(1)}, u32[]{:S(2)}, u32[]{:S(2)}) collective-permute-start(bf16[128,1024]{1,0:T(8,128)(2,1)S(1)} %pair.1.refs_0_), channel_id=1, source_target_pairs={{0,4},{1,3},{2,6},{3,1},{4,0},{5,7},{6,2},{7,5},{8,12},{9,11},{10,... | collective-permute-start | bytes 786440 | tf_op jit(solution)/shard_map/ppermute | solution.py:330
  10.9 19.1 %all-to-all-start = ((bf16[16,16,1024]{2,1,0:T(8,128)(2,1)}), bf16[16,16,1024]{2,1,0:T(8,128)(2,1)S(1)}, u32[]{:S(2)}, u32[]{:S(2)}) async-start(bf16[16,16,1024]{2,1,0:T(8,128)(2,1)} %pack.1), calls=%async_computation | async-start | bytes 1048576 | tf_op jit(solution)/shard_map/all_to_all | solution.py:374
  15.4 2.3 %copy-start = (s32[1024]{0:T(1024)S(1)}, s32[1024]{0:T(1024)}, u32[]{:S(2)}) copy-start(s32[1024]{0:T(1024)} %param.8) | copy-start | bytes 12292
  15.4 2.2 %copy-start.1 = (s32[4]{0:T(128)S(1)}, s32[4]{0:T(128)}, u32[]{:S(2)}) copy-start(s32[4]{0:T(128)} %lengths_ref.1) | copy-start | bytes 52
  15.4 9.2 %collective-permute-start.4 = (bf16[128,512]{1,0:T(8,128)(2,1)S(1)}, bf16[128,512]{1,0:T(8,128)(2,1)S(1)}, u32[]{:S(2)}, u32[]{:S(2)}) collective-permute-start(bf16[128,512]{1,0:T(8,128)(2,1)S(1)} %get-tuple-element.30.refs_0_), channel_id=1, source_target_pairs={{0,2},{1,3},{2,0},{3,1},{4,6},{5,7},{6,4},{7,5},{8,10},{9,11},{10,... | collective-permute-start | bytes 393224 | tf_op jit(solution)/shard_map/ppermute | solution.py:330
  17.3 10.2 %collective-permute-start.5 = (bf16[128,512]{1,0:T(8,128)(2,1)S(1)}, bf16[128,512]{1,0:T(8,128)(2,1)S(1)}, u32[]{:S(2)}, u32[]{:S(2)}) collective-permute-start(bf16[128,512]{1,0:T(8,128)(2,1)S(1)} %get-tuple-element.31), channel_id=1, source_target_pairs={{0,3},{1,2},{2,1},{3,0},{4,7},{5,6},{6,5},{7,4},{8,11},{9,10},{10,... | collective-permute-start | bytes 393224 | tf_op jit(solution)/shard_map/ppermute | solution.py:330
  17.3 10.2 %collective-permute-start.3 = (bf16[128,512]{1,0:T(8,128)(2,1)S(1)}, bf16[128,512]{1,0:T(8,128)(2,1)S(1)}, u32[]{:S(2)}, u32[]{:S(2)}) collective-permute-start(bf16[128,512]{1,0:T(8,128)(2,1)S(1)} %get-tuple-element.31), channel_id=1, source_target_pairs={{0,1},{1,0},{2,3},{3,2},{4,5},{5,4},{6,7},{7,6},{8,9},{9,8},{10,11... | collective-permute-start | bytes 393224 | tf_op jit(solution)/shard_map/ppermute | solution.py:330
  27.6 2.2 %collective-permute-start.8 = (bf16[192,512]{1,0:T(8,128)(2,1)S(1)}, bf16[192,512]{1,0:T(8,128)(2,1)S(1)}, u32[]{:S(2)}, u32[]{:S(2)}) collective-permute-start(bf16[192,512]{1,0:T(8,128)(2,1)S(1)} %get-tuple-element.36), channel_id=1, source_target_pairs={{0,1},{1,0},{2,3},{3,2},{4,5},{5,4},{6,7},{7,6},{8,9},{9,8},{10,11... | collective-permute-start | bytes 589832 | tf_op jit(solution)/shard_map/ppermute | solution.py:330
  31.9 1.6 %collective-permute-start.9 = (bf16[64,2048]{1,0:T(8,128)(2,1)S(1)}, bf16[64,2048]{1,0:T(8,128)(2,1)S(1)}, u32[]{:S(2)}, u32[]{:S(2)}) collective-permute-start(bf16[64,2048]{1,0:T(8,128)(2,1)S(1)} %get-tuple-element.39), channel_id=1, source_target_pairs={{0,1},{1,0},{2,3},{3,2},{4,5},{5,4},{6,7},{7,6},{8,9},{9,8},{10,11... | collective-permute-start | bytes 786440 | tf_op jit(solution)/shard_map/ppermute | solution.py:330

commit v10 on v9

--- a/solution.py
+++ b/solution.py
@@ -102,19 +102,24 @@
     out_ref[pl.ds(pl.multiple_of((1 - core) * rows, rows), rows), :] = other_ref[...]
 
 
-def heads_kernel(*refs):
-    outs = refs[-CORES:]
+def heads_kernel(count, *refs):
+    blocks, mine, others = refs[: -count - 1], refs[-count - 1], refs[-count:]
     core = lax.axis_index("ctx") % CORES
     width = HEADS * HD
-    for index in range(CORES):
-        col = jnp.bitwise_xor(core, index) * width
-        first = 0
-        for ref in refs[:-CORES]:
-            here = slice(first, first + ref.shape[0])
-            first = here.stop
+    rows = others[0].shape[0]
+    first = 0
+    for ref in blocks:
+        size = min(rows, ref.shape[0])
+        for begin in range(0, ref.shape[0], size):
             for half in range(2):
-                side = pl.ds(pl.multiple_of(col + half * KVH * HD, width), width)
-                outs[index][here, half * width : (half + 1) * width] = ref[:, side]
+                to = slice(half * width, (half + 1) * width)
+                col = half * KVH * HD
+                side = pl.ds(pl.multiple_of(core * width + col, width), width)
+                mine[first : first + size, to] = ref[begin : begin + size, side]
+                side = pl.ds(pl.multiple_of((1 - core) * width + col, width), width)
+                at = first % rows
+                others[first // rows][at : at + size, to] = ref[begin : begin + size, side]
+            first += size
 
 
 def place_kernel(per_chip, lengths_ref, owner_ref, pos_ref, start_ref, order_ref):
@@ -195,7 +200,8 @@
 
     senders = [jnp.bitwise_xor(me, index) for index in range(2 * CORES)]
     nodes = [[jnp.bitwise_xor(sender, offset) for offset in FAR] for sender in senders]
-    nodes += [[jnp.bitwise_xor(sender, DIAGONAL)] + chip_of(sender) for sender in senders[:CORES]]
+    nodes.append([jnp.bitwise_xor(me, DIAGONAL)] + chip_of(me))
+    nodes += [[node] for node in [jnp.bitwise_xor(senders[1], DIAGONAL)] + chip_of(senders[1])]
     nodes.append([me // CORES * CORES + core for core in range(CORES)])
     for ref, held in zip(pieces, nodes):
         for place, node in enumerate(held):
@@ -388,27 +394,26 @@
 
     if apart:
 
-        def heads_of(flops, *blocks):
-            count = sum(block.shape[0] for block in blocks)
+        def heads_of(flops, count, *blocks):
+            total_rows = sum(block.shape[0] for block in blocks)
+            shapes = [total_rows] + [total_rows // count] * count
             return pl.pallas_call(
-                heads_kernel,
-                out_shape=[jax.ShapeDtypeStruct((count, 2 * HEADS * HD), jnp.bfloat16)] * CORES,
+                functools.partial(heads_kernel, count),
+                out_shape=[jax.ShapeDtypeStruct((n, 2 * HEADS * HD), jnp.bfloat16) for n in shapes],
                 in_specs=[whole] * len(blocks),
-                out_specs=[whole] * CORES,
+                out_specs=[whole] * (1 + count),
                 compiler_params=VMEM,
                 cost_estimate=pl.CostEstimate(flops=flops, bytes_accessed=2**20, transcendentals=0),
                 name="heads",
             )(*blocks)
 
-        mine_far, other_far = heads_of(2 * 10**10, *far)
+        mine_far, other_far = heads_of(2 * 10**10, 1, *far)
         from_core, from_y, from_both = swap(other_far, 1), swap(mine_far, 2), swap(other_far, 3)
-        mine_chip, _ = heads_of(10**6, chip)
-        diagonal, next_chip, *_ = lax.optimization_barrier(
-            (diagonal, next_chip, from_core, from_y, from_both, mine_chip, order)
-        )
-        mine_near, other_near = heads_of(10**6, diagonal, next_chip)
-        kv_parts = [mine_far, from_core, from_y, from_both]
-        kv_parts += [mine_near, swap(other_near, 1), mine_chip]
+        mine_chip, _ = heads_of(10**6, 1, chip)
+        diagonal, next_chip, *_ = lax.optimization_barrier((diagonal, next_chip, order, mine_chip))
+        mine_near, *other_near = heads_of(10**6, 1 + CORES, diagonal, next_chip)
+        kv_parts = [mine_far, from_core, from_y, from_both, mine_near]
+        kv_parts += [swap(part, 1) for part in other_near] + [mine_chip]
         q_part = moved
     else:
         kv_parts = [moved]

time: 34.5 us -> 33.7 us (0.977)
  starting transfers between devices: 16.2 us -> 15.4 us
    all_to_all x1, waiting for transfers between devices: 0.01 us -> 1.26 us  [on_device(): lax.all_to_all(packed, 'ctx', split_axis=0, concat_axis=0, tiled=True)]
    ppermute x10 -> x12, waiting for transfers between devices: 9.74 us -> 8.52 us  [swap(): return lax.ppermute(array, 'ctx', pairs)]
    ppermute x10 -> x12, starting transfers between devices: 12.4 us -> 11.5 us  [swap(): return lax.ppermute(array, 'ctx', pairs)]
  transfers between devices with their start and end apart: 11 -> 13, of which waited for: 5 -> 6; matrix products, arithmetic and copies ran while one was open for 0% -> 0% of each run, Pallas kernels for 13% -> 13%
where the time goes in v10:
time: 33.7 us; the launch traced here: 33.4 us
  starting transfers between devices  15.4 us (46%)
  waiting for transfers between devices  9.78 us (29%)
  Pallas kernels  8.16 us (24%)
    ppermute x12, starting transfers between devices, swap(): return lax.ppermute(array, 'ctx', pairs)  11.5 us
    ppermute x12, waiting for transfers between devices, swap(): return lax.ppermute(array, 'ctx', pairs)  8.52 us
    all_to_all x1, starting transfers between devices, on_device(): lax.all_to_all(packed, 'ctx', split_axis=0, concat_axis=0, tiled=True)  3.86 us
    pallas_call x1, Pallas kernels, on_device(): pl.pallas_call(attend_kernel, out_shape=(jax.ShapeDtypeStruct((rows, HEAD...  1.9 us
    pallas_call x1, Pallas kernels, on_device(): pl.pallas_call(functools.partial(place_kernel, per_chip), out_shape=(jax....  1.57 us
    all_to_all x1, waiting for transfers between devices, on_device(): lax.all_to_all(packed, 'ctx', split_axis=0, concat_axis=0, tiled=True)  1.26 us
    pallas_call x1, Pallas kernels, on_device(): pl.pallas_call(fetch_kernel, out_shape=[jax.ShapeDtypeStruct((rows, rows)...  1.17 us
    pallas_call x1, Pallas kernels, on_device(): pl.pallas_call(functools.partial(pack_kernel, chips), out_shape=message,...  1.07 us
  transfers between devices with their start and end apart: 13, of which 6 were waited for; matrix products, arithmetic and copies ran while one was open for 0% of the time, Pallas kernels for 13%

profile of v10, /device:TPU:0, one launch (start us, length us, event | category | flops | bytes accessed | tf_op | source)
XLA Modules:
  0.0 33.4 jit_solution(13153434996724979784)
XLA Ops:
  0.0 1.2 %fetch.1 = (bf16[64,64]{1,0:T(8,128)(2,1)S(1)}, bf16[64,4096]{1,0:T(8,128)(2,1)S(1)}, bf16[64,1024]{1,0:T(8,128)(2,1)S(1)}) custom-call(s32[8,128]{1,0:T(8,128)} %bitcast.1, bf16[64,4096]{1,0:T(8,128)(2,1)} %q_hbm.1, bf16[64,512]{1,0:T(8,128)(2,1)} %k_hbm.1, bf16[64,512]{1,0:T(8,128)(2,1)} %v_hbm.1), custom_call_target="tpu_custom_call" | custom-call | tf_op jit(solution)/shard_map/fetch/pallas_call | solution.py:340
  1.2 0.5 %collective-permute-start = (bf16[64,1024]{1,0:T(8,128)(2,1)S(1)}, bf16[64,1024]{1,0:T(8,128)(2,1)S(1)}, u32[]{:S(2)}, u32[]{:S(2)}) collective-permute-start(bf16[64,1024]{1,0:T(8,128)(2,1)S(1)} %get-tuple-element.27.mine_ref), channel_id=1, source_target_pairs={{0,1},{1,0},{2,3},{3,2},{4,5},{5,4},{6,7},{7,6},{8,9},{9,8},{10,11... | collective-permute-start | bytes 393224 | tf_op jit(solution)/shard_map/ppermute | solution.py:336
  1.7 3.7 %collective-permute-start.2 = (bf16[64,1024]{1,0:T(8,128)(2,1)S(1)}, bf16[64,1024]{1,0:T(8,128)(2,1)S(1)}, u32[]{:S(2)}, u32[]{:S(2)}) collective-permute-start(bf16[64,1024]{1,0:T(8,128)(2,1)S(1)} %get-tuple-element.27.mine_ref), channel_id=1, source_target_pairs={{0,8},{1,9},{2,10},{3,11},{4,12},{5,13},{6,14},{7,15},{8,0},{9,1},... | collective-permute-start | bytes 393224 | tf_op jit(solution)/shard_map/ppermute | solution.py:336
  5.4 1.3 %collective-permute-start.1 = (bf16[64,1024]{1,0:T(8,128)(2,1)S(1)}, bf16[64,1024]{1,0:T(8,128)(2,1)S(1)}, u32[]{:S(2)}, u32[]{:S(2)}) collective-permute-start(bf16[64,1024]{1,0:T(8,128)(2,1)S(1)} %get-tuple-element.27.mine_ref), channel_id=1, source_target_pairs={{0,12},{1,13},{2,14},{3,15},{4,8},{5,9},{6,10},{7,11},{8,4},{9,5},... | collective-permute-start | bytes 393224 | tf_op jit(solution)/shard_map/ppermute | solution.py:336
  6.7 1.2 %collective-permute-start.6 = (bf16[64,1024]{1,0:T(8,128)(2,1)S(1)}, bf16[64,1024]{1,0:T(8,128)(2,1)S(1)}, u32[]{:S(2)}, u32[]{:S(2)}) collective-permute-start(bf16[64,1024]{1,0:T(8,128)(2,1)S(1)} %get-tuple-element.27.mine_ref), channel_id=1, source_target_pairs={{0,6},{1,7},{2,4},{3,5},{4,2},{5,3},{6,0},{7,1},{8,14},{9,15},{10,... | collective-permute-start | bytes 393224 | tf_op jit(solution)/shard_map/ppermute | solution.py:336
  7.9 0.0 collective-permute-done.other_ref
  7.9 1.9 %collective-permute-start.7 = (bf16[128,1024]{1,0:T(8,128)(2,1)S(1)}, bf16[128,1024]{1,0:T(8,128)(2,1)S(1)}, u32[]{:S(2)}, u32[]{:S(2)}) collective-permute-start(bf16[128,1024]{1,0:T(8,128)(2,1)S(1)} %pair.1.refs_0_), channel_id=1, source_target_pairs={{0,4},{1,3},{2,6},{3,1},{4,0},{5,7},{6,2},{7,5},{8,12},{9,11},{10,... | collective-permute-start | bytes 786440 | tf_op jit(solution)/shard_map/ppermute | solution.py:336
  9.8 1.1 %pack.1 = bf16[16,16,1024]{2,1,0:T(8,128)(2,1)} custom-call(bf16[64,64]{1,0:T(8,128)(2,1)S(1)} %get-tuple-element.25.order_ref, bf16[64,4096]{1,0:T(8,128)(2,1)S(1)} %get-tuple-element.28.q_ref), custom_call_target="tpu_custom_call" | custom-call | flops 33554432 | bytes 1048576 | tf_op jit(solution)/shard_map/pack/pallas_call | solution.py:369
  10.9 3.9 %all-to-all-start = ((bf16[16,16,1024]{2,1,0:T(8,128)(2,1)}), bf16[16,16,1024]{2,1,0:T(8,128)(2,1)S(1)}, u32[]{:S(2)}, u32[]{:S(2)}) async-start(bf16[16,16,1024]{2,1,0:T(8,128)(2,1)} %pack.1), calls=%async_computation | async-start | bytes 1048576 | tf_op jit(solution)/shard_map/all_to_all | solution.py:380
  14.7 0.6 %collective-permute-done.2.refs_1_ = bf16[64,1024]{1,0:T(8,128)(2,1)S(1)} collective-permute-done((bf16[64,1024]{1,0:T(8,128)(2,1)S(1)}, bf16[64,1024]{1,0:T(8,128)(2,1)S(1)}, u32[]{:S(2)}, u32[]{:S(2)}) %collective-permute-start.2) | collective-permute-done | bytes 131104 | tf_op jit(solution)/shard_map/ppermute | solution.py:336
  15.4 0.0 collective-permute-done.1.refs_0_
  15.4 0.0 copy-start
  15.4 0.0 copy-start.1
  15.4 1.8 %collective-permute-start.4 = (bf16[128,512]{1,0:T(8,128)(2,1)S(1)}, bf16[128,512]{1,0:T(8,128)(2,1)S(1)}, u32[]{:S(2)}, u32[]{:S(2)}) collective-permute-start(bf16[128,512]{1,0:T(8,128)(2,1)S(1)} %get-tuple-element.32.refs_0_), channel_id=1, source_target_pairs={{0,2},{1,3},{2,0},{3,1},{4,6},{5,7},{6,4},{7,5},{8,10},{9,11},{10,... | collective-permute-start | bytes 393224 | tf_op jit(solution)/shard_map/ppermute | solution.py:336
  17.3 0.0 collective-permute-start.5
  17.3 0.4 %collective-permute-start.3 = (bf16[128,512]{1,0:T(8,128)(2,1)S(1)}, bf16[128,512]{1,0:T(8,128)(2,1)S(1)}, u32[]{:S(2)}, u32[]{:S(2)}) collective-permute-start(bf16[128,512]{1,0:T(8,128)(2,1)S(1)} %get-tuple-element.33), channel_id=1, source_target_pairs={{0,1},{1,0},{2,3},{3,2},{4,5},{5,4},{6,7},{7,6},{8,9},{9,8},{10,11... | collective-permute-start | bytes 393224 | tf_op jit(solution)/shard_map/ppermute | solution.py:336
  17.6 0.0 copy-done
  17.6 0.0 copy-done.1
  17.6 1.6 %place.1 = (s32[128,128]{1,0:T(8,128)S(1)}, s32[128,128]{1,0:T(8,128)S(1)}, bf16[128,128]{1,0:T(8,128)(2,1)S(1)}) custom-call(s32[4]{0:T(128)S(1)} %copy-done.1, s32[8,128]{1,0:T(8,128)S(1)} %bitcast.2), custom_call_target="tpu_custom_call" | custom-call | tf_op jit(solution)/shard_map/place/pallas_call | solution.py:382
  19.2 0.7 %heads.4 = (bf16[128,512]{1,0:T(8,128)(2,1)S(1)}, bf16[128,512]{1,0:T(8,128)(2,1)}) custom-call(bf16[128,1024]{1,0:T(8,128)(2,1)S(1)} %pair.1.refs_0_), custom_call_target="tpu_custom_call" | custom-call | flops 1000000 | bytes 1048576 | tf_op jit(solution)/shard_map/heads/pallas_call | solution.py:400
  19.9 0.0 collective-permute-done.6.refs_0_
  19.9 5.9 %collective-permute-done.7.refs_1_ = bf16[128,1024]{1,0:T(8,128)(2,1)S(1)} collective-permute-done((bf16[128,1024]{1,0:T(8,128)(2,1)S(1)}, bf16[128,1024]{1,0:T(8,128)(2,1)S(1)}, u32[]{:S(2)}, u32[]{:S(2)}) %collective-permute-start.7) | collective-permute-done | bytes 262176 | tf_op jit(solution)/shard_map/ppermute | solution.py:336
  25.8 0.1 heads.5
  25.9 0.1 collective-permute-start.8
  26.0 0.5 %collective-permute-start.9 = (bf16[64,512]{1,0:T(8,128)(2,1)S(1)}, bf16[64,512]{1,0:T(8,128)(2,1)S(1)}, u32[]{:S(2)}, u32[]{:S(2)}) collective-permute-start(bf16[64,512]{1,0:T(8,128)(2,1)S(1)} %get-tuple-element.39), channel_id=1, source_target_pairs={{0,1},{1,0},{2,3},{3,2},{4,5},{5,4},{6,7},{7,6},{8,9},{9,8},{10,11... | collective-permute-start | bytes 196616 | tf_op jit(solution)/shard_map/ppermute | solution.py:336
  26.5 0.0 collective-permute-done.4.refs_2_
  26.5 0.1 collective-permute-start.10
  26.5 0.9 %collective-permute-done.5.refs_3_ = bf16[128,512]{1,0:T(8,128)(2,1)S(1)} collective-permute-done((bf16[128,512]{1,0:T(8,128)(2,1)S(1)}, bf16[128,512]{1,0:T(8,128)(2,1)S(1)}, u32[]{:S(2)}, u32[]{:S(2)}) %collective-permute-start.5) | collective-permute-done | bytes 131104 | tf_op jit(solution)/shard_map/ppermute | solution.py:336
  27.5 0.0 collective-permute-done.3.refs_1_
  27.5 0.0 collective-permute-done.8.refs_5_
  27.5 0.0 collective-permute-done.9.refs_6_
  27.5 0.2 collective-permute-done.10.refs_7_
  27.7 0.2 unpack.1
  27.9 1.3 %all-to-all-done.q_ref = bf16[16,16,1024]{2,1,0:T(8,128)(2,1)S(1)} async-done(((bf16[16,16,1024]{2,1,0:T(8,128)(2,1)}), bf16[16,16,1024]{2,1,0:T(8,128)(2,1)S(1)}, u32[]{:S(2)}, u32[]{:S(2)}) %all-to-all-start) | async-done | bytes 524320 | tf_op jit(solution)/shard_map/all_to_all | solution.py:380
  29.2 1.9 %attend.1 = (bf16[64,2048]{1,0:T(8,128)(2,1)S(1)}, bf16[64,2048]{1,0:T(8,128)(2,1)S(1)}) custom-call(bf16[16,16,1024]{2,1,0:T(8,128)(2,1)S(1)} %all-to-all-done.q_ref, s32[128,128]{1,0:T(8,128)S(1)} %get-tuple-element.29.pos_ref, s32[128,128]{1,0:T(8,128)S(1)} %get-tuple-element.30.start_ref, bf16[128,128]{1,0:T(8,128)(2,1)S(1)} %get-tuple-element.31.order_ref, ...), custom_call_target="tpu_custom_call" | custom-call | tf_op jit(solution)/shard_map/attend/pallas_call | solution.py:435
  31.1 0.1 collective-permute-start.11
  31.2 0.7 %write_own.1.refs_0_ = bf16[64,4096]{1,0:T(8,128)(2,1)} custom-call(bf16[64,2048]{1,0:T(8,128)(2,1)S(1)} %get-tuple-element.44.heads_ref), custom_call_target="tpu_custom_call" | custom-call | tf_op jit(solution)/shard_map/write_own/pallas_call | solution.py:446
  31.9 0.8 %collective-permute-done.11.heads_ref = bf16[64,2048]{1,0:T(8,128)(2,1)S(1)} collective-permute-done((bf16[64,2048]{1,0:T(8,128)(2,1)S(1)}, bf16[64,2048]{1,0:T(8,128)(2,1)S(1)}, u32[]{:S(2)}, u32[]{:S(2)}) %collective-permute-start.11) | collective-permute-done | bytes 262176 | tf_op jit(solution)/shard_map/ppermute | solution.py:336
  32.7 0.7 %write_received.1 = bf16[64,4096]{1,0:T(8,128)(2,1)} custom-call(bf16[64,2048]{1,0:T(8,128)(2,1)S(1)} %collective-permute-done.11.heads_ref, bf16[64,4096]{1,0:T(8,128)(2,1)} %write_own.1.refs_0_), custom_call_target="tpu_custom_call", output_to_operand_aliasing={{}: (1, {})} | custom-call | tf_op jit(solution)/shard_map/write_received/pallas_call | solution.py:455
  (2 shorter events, 0.1 us)
Async XLA Ops:
  1.2 6.7 %collective-permute-start = (bf16[64,1024]{1,0:T(8,128)(2,1)S(1)}, bf16[64,1024]{1,0:T(8,128)(2,1)S(1)}, u32[]{:S(2)}, u32[]{:S(2)}) collective-permute-start(bf16[64,1024]{1,0:T(8,128)(2,1)S(1)} %get-tuple-element.27.mine_ref), channel_id=1, source_target_pairs={{0,1},{1,0},{2,3},{3,2},{4,5},{5,4},{6,7},{7,6},{8,9},{9,8},{10,11... | collective-permute-start | bytes 393224 | tf_op jit(solution)/shard_map/ppermute | solution.py:336
  1.7 13.7 %collective-permute-start.2 = (bf16[64,1024]{1,0:T(8,128)(2,1)S(1)}, bf16[64,1024]{1,0:T(8,128)(2,1)S(1)}, u32[]{:S(2)}, u32[]{:S(2)}) collective-permute-start(bf16[64,1024]{1,0:T(8,128)(2,1)S(1)} %get-tuple-element.27.mine_ref), channel_id=1, source_target_pairs={{0,8},{1,9},{2,10},{3,11},{4,12},{5,13},{6,14},{7,15},{8,0},{9,1},... | collective-permute-start | bytes 393224 | tf_op jit(solution)/shard_map/ppermute | solution.py:336
  5.4 10.0 %collective-permute-start.1 = (bf16[64,1024]{1,0:T(8,128)(2,1)S(1)}, bf16[64,1024]{1,0:T(8,128)(2,1)S(1)}, u32[]{:S(2)}, u32[]{:S(2)}) collective-permute-start(bf16[64,1024]{1,0:T(8,128)(2,1)S(1)} %get-tuple-element.27.mine_ref), channel_id=1, source_target_pairs={{0,12},{1,13},{2,14},{3,15},{4,8},{5,9},{6,10},{7,11},{8,4},{9,5},... | collective-permute-start | bytes 393224 | tf_op jit(solution)/shard_map/ppermute | solution.py:336
  6.7 13.2 %collective-permute-start.6 = (bf16[64,1024]{1,0:T(8,128)(2,1)S(1)}, bf16[64,1024]{1,0:T(8,128)(2,1)S(1)}, u32[]{:S(2)}, u32[]{:S(2)}) collective-permute-start(bf16[64,1024]{1,0:T(8,128)(2,1)S(1)} %get-tuple-element.27.mine_ref), channel_id=1, source_target_pairs={{0,6},{1,7},{2,4},{3,5},{4,2},{5,3},{6,0},{7,1},{8,14},{9,15},{10,... | collective-permute-start | bytes 393224 | tf_op jit(solution)/shard_map/ppermute | solution.py:336
  7.9 17.9 %collective-permute-start.7 = (bf16[128,1024]{1,0:T(8,128)(2,1)S(1)}, bf16[128,1024]{1,0:T(8,128)(2,1)S(1)}, u32[]{:S(2)}, u32[]{:S(2)}) collective-permute-start(bf16[128,1024]{1,0:T(8,128)(2,1)S(1)} %pair.1.refs_0_), channel_id=1, source_target_pairs={{0,4},{1,3},{2,6},{3,1},{4,0},{5,7},{6,2},{7,5},{8,12},{9,11},{10,... | collective-permute-start | bytes 786440 | tf_op jit(solution)/shard_map/ppermute | solution.py:336
  10.9 18.3 %all-to-all-start = ((bf16[16,16,1024]{2,1,0:T(8,128)(2,1)}), bf16[16,16,1024]{2,1,0:T(8,128)(2,1)S(1)}, u32[]{:S(2)}, u32[]{:S(2)}) async-start(bf16[16,16,1024]{2,1,0:T(8,128)(2,1)} %pack.1), calls=%async_computation | async-start | bytes 1048576 | tf_op jit(solution)/shard_map/all_to_all | solution.py:380
  15.4 2.3 %copy-start = (s32[1024]{0:T(1024)S(1)}, s32[1024]{0:T(1024)}, u32[]{:S(2)}) copy-start(s32[1024]{0:T(1024)} %param.8) | copy-start | bytes 12292
  15.4 2.2 %copy-start.1 = (s32[4]{0:T(128)S(1)}, s32[4]{0:T(128)}, u32[]{:S(2)}) copy-start(s32[4]{0:T(128)} %lengths_ref.1) | copy-start | bytes 52
  15.4 11.0 %collective-permute-start.4 = (bf16[128,512]{1,0:T(8,128)(2,1)S(1)}, bf16[128,512]{1,0:T(8,128)(2,1)S(1)}, u32[]{:S(2)}, u32[]{:S(2)}) collective-permute-start(bf16[128,512]{1,0:T(8,128)(2,1)S(1)} %get-tuple-element.32.refs_0_), channel_id=1, source_target_pairs={{0,2},{1,3},{2,0},{3,1},{4,6},{5,7},{6,4},{7,5},{8,10},{9,11},{10,... | collective-permute-start | bytes 393224 | tf_op jit(solution)/shard_map/ppermute | solution.py:336
  17.3 10.2 %collective-permute-start.5 = (bf16[128,512]{1,0:T(8,128)(2,1)S(1)}, bf16[128,512]{1,0:T(8,128)(2,1)S(1)}, u32[]{:S(2)}, u32[]{:S(2)}) collective-permute-start(bf16[128,512]{1,0:T(8,128)(2,1)S(1)} %get-tuple-element.33), channel_id=1, source_target_pairs={{0,3},{1,2},{2,1},{3,0},{4,7},{5,6},{6,5},{7,4},{8,11},{9,10},{10,... | collective-permute-start | bytes 393224 | tf_op jit(solution)/shard_map/ppermute | solution.py:336
  17.3 10.2 %collective-permute-start.3 = (bf16[128,512]{1,0:T(8,128)(2,1)S(1)}, bf16[128,512]{1,0:T(8,128)(2,1)S(1)}, u32[]{:S(2)}, u32[]{:S(2)}) collective-permute-start(bf16[128,512]{1,0:T(8,128)(2,1)S(1)} %get-tuple-element.33), channel_id=1, source_target_pairs={{0,1},{1,0},{2,3},{3,2},{4,5},{5,4},{6,7},{7,6},{8,9},{9,8},{10,11... | collective-permute-start | bytes 393224 | tf_op jit(solution)/shard_map/ppermute | solution.py:336
  25.9 1.6 %collective-permute-start.8 = (bf16[64,512]{1,0:T(8,128)(2,1)S(1)}, bf16[64,512]{1,0:T(8,128)(2,1)S(1)}, u32[]{:S(2)}, u32[]{:S(2)}) collective-permute-start(bf16[64,512]{1,0:T(8,128)(2,1)S(1)} %get-tuple-element.38), channel_id=1, source_target_pairs={{0,1},{1,0},{2,3},{3,2},{4,5},{5,4},{6,7},{7,6},{8,9},{9,8},{10,11... | collective-permute-start | bytes 196616 | tf_op jit(solution)/shard_map/ppermute | solution.py:336
  26.0 1.5 %collective-permute-start.9 = (bf16[64,512]{1,0:T(8,128)(2,1)S(1)}, bf16[64,512]{1,0:T(8,128)(2,1)S(1)}, u32[]{:S(2)}, u32[]{:S(2)}) collective-permute-start(bf16[64,512]{1,0:T(8,128)(2,1)S(1)} %get-tuple-element.39), channel_id=1, source_target_pairs={{0,1},{1,0},{2,3},{3,2},{4,5},{5,4},{6,7},{7,6},{8,9},{9,8},{10,11... | collective-permute-start | bytes 196616 | tf_op jit(solution)/shard_map/ppermute | solution.py:336
  26.5 1.3 %collective-permute-start.10 = (bf16[64,512]{1,0:T(8,128)(2,1)S(1)}, bf16[64,512]{1,0:T(8,128)(2,1)S(1)}, u32[]{:S(2)}, u32[]{:S(2)}) collective-permute-start(bf16[64,512]{1,0:T(8,128)(2,1)S(1)} %get-tuple-element.40), channel_id=1, source_target_pairs={{0,1},{1,0},{2,3},{3,2},{4,5},{5,4},{6,7},{7,6},{8,9},{9,8},{10,11... | collective-permute-start | bytes 196616 | tf_op jit(solution)/shard_map/ppermute | solution.py:336
  31.1 1.6 %collective-permute-start.11 = (bf16[64,2048]{1,0:T(8,128)(2,1)S(1)}, bf16[64,2048]{1,0:T(8,128)(2,1)S(1)}, u32[]{:S(2)}, u32[]{:S(2)}) collective-permute-start(bf16[64,2048]{1,0:T(8,128)(2,1)S(1)} %get-tuple-element.43), channel_id=1, source_target_pairs={{0,1},{1,0},{2,3},{3,2},{4,5},{5,4},{6,7},{7,6},{8,9},{9,8},{10,11... | collective-permute-start | bytes 786440 | tf_op jit(solution)/shard_map/ppermute | solution.py:336

commit v11 on v10

--- a/solution.py
+++ b/solution.py
@@ -224,8 +224,7 @@
         unpack_pieces(kv_refs, tokens, k_all, v_all)
 
 
-def attend_kernel(q_ref, pos_ref, start_ref, order_ref, k_all, v_all, *refs):
-    out_refs, context = refs[:CORES], refs[CORES]
+def attend_kernel(q_ref, pos_ref, start_ref, order_ref, k_all, v_all, context, other_ref):
     total = k_all.shape[0]
     held = context.shape[0]
     block_rows = 32
@@ -302,21 +301,27 @@
                 peak = top
             store(block, head, sums)
 
-    rows = held // CORES
-    for core in range(CORES):
-        order = order_ref[core * rows : (core + 1) * rows, :]
-        moved = jnp.dot(order, context[...], preferred_element_type=jnp.float32)
-        out_refs[core][...] = moved.astype(jnp.bfloat16)
-
-
-def write_kernel(other, heads_ref, *refs):
-    out_hbm, sem = refs[-2:]
-    core = jnp.bitwise_xor(lax.axis_index("ctx") % CORES, other)
+    moved = jnp.dot(order_ref[held // CORES :, :], context[...], preferred_element_type=jnp.float32)
+    other_ref[...] = moved.astype(jnp.bfloat16)
+
+
+def copy_to_columns(core, source_ref, out_hbm, sem):
     width = HEADS * WIDE
     side = pl.ds(pl.multiple_of(core * width, width), width)
-    copy = pltpu.make_async_copy(heads_ref, out_hbm.at[:, side], sem)
+    copy = pltpu.make_async_copy(source_ref, out_hbm.at[:, side], sem)
     copy.start()
     copy.wait()
+
+
+def write_own_kernel(order_ref, context_ref, out_hbm, own_ref, sem):
+    order = order_ref[: own_ref.shape[0], :]
+    moved = jnp.dot(order, context_ref[...], preferred_element_type=jnp.float32)
+    own_ref[...] = moved.astype(jnp.bfloat16)
+    copy_to_columns(lax.axis_index("ctx") % CORES, own_ref, out_hbm, sem)
+
+
+def write_received_kernel(received_ref, half_hbm, out_hbm, sem):
+    copy_to_columns(1 - lax.axis_index("ctx") % CORES, received_ref, out_hbm, sem)
 
 
 def on_device(queries, keys, values, owner, rollout_lengths):
@@ -410,7 +415,7 @@
         mine_far, other_far = heads_of(2 * 10**10, 1, *far)
         from_core, from_y, from_both = swap(other_far, 1), swap(mine_far, 2), swap(other_far, 3)
         mine_chip, _ = heads_of(10**6, 1, chip)
-        diagonal, next_chip, *_ = lax.optimization_barrier((diagonal, next_chip, order, mine_chip))
+        diagonal, next_chip, *_ = lax.optimization_barrier((diagonal, next_chip, order))
         mine_near, *other_near = heads_of(10**6, 1 + CORES, diagonal, next_chip)
         kv_parts = [mine_far, from_core, from_y, from_both, mine_near]
         kv_parts += [swap(part, 1) for part in other_near] + [mine_chip]
@@ -432,28 +437,30 @@
         compiler_params=VMEM,
         name="unpack",
     )(*kv_parts)
-    own, other = pl.pallas_call(
+    context, other = pl.pallas_call(
         attend_kernel,
-        out_shape=(jax.ShapeDtypeStruct((rows, HEADS * WIDE), jnp.bfloat16),) * CORES,
+        out_shape=(
+            jax.ShapeDtypeStruct((held, HEADS * WIDE), jnp.bfloat16),
+            jax.ShapeDtypeStruct((rows, HEADS * WIDE), jnp.bfloat16),
+        ),
         in_specs=[whole] * 6,
-        out_specs=(whole,) * CORES,
-        scratch_shapes=[pltpu.VMEM((held, HEADS * WIDE), jnp.bfloat16)],
+        out_specs=(whole, whole),
         compiler_params=VMEM,
         name="attend",
     )(q_part, pos, start, order, k_all, v_all)
 
     result = jax.ShapeDtypeStruct((rows, H * HD), jnp.bfloat16)
     half = pl.pallas_call(
-        functools.partial(write_kernel, 0),
+        write_own_kernel,
         out_shape=result,
-        in_specs=[whole],
+        in_specs=[whole] * 2,
         out_specs=hbm,
-        scratch_shapes=[pltpu.SemaphoreType.DMA],
+        scratch_shapes=[pltpu.VMEM((rows, HEADS * WIDE), jnp.bfloat16), pltpu.SemaphoreType.DMA],
         compiler_params=VMEM,
         name="write_own",
-    )(own)
+    )(order, context)
     return pl.pallas_call(
-        functools.partial(write_kernel, 1),
+        write_received_kernel,
         out_shape=result,
         in_specs=[whole, hbm],
         out_specs=hbm,

time: 33.7 us -> 33.6 us (level)
  transfers between devices with their start and end apart: 13 -> 13, of which waited for: 6 -> 6; matrix products, arithmetic and copies ran while one was open for 0% -> 0% of each run, Pallas kernels for 13% -> 14%
where the time goes in v11:
time: 33.6 us; the launch traced here: 33.3 us
  starting transfers between devices  15.4 us (46%)
  waiting for transfers between devices  9.58 us (29%)
  Pallas kernels  8.29 us (25%)
    ppermute x12, starting transfers between devices, swap(): return lax.ppermute(array, 'ctx', pairs)  11.5 us
    ppermute x12, waiting for transfers between devices, swap(): return lax.ppermute(array, 'ctx', pairs)  8.32 us
    all_to_all x1, starting transfers between devices, on_device(): lax.all_to_all(packed, 'ctx', split_axis=0, concat_axis=0, tiled=True)  3.86 us
    pallas_call x1, Pallas kernels, on_device(): pl.pallas_call(attend_kernel, out_shape=(jax.ShapeDtypeStruct((held, HEAD...  1.84 us
    pallas_call x1, Pallas kernels, on_device(): pl.pallas_call(functools.partial(place_kernel, per_chip), out_shape=(jax....  1.57 us
    all_to_all x1, waiting for transfers between devices, on_device(): lax.all_to_all(packed, 'ctx', split_axis=0, concat_axis=0, tiled=True)  1.26 us
    pallas_call x1, Pallas kernels, on_device(): pl.pallas_call(fetch_kernel, out_shape=[jax.ShapeDtypeStruct((rows, rows)...  1.17 us
    pallas_call x1, Pallas kernels, on_device(): pl.pallas_call(functools.partial(pack_kernel, chips), out_shape=message,...  1.07 us
  transfers between devices with their start and end apart: 13, of which 6 were waited for; matrix products, arithmetic and copies ran while one was open for 0% of the time, Pallas kernels for 14%

profile of v11, /device:TPU:0, one launch (start us, length us, event | category | flops | bytes accessed | tf_op | source)
XLA Modules:
  0.0 33.3 jit_solution(2999030441462574903)
XLA Ops:
  0.0 1.2 %fetch.1 = (bf16[64,64]{1,0:T(8,128)(2,1)S(1)}, bf16[64,4096]{1,0:T(8,128)(2,1)S(1)}, bf16[64,1024]{1,0:T(8,128)(2,1)S(1)}) custom-call(s32[8,128]{1,0:T(8,128)} %bitcast.1, bf16[64,4096]{1,0:T(8,128)(2,1)} %q_hbm.1, bf16[64,512]{1,0:T(8,128)(2,1)} %k_hbm.1, bf16[64,512]{1,0:T(8,128)(2,1)} %v_hbm.1), custom_call_target="tpu_custom_call" | custom-call | tf_op jit(solution)/shard_map/fetch/pallas_call | solution.py:345
  1.2 0.5 %collective-permute-start = (bf16[64,1024]{1,0:T(8,128)(2,1)S(1)}, bf16[64,1024]{1,0:T(8,128)(2,1)S(1)}, u32[]{:S(2)}, u32[]{:S(2)}) collective-permute-start(bf16[64,1024]{1,0:T(8,128)(2,1)S(1)} %get-tuple-element.27.mine_ref), channel_id=1, source_target_pairs={{0,1},{1,0},{2,3},{3,2},{4,5},{5,4},{6,7},{7,6},{8,9},{9,8},{10,11... | collective-permute-start | bytes 393224 | tf_op jit(solution)/shard_map/ppermute | solution.py:341
  1.7 3.7 %collective-permute-start.2 = (bf16[64,1024]{1,0:T(8,128)(2,1)S(1)}, bf16[64,1024]{1,0:T(8,128)(2,1)S(1)}, u32[]{:S(2)}, u32[]{:S(2)}) collective-permute-start(bf16[64,1024]{1,0:T(8,128)(2,1)S(1)} %get-tuple-element.27.mine_ref), channel_id=1, source_target_pairs={{0,8},{1,9},{2,10},{3,11},{4,12},{5,13},{6,14},{7,15},{8,0},{9,1},... | collective-permute-start | bytes 393224 | tf_op jit(solution)/shard_map/ppermute | solution.py:341
  5.4 1.3 %collective-permute-start.1 = (bf16[64,1024]{1,0:T(8,128)(2,1)S(1)}, bf16[64,1024]{1,0:T(8,128)(2,1)S(1)}, u32[]{:S(2)}, u32[]{:S(2)}) collective-permute-start(bf16[64,1024]{1,0:T(8,128)(2,1)S(1)} %get-tuple-element.27.mine_ref), channel_id=1, source_target_pairs={{0,12},{1,13},{2,14},{3,15},{4,8},{5,9},{6,10},{7,11},{8,4},{9,5},... | collective-permute-start | bytes 393224 | tf_op jit(solution)/shard_map/ppermute | solution.py:341
  6.7 1.2 %collective-permute-start.6 = (bf16[64,1024]{1,0:T(8,128)(2,1)S(1)}, bf16[64,1024]{1,0:T(8,128)(2,1)S(1)}, u32[]{:S(2)}, u32[]{:S(2)}) collective-permute-start(bf16[64,1024]{1,0:T(8,128)(2,1)S(1)} %get-tuple-element.27.mine_ref), channel_id=1, source_target_pairs={{0,6},{1,7},{2,4},{3,5},{4,2},{5,3},{6,0},{7,1},{8,14},{9,15},{10,... | collective-permute-start | bytes 393224 | tf_op jit(solution)/shard_map/ppermute | solution.py:341
  7.9 0.0 collective-permute-done.other_ref
  7.9 1.9 %collective-permute-start.7 = (bf16[128,1024]{1,0:T(8,128)(2,1)S(1)}, bf16[128,1024]{1,0:T(8,128)(2,1)S(1)}, u32[]{:S(2)}, u32[]{:S(2)}) collective-permute-start(bf16[128,1024]{1,0:T(8,128)(2,1)S(1)} %pair.1.refs_0_), channel_id=1, source_target_pairs={{0,4},{1,3},{2,6},{3,1},{4,0},{5,7},{6,2},{7,5},{8,12},{9,11},{10,... | collective-permute-start | bytes 786440 | tf_op jit(solution)/shard_map/ppermute | solution.py:341
  9.8 1.1 %pack.1 = bf16[16,16,1024]{2,1,0:T(8,128)(2,1)} custom-call(bf16[64,64]{1,0:T(8,128)(2,1)S(1)} %get-tuple-element.25.order_ref, bf16[64,4096]{1,0:T(8,128)(2,1)S(1)} %get-tuple-element.28.q_ref), custom_call_target="tpu_custom_call" | custom-call | flops 33554432 | bytes 1048576 | tf_op jit(solution)/shard_map/pack/pallas_call | solution.py:374
  10.9 3.9 %all-to-all-start = ((bf16[16,16,1024]{2,1,0:T(8,128)(2,1)}), bf16[16,16,1024]{2,1,0:T(8,128)(2,1)S(1)}, u32[]{:S(2)}, u32[]{:S(2)}) async-start(bf16[16,16,1024]{2,1,0:T(8,128)(2,1)} %pack.1), calls=%async_computation | async-start | bytes 1048576 | tf_op jit(solution)/shard_map/all_to_all | solution.py:385
  14.7 0.6 %collective-permute-done.2.refs_1_ = bf16[64,1024]{1,0:T(8,128)(2,1)S(1)} collective-permute-done((bf16[64,1024]{1,0:T(8,128)(2,1)S(1)}, bf16[64,1024]{1,0:T(8,128)(2,1)S(1)}, u32[]{:S(2)}, u32[]{:S(2)}) %collective-permute-start.2) | collective-permute-done | bytes 131104 | tf_op jit(solution)/shard_map/ppermute | solution.py:341
  15.4 0.0 collective-permute-done.1.refs_0_
  15.4 0.0 copy-start
  15.4 0.0 copy-start.1
  15.4 1.8 %collective-permute-start.4 = (bf16[128,512]{1,0:T(8,128)(2,1)S(1)}, bf16[128,512]{1,0:T(8,128)(2,1)S(1)}, u32[]{:S(2)}, u32[]{:S(2)}) collective-permute-start(bf16[128,512]{1,0:T(8,128)(2,1)S(1)} %get-tuple-element.32.refs_0_), channel_id=1, source_target_pairs={{0,2},{1,3},{2,0},{3,1},{4,6},{5,7},{6,4},{7,5},{8,10},{9,11},{10,... | collective-permute-start | bytes 393224 | tf_op jit(solution)/shard_map/ppermute | solution.py:341
  17.3 0.0 collective-permute-start.5
  17.3 0.4 %collective-permute-start.3 = (bf16[128,512]{1,0:T(8,128)(2,1)S(1)}, bf16[128,512]{1,0:T(8,128)(2,1)S(1)}, u32[]{:S(2)}, u32[]{:S(2)}) collective-permute-start(bf16[128,512]{1,0:T(8,128)(2,1)S(1)} %get-tuple-element.33), channel_id=1, source_target_pairs={{0,1},{1,0},{2,3},{3,2},{4,5},{5,4},{6,7},{7,6},{8,9},{9,8},{10,11... | collective-permute-start | bytes 393224 | tf_op jit(solution)/shard_map/ppermute | solution.py:341
  17.6 0.0 copy-done
  17.6 0.0 copy-done.1
  17.6 1.6 %place.1 = (s32[128,128]{1,0:T(8,128)S(1)}, s32[128,128]{1,0:T(8,128)S(1)}, bf16[128,128]{1,0:T(8,128)(2,1)S(1)}) custom-call(s32[4]{0:T(128)S(1)} %copy-done.1, s32[8,128]{1,0:T(8,128)S(1)} %bitcast.2), custom_call_target="tpu_custom_call" | custom-call | tf_op jit(solution)/shard_map/place/pallas_call | solution.py:387
  19.2 0.0 collective-permute-done.6.refs_0_
  19.2 6.6 %collective-permute-done.7.refs_1_ = bf16[128,1024]{1,0:T(8,128)(2,1)S(1)} collective-permute-done((bf16[128,1024]{1,0:T(8,128)(2,1)S(1)}, bf16[128,1024]{1,0:T(8,128)(2,1)S(1)}, u32[]{:S(2)}, u32[]{:S(2)}) %collective-permute-start.7) | collective-permute-done | bytes 262176 | tf_op jit(solution)/shard_map/ppermute | solution.py:341
  25.8 0.1 heads.4
  25.9 0.1 collective-permute-start.8
  26.0 0.5 %collective-permute-start.9 = (bf16[64,512]{1,0:T(8,128)(2,1)S(1)}, bf16[64,512]{1,0:T(8,128)(2,1)S(1)}, u32[]{:S(2)}, u32[]{:S(2)}) collective-permute-start(bf16[64,512]{1,0:T(8,128)(2,1)S(1)} %get-tuple-element.38), channel_id=1, source_target_pairs={{0,1},{1,0},{2,3},{3,2},{4,5},{5,4},{6,7},{7,6},{8,9},{9,8},{10,11... | collective-permute-start | bytes 196616 | tf_op jit(solution)/shard_map/ppermute | solution.py:341
  26.5 0.0 collective-permute-done.4.refs_2_
  26.5 0.1 collective-permute-start.10
  26.5 0.7 %heads.5 = (bf16[128,512]{1,0:T(8,128)(2,1)S(1)}, bf16[128,512]{1,0:T(8,128)(2,1)}) custom-call(bf16[128,1024]{1,0:T(8,128)(2,1)S(1)} %pair.1.refs_0_), custom_call_target="tpu_custom_call" | custom-call | flops 1000000 | bytes 1048576 | tf_op jit(solution)/shard_map/heads/pallas_call | solution.py:405
  27.2 0.3 collective-permute-done.5.refs_3_
  27.5 0.0 collective-permute-done.3.refs_1_
  27.5 0.0 collective-permute-done.8.refs_5_
  27.5 0.0 collective-permute-done.9.refs_6_
  27.5 0.2 collective-permute-done.10.refs_7_
  27.7 0.2 unpack.1
  27.9 1.3 %all-to-all-done.q_ref = bf16[16,16,1024]{2,1,0:T(8,128)(2,1)S(1)} async-done(((bf16[16,16,1024]{2,1,0:T(8,128)(2,1)}), bf16[16,16,1024]{2,1,0:T(8,128)(2,1)S(1)}, u32[]{:S(2)}, u32[]{:S(2)}) %all-to-all-start) | async-done | bytes 524320 | tf_op jit(solution)/shard_map/all_to_all | solution.py:385
  29.2 1.8 %attend.1 = (bf16[128,2048]{1,0:T(8,128)(2,1)S(1)}, bf16[64,2048]{1,0:T(8,128)(2,1)S(1)}) custom-call(bf16[16,16,1024]{2,1,0:T(8,128)(2,1)S(1)} %all-to-all-done.q_ref, s32[128,128]{1,0:T(8,128)S(1)} %get-tuple-element.29.pos_ref, s32[128,128]{1,0:T(8,128)S(1)} %get-tuple-element.30.start_ref, bf16[128,128]{1,0:T(8,128)(2,1)S(1)} %get-tuple-element.31.order_ref, ...), custom_call_target="tpu_custom_call" | custom-call | tf_op jit(solution)/shard_map/attend/pallas_call | solution.py:440
  31.0 0.1 collective-permute-start.11
  31.1 0.9 %write_own.1.half_hbm = bf16[64,4096]{1,0:T(8,128)(2,1)} custom-call(bf16[128,128]{1,0:T(8,128)(2,1)S(1)} %get-tuple-element.31.order_ref, bf16[128,2048]{1,0:T(8,128)(2,1)S(1)} %get-tuple-element.44.context_ref), custom_call_target="tpu_custom_call" | custom-call | tf_op jit(solution)/shard_map/write_own/pallas_call | solution.py:453
  32.1 0.6 %collective-permute-done.11.received_ref = bf16[64,2048]{1,0:T(8,128)(2,1)S(1)} collective-permute-done((bf16[64,2048]{1,0:T(8,128)(2,1)S(1)}, bf16[64,2048]{1,0:T(8,128)(2,1)S(1)}, u32[]{:S(2)}, u32[]{:S(2)}) %collective-permute-start.11) | collective-permute-done | bytes 262176 | tf_op jit(solution)/shard_map/ppermute | solution.py:341
  32.6 0.7 %write_received.1 = bf16[64,4096]{1,0:T(8,128)(2,1)} custom-call(bf16[64,2048]{1,0:T(8,128)(2,1)S(1)} %collective-permute-done.11.received_ref, bf16[64,4096]{1,0:T(8,128)(2,1)} %write_own.1.half_hbm), custom_call_target="tpu_custom_call", output_to_operand_aliasing={{}: (1, {})} | custom-call | tf_op jit(solution)/shard_map/write_received/pallas_call | solution.py:462
  (2 shorter events, 0.1 us)
Async XLA Ops:
  1.2 6.7 %collective-permute-start = (bf16[64,1024]{1,0:T(8,128)(2,1)S(1)}, bf16[64,1024]{1,0:T(8,128)(2,1)S(1)}, u32[]{:S(2)}, u32[]{:S(2)}) collective-permute-start(bf16[64,1024]{1,0:T(8,128)(2,1)S(1)} %get-tuple-element.27.mine_ref), channel_id=1, source_target_pairs={{0,1},{1,0},{2,3},{3,2},{4,5},{5,4},{6,7},{7,6},{8,9},{9,8},{10,11... | collective-permute-start | bytes 393224 | tf_op jit(solution)/shard_map/ppermute | solution.py:341
  1.7 13.7 %collective-permute-start.2 = (bf16[64,1024]{1,0:T(8,128)(2,1)S(1)}, bf16[64,1024]{1,0:T(8,128)(2,1)S(1)}, u32[]{:S(2)}, u32[]{:S(2)}) collective-permute-start(bf16[64,1024]{1,0:T(8,128)(2,1)S(1)} %get-tuple-element.27.mine_ref), channel_id=1, source_target_pairs={{0,8},{1,9},{2,10},{3,11},{4,12},{5,13},{6,14},{7,15},{8,0},{9,1},... | collective-permute-start | bytes 393224 | tf_op jit(solution)/shard_map/ppermute | solution.py:341
  5.4 10.0 %collective-permute-start.1 = (bf16[64,1024]{1,0:T(8,128)(2,1)S(1)}, bf16[64,1024]{1,0:T(8,128)(2,1)S(1)}, u32[]{:S(2)}, u32[]{:S(2)}) collective-permute-start(bf16[64,1024]{1,0:T(8,128)(2,1)S(1)} %get-tuple-element.27.mine_ref), channel_id=1, source_target_pairs={{0,12},{1,13},{2,14},{3,15},{4,8},{5,9},{6,10},{7,11},{8,4},{9,5},... | collective-permute-start | bytes 393224 | tf_op jit(solution)/shard_map/ppermute | solution.py:341
  6.7 12.5 %collective-permute-start.6 = (bf16[64,1024]{1,0:T(8,128)(2,1)S(1)}, bf16[64,1024]{1,0:T(8,128)(2,1)S(1)}, u32[]{:S(2)}, u32[]{:S(2)}) collective-permute-start(bf16[64,1024]{1,0:T(8,128)(2,1)S(1)} %get-tuple-element.27.mine_ref), channel_id=1, source_target_pairs={{0,6},{1,7},{2,4},{3,5},{4,2},{5,3},{6,0},{7,1},{8,14},{9,15},{10,... | collective-permute-start | bytes 393224 | tf_op jit(solution)/shard_map/ppermute | solution.py:341
  7.9 17.9 %collective-permute-start.7 = (bf16[128,1024]{1,0:T(8,128)(2,1)S(1)}, bf16[128,1024]{1,0:T(8,128)(2,1)S(1)}, u32[]{:S(2)}, u32[]{:S(2)}) collective-permute-start(bf16[128,1024]{1,0:T(8,128)(2,1)S(1)} %pair.1.refs_0_), channel_id=1, source_target_pairs={{0,4},{1,3},{2,6},{3,1},{4,0},{5,7},{6,2},{7,5},{8,12},{9,11},{10,... | collective-permute-start | bytes 786440 | tf_op jit(solution)/shard_map/ppermute | solution.py:341
  10.9 18.3 %all-to-all-start = ((bf16[16,16,1024]{2,1,0:T(8,128)(2,1)}), bf16[16,16,1024]{2,1,0:T(8,128)(2,1)S(1)}, u32[]{:S(2)}, u32[]{:S(2)}) async-start(bf16[16,16,1024]{2,1,0:T(8,128)(2,1)} %pack.1), calls=%async_computation | async-start | bytes 1048576 | tf_op jit(solution)/shard_map/all_to_all | solution.py:385
  15.4 2.3 %copy-start = (s32[1024]{0:T(1024)S(1)}, s32[1024]{0:T(1024)}, u32[]{:S(2)}) copy-start(s32[1024]{0:T(1024)} %param.8) | copy-start | bytes 12292
  15.4 2.2 %copy-start.1 = (s32[4]{0:T(128)S(1)}, s32[4]{0:T(128)}, u32[]{:S(2)}) copy-start(s32[4]{0:T(128)} %lengths_ref.1) | copy-start | bytes 52
  15.4 11.0 %collective-permute-start.4 = (bf16[128,512]{1,0:T(8,128)(2,1)S(1)}, bf16[128,512]{1,0:T(8,128)(2,1)S(1)}, u32[]{:S(2)}, u32[]{:S(2)}) collective-permute-start(bf16[128,512]{1,0:T(8,128)(2,1)S(1)} %get-tuple-element.32.refs_0_), channel_id=1, source_target_pairs={{0,2},{1,3},{2,0},{3,1},{4,6},{5,7},{6,4},{7,5},{8,10},{9,11},{10,... | collective-permute-start | bytes 393224 | tf_op jit(solution)/shard_map/ppermute | solution.py:341
  17.3 10.2 %collective-permute-start.5 = (bf16[128,512]{1,0:T(8,128)(2,1)S(1)}, bf16[128,512]{1,0:T(8,128)(2,1)S(1)}, u32[]{:S(2)}, u32[]{:S(2)}) collective-permute-start(bf16[128,512]{1,0:T(8,128)(2,1)S(1)} %get-tuple-element.33), channel_id=1, source_target_pairs={{0,3},{1,2},{2,1},{3,0},{4,7},{5,6},{6,5},{7,4},{8,11},{9,10},{10,... | collective-permute-start | bytes 393224 | tf_op jit(solution)/shard_map/ppermute | solution.py:341
  17.3 10.2 %collective-permute-start.3 = (bf16[128,512]{1,0:T(8,128)(2,1)S(1)}, bf16[128,512]{1,0:T(8,128)(2,1)S(1)}, u32[]{:S(2)}, u32[]{:S(2)}) collective-permute-start(bf16[128,512]{1,0:T(8,128)(2,1)S(1)} %get-tuple-element.33), channel_id=1, source_target_pairs={{0,1},{1,0},{2,3},{3,2},{4,5},{5,4},{6,7},{7,6},{8,9},{9,8},{10,11... | collective-permute-start | bytes 393224 | tf_op jit(solution)/shard_map/ppermute | solution.py:341
  25.9 1.6 %collective-permute-start.8 = (bf16[64,512]{1,0:T(8,128)(2,1)S(1)}, bf16[64,512]{1,0:T(8,128)(2,1)S(1)}, u32[]{:S(2)}, u32[]{:S(2)}) collective-permute-start(bf16[64,512]{1,0:T(8,128)(2,1)S(1)} %get-tuple-element.37), channel_id=1, source_target_pairs={{0,1},{1,0},{2,3},{3,2},{4,5},{5,4},{6,7},{7,6},{8,9},{9,8},{10,11... | collective-permute-start | bytes 196616 | tf_op jit(solution)/shard_map/ppermute | solution.py:341
  26.0 1.5 %collective-permute-start.9 = (bf16[64,512]{1,0:T(8,128)(2,1)S(1)}, bf16[64,512]{1,0:T(8,128)(2,1)S(1)}, u32[]{:S(2)}, u32[]{:S(2)}) collective-permute-start(bf16[64,512]{1,0:T(8,128)(2,1)S(1)} %get-tuple-element.38), channel_id=1, source_target_pairs={{0,1},{1,0},{2,3},{3,2},{4,5},{5,4},{6,7},{7,6},{8,9},{9,8},{10,11... | collective-permute-start | bytes 196616 | tf_op jit(solution)/shard_map/ppermute | solution.py:341
  26.5 1.3 %collective-permute-start.10 = (bf16[64,512]{1,0:T(8,128)(2,1)S(1)}, bf16[64,512]{1,0:T(8,128)(2,1)S(1)}, u32[]{:S(2)}, u32[]{:S(2)}) collective-permute-start(bf16[64,512]{1,0:T(8,128)(2,1)S(1)} %get-tuple-element.39), channel_id=1, source_target_pairs={{0,1},{1,0},{2,3},{3,2},{4,5},{5,4},{6,7},{7,6},{8,9},{9,8},{10,11... | collective-permute-start | bytes 196616 | tf_op jit(solution)/shard_map/ppermute | solution.py:341
  31.0 1.6 %collective-permute-start.11 = (bf16[64,2048]{1,0:T(8,128)(2,1)S(1)}, bf16[64,2048]{1,0:T(8,128)(2,1)S(1)}, u32[]{:S(2)}, u32[]{:S(2)}) collective-permute-start(bf16[64,2048]{1,0:T(8,128)(2,1)S(1)} %get-tuple-element.43), channel_id=1, source_target_pairs={{0,1},{1,0},{2,3},{3,2},{4,5},{5,4},{6,7},{7,6},{8,9},{9,8},{10,11... | collective-permute-start | bytes 786440 | tf_op jit(solution)/shard_map/ppermute | solution.py:341

commit v12 on v11

--- a/solution.py
+++ b/solution.py
@@ -413,7 +413,7 @@
             )(*blocks)
 
         mine_far, other_far = heads_of(2 * 10**10, 1, *far)
-        from_core, from_y, from_both = swap(other_far, 1), swap(mine_far, 2), swap(other_far, 3)
+        from_both, from_y, from_core = swap(other_far, 3), swap(mine_far, 2), swap(other_far, 1)
         mine_chip, _ = heads_of(10**6, 1, chip)
         diagonal, next_chip, *_ = lax.optimization_barrier((diagonal, next_chip, order))
         mine_near, *other_near = heads_of(10**6, 1 + CORES, diagonal, next_chip)

time: 33.6 us -> 33.6 us (level)
  no operation moved by 1% of the time
where the time goes in v12:
time: 33.6 us; the launch traced here: 33.3 us
  starting transfers between devices  15.4 us (46%)
  waiting for transfers between devices  9.58 us (29%)
  Pallas kernels  8.29 us (25%)
    ppermute x12, starting transfers between devices, swap(): return lax.ppermute(array, 'ctx', pairs)  11.5 us
    ppermute x12, waiting for transfers between devices, swap(): return lax.ppermute(array, 'ctx', pairs)  8.32 us
    all_to_all x1, starting transfers between devices, on_device(): lax.all_to_all(packed, 'ctx', split_axis=0, concat_axis=0, tiled=True)  3.86 us
    pallas_call x1, Pallas kernels, on_device(): pl.pallas_call(attend_kernel, out_shape=(jax.ShapeDtypeStruct((held, HEAD...  1.84 us
    pallas_call x1, Pallas kernels, on_device(): pl.pallas_call(functools.partial(place_kernel, per_chip), out_shape=(jax....  1.57 us
    all_to_all x1, waiting for transfers between devices, on_device(): lax.all_to_all(packed, 'ctx', split_axis=0, concat_axis=0, tiled=True)  1.26 us
    pallas_call x1, Pallas kernels, on_device(): pl.pallas_call(fetch_kernel, out_shape=[jax.ShapeDtypeStruct((rows, rows)...  1.17 us
    pallas_call x1, Pallas kernels, on_device(): pl.pallas_call(functools.partial(pack_kernel, chips), out_shape=message,...  1.07 us
  transfers between devices with their start and end apart: 13, of which 6 were waited for; matrix products, arithmetic and copies ran while one was open for 0% of the time, Pallas kernels for 14%

profile of v12, /device:TPU:0, one launch (start us, length us, event | category | flops | bytes accessed | tf_op | source)
XLA Modules:
  0.0 33.3 jit_solution(2999030441462574903)
XLA Ops:
  0.0 1.2 %fetch.1 = (bf16[64,64]{1,0:T(8,128)(2,1)S(1)}, bf16[64,4096]{1,0:T(8,128)(2,1)S(1)}, bf16[64,1024]{1,0:T(8,128)(2,1)S(1)}) custom-call(s32[8,128]{1,0:T(8,128)} %bitcast.1, bf16[64,4096]{1,0:T(8,128)(2,1)} %q_hbm.1, bf16[64,512]{1,0:T(8,128)(2,1)} %k_hbm.1, bf16[64,512]{1,0:T(8,128)(2,1)} %v_hbm.1), custom_call_target="tpu_custom_call" | custom-call | tf_op jit(solution)/shard_map/fetch/pallas_call | solution.py:345
  1.2 0.5 %collective-permute-start = (bf16[64,1024]{1,0:T(8,128)(2,1)S(1)}, bf16[64,1024]{1,0:T(8,128)(2,1)S(1)}, u32[]{:S(2)}, u32[]{:S(2)}) collective-permute-start(bf16[64,1024]{1,0:T(8,128)(2,1)S(1)} %get-tuple-element.27.mine_ref), channel_id=1, source_target_pairs={{0,1},{1,0},{2,3},{3,2},{4,5},{5,4},{6,7},{7,6},{8,9},{9,8},{10,11... | collective-permute-start | bytes 393224 | tf_op jit(solution)/shard_map/ppermute | solution.py:341
  1.7 3.7 %collective-permute-start.2 = (bf16[64,1024]{1,0:T(8,128)(2,1)S(1)}, bf16[64,1024]{1,0:T(8,128)(2,1)S(1)}, u32[]{:S(2)}, u32[]{:S(2)}) collective-permute-start(bf16[64,1024]{1,0:T(8,128)(2,1)S(1)} %get-tuple-element.27.mine_ref), channel_id=1, source_target_pairs={{0,8},{1,9},{2,10},{3,11},{4,12},{5,13},{6,14},{7,15},{8,0},{9,1},... | collective-permute-start | bytes 393224 | tf_op jit(solution)/shard_map/ppermute | solution.py:341
  5.4 1.3 %collective-permute-start.1 = (bf16[64,1024]{1,0:T(8,128)(2,1)S(1)}, bf16[64,1024]{1,0:T(8,128)(2,1)S(1)}, u32[]{:S(2)}, u32[]{:S(2)}) collective-permute-start(bf16[64,1024]{1,0:T(8,128)(2,1)S(1)} %get-tuple-element.27.mine_ref), channel_id=1, source_target_pairs={{0,12},{1,13},{2,14},{3,15},{4,8},{5,9},{6,10},{7,11},{8,4},{9,5},... | collective-permute-start | bytes 393224 | tf_op jit(solution)/shard_map/ppermute | solution.py:341
  6.7 1.2 %collective-permute-start.6 = (bf16[64,1024]{1,0:T(8,128)(2,1)S(1)}, bf16[64,1024]{1,0:T(8,128)(2,1)S(1)}, u32[]{:S(2)}, u32[]{:S(2)}) collective-permute-start(bf16[64,1024]{1,0:T(8,128)(2,1)S(1)} %get-tuple-element.27.mine_ref), channel_id=1, source_target_pairs={{0,6},{1,7},{2,4},{3,5},{4,2},{5,3},{6,0},{7,1},{8,14},{9,15},{10,... | collective-permute-start | bytes 393224 | tf_op jit(solution)/shard_map/ppermute | solution.py:341
  7.9 0.0 collective-permute-done.other_ref
  7.9 1.9 %collective-permute-start.7 = (bf16[128,1024]{1,0:T(8,128)(2,1)S(1)}, bf16[128,1024]{1,0:T(8,128)(2,1)S(1)}, u32[]{:S(2)}, u32[]{:S(2)}) collective-permute-start(bf16[128,1024]{1,0:T(8,128)(2,1)S(1)} %pair.1.refs_0_), channel_id=1, source_target_pairs={{0,4},{1,3},{2,6},{3,1},{4,0},{5,7},{6,2},{7,5},{8,12},{9,11},{10,... | collective-permute-start | bytes 786440 | tf_op jit(solution)/shard_map/ppermute | solution.py:341
  9.8 1.1 %pack.1 = bf16[16,16,1024]{2,1,0:T(8,128)(2,1)} custom-call(bf16[64,64]{1,0:T(8,128)(2,1)S(1)} %get-tuple-element.25.order_ref, bf16[64,4096]{1,0:T(8,128)(2,1)S(1)} %get-tuple-element.28.q_ref), custom_call_target="tpu_custom_call" | custom-call | flops 33554432 | bytes 1048576 | tf_op jit(solution)/shard_map/pack/pallas_call | solution.py:374
  10.9 3.9 %all-to-all-start = ((bf16[16,16,1024]{2,1,0:T(8,128)(2,1)}), bf16[16,16,1024]{2,1,0:T(8,128)(2,1)S(1)}, u32[]{:S(2)}, u32[]{:S(2)}) async-start(bf16[16,16,1024]{2,1,0:T(8,128)(2,1)} %pack.1), calls=%async_computation | async-start | bytes 1048576 | tf_op jit(solution)/shard_map/all_to_all | solution.py:385
  14.7 0.6 %collective-permute-done.2.refs_1_ = bf16[64,1024]{1,0:T(8,128)(2,1)S(1)} collective-permute-done((bf16[64,1024]{1,0:T(8,128)(2,1)S(1)}, bf16[64,1024]{1,0:T(8,128)(2,1)S(1)}, u32[]{:S(2)}, u32[]{:S(2)}) %collective-permute-start.2) | collective-permute-done | bytes 131104 | tf_op jit(solution)/shard_map/ppermute | solution.py:341
  15.4 0.0 collective-permute-done.1.refs_0_
  15.4 0.0 copy-start
  15.4 0.0 copy-start.1
  15.4 1.8 %collective-permute-start.4 = (bf16[128,512]{1,0:T(8,128)(2,1)S(1)}, bf16[128,512]{1,0:T(8,128)(2,1)S(1)}, u32[]{:S(2)}, u32[]{:S(2)}) collective-permute-start(bf16[128,512]{1,0:T(8,128)(2,1)S(1)} %get-tuple-element.32.refs_0_), channel_id=1, source_target_pairs={{0,2},{1,3},{2,0},{3,1},{4,6},{5,7},{6,4},{7,5},{8,10},{9,11},{10,... | collective-permute-start | bytes 393224 | tf_op jit(solution)/shard_map/ppermute | solution.py:341
  17.3 0.0 collective-permute-start.5
  17.3 0.4 %collective-permute-start.3 = (bf16[128,512]{1,0:T(8,128)(2,1)S(1)}, bf16[128,512]{1,0:T(8,128)(2,1)S(1)}, u32[]{:S(2)}, u32[]{:S(2)}) collective-permute-start(bf16[128,512]{1,0:T(8,128)(2,1)S(1)} %get-tuple-element.33), channel_id=1, source_target_pairs={{0,1},{1,0},{2,3},{3,2},{4,5},{5,4},{6,7},{7,6},{8,9},{9,8},{10,11... | collective-permute-start | bytes 393224 | tf_op jit(solution)/shard_map/ppermute | solution.py:341
  17.6 0.0 copy-done
  17.6 0.0 copy-done.1
  17.6 1.6 %place.1 = (s32[128,128]{1,0:T(8,128)S(1)}, s32[128,128]{1,0:T(8,128)S(1)}, bf16[128,128]{1,0:T(8,128)(2,1)S(1)}) custom-call(s32[4]{0:T(128)S(1)} %copy-done.1, s32[8,128]{1,0:T(8,128)S(1)} %bitcast.2), custom_call_target="tpu_custom_call" | custom-call | tf_op jit(solution)/shard_map/place/pallas_call | solution.py:387
  19.2 0.0 collective-permute-done.6.refs_0_
  19.2 6.6 %collective-permute-done.7.refs_1_ = bf16[128,1024]{1,0:T(8,128)(2,1)S(1)} collective-permute-done((bf16[128,1024]{1,0:T(8,128)(2,1)S(1)}, bf16[128,1024]{1,0:T(8,128)(2,1)S(1)}, u32[]{:S(2)}, u32[]{:S(2)}) %collective-permute-start.7) | collective-permute-done | bytes 262176 | tf_op jit(solution)/shard_map/ppermute | solution.py:341
  25.8 0.1 heads.4
  25.9 0.1 collective-permute-start.8
  26.0 0.5 %collective-permute-start.9 = (bf16[64,512]{1,0:T(8,128)(2,1)S(1)}, bf16[64,512]{1,0:T(8,128)(2,1)S(1)}, u32[]{:S(2)}, u32[]{:S(2)}) collective-permute-start(bf16[64,512]{1,0:T(8,128)(2,1)S(1)} %get-tuple-element.38), channel_id=1, source_target_pairs={{0,1},{1,0},{2,3},{3,2},{4,5},{5,4},{6,7},{7,6},{8,9},{9,8},{10,11... | collective-permute-start | bytes 196616 | tf_op jit(solution)/shard_map/ppermute | solution.py:341
  26.5 0.0 collective-permute-done.4.refs_2_
  26.5 0.1 collective-permute-start.10
  26.5 0.7 %heads.5 = (bf16[128,512]{1,0:T(8,128)(2,1)S(1)}, bf16[128,512]{1,0:T(8,128)(2,1)}) custom-call(bf16[128,1024]{1,0:T(8,128)(2,1)S(1)} %pair.1.refs_0_), custom_call_target="tpu_custom_call" | custom-call | flops 1000000 | bytes 1048576 | tf_op jit(solution)/shard_map/heads/pallas_call | solution.py:405
  27.2 0.3 collective-permute-done.5.refs_3_
  27.5 0.0 collective-permute-done.3.refs_1_
  27.5 0.0 collective-permute-done.8.refs_5_
  27.5 0.0 collective-permute-done.9.refs_6_
  27.5 0.2 collective-permute-done.10.refs_7_
  27.7 0.2 unpack.1
  27.9 1.3 %all-to-all-done.q_ref = bf16[16,16,1024]{2,1,0:T(8,128)(2,1)S(1)} async-done(((bf16[16,16,1024]{2,1,0:T(8,128)(2,1)}), bf16[16,16,1024]{2,1,0:T(8,128)(2,1)S(1)}, u32[]{:S(2)}, u32[]{:S(2)}) %all-to-all-start) | async-done | bytes 524320 | tf_op jit(solution)/shard_map/all_to_all | solution.py:385
  29.2 1.8 %attend.1 = (bf16[128,2048]{1,0:T(8,128)(2,1)S(1)}, bf16[64,2048]{1,0:T(8,128)(2,1)S(1)}) custom-call(bf16[16,16,1024]{2,1,0:T(8,128)(2,1)S(1)} %all-to-all-done.q_ref, s32[128,128]{1,0:T(8,128)S(1)} %get-tuple-element.29.pos_ref, s32[128,128]{1,0:T(8,128)S(1)} %get-tuple-element.30.start_ref, bf16[128,128]{1,0:T(8,128)(2,1)S(1)} %get-tuple-element.31.order_ref, ...), custom_call_target="tpu_custom_call" | custom-call | tf_op jit(solution)/shard_map/attend/pallas_call | solution.py:440
  31.0 0.1 collective-permute-start.11
  31.1 0.9 %write_own.1.half_hbm = bf16[64,4096]{1,0:T(8,128)(2,1)} custom-call(bf16[128,128]{1,0:T(8,128)(2,1)S(1)} %get-tuple-element.31.order_ref, bf16[128,2048]{1,0:T(8,128)(2,1)S(1)} %get-tuple-element.44.context_ref), custom_call_target="tpu_custom_call" | custom-call | tf_op jit(solution)/shard_map/write_own/pallas_call | solution.py:453
  32.1 0.6 %collective-permute-done.11.received_ref = bf16[64,2048]{1,0:T(8,128)(2,1)S(1)} collective-permute-done((bf16[64,2048]{1,0:T(8,128)(2,1)S(1)}, bf16[64,2048]{1,0:T(8,128)(2,1)S(1)}, u32[]{:S(2)}, u32[]{:S(2)}) %collective-permute-start.11) | collective-permute-done | bytes 262176 | tf_op jit(solution)/shard_map/ppermute | solution.py:341
  32.6 0.7 %write_received.1 = bf16[64,4096]{1,0:T(8,128)(2,1)} custom-call(bf16[64,2048]{1,0:T(8,128)(2,1)S(1)} %collective-permute-done.11.received_ref, bf16[64,4096]{1,0:T(8,128)(2,1)} %write_own.1.half_hbm), custom_call_target="tpu_custom_call", output_to_operand_aliasing={{}: (1, {})} | custom-call | tf_op jit(solution)/shard_map/write_received/pallas_call | solution.py:462
  (2 shorter events, 0.1 us)
Async XLA Ops:
  1.2 6.7 %collective-permute-start = (bf16[64,1024]{1,0:T(8,128)(2,1)S(1)}, bf16[64,1024]{1,0:T(8,128)(2,1)S(1)}, u32[]{:S(2)}, u32[]{:S(2)}) collective-permute-start(bf16[64,1024]{1,0:T(8,128)(2,1)S(1)} %get-tuple-element.27.mine_ref), channel_id=1, source_target_pairs={{0,1},{1,0},{2,3},{3,2},{4,5},{5,4},{6,7},{7,6},{8,9},{9,8},{10,11... | collective-permute-start | bytes 393224 | tf_op jit(solution)/shard_map/ppermute | solution.py:341
  1.7 13.7 %collective-permute-start.2 = (bf16[64,1024]{1,0:T(8,128)(2,1)S(1)}, bf16[64,1024]{1,0:T(8,128)(2,1)S(1)}, u32[]{:S(2)}, u32[]{:S(2)}) collective-permute-start(bf16[64,1024]{1,0:T(8,128)(2,1)S(1)} %get-tuple-element.27.mine_ref), channel_id=1, source_target_pairs={{0,8},{1,9},{2,10},{3,11},{4,12},{5,13},{6,14},{7,15},{8,0},{9,1},... | collective-permute-start | bytes 393224 | tf_op jit(solution)/shard_map/ppermute | solution.py:341
  5.4 10.0 %collective-permute-start.1 = (bf16[64,1024]{1,0:T(8,128)(2,1)S(1)}, bf16[64,1024]{1,0:T(8,128)(2,1)S(1)}, u32[]{:S(2)}, u32[]{:S(2)}) collective-permute-start(bf16[64,1024]{1,0:T(8,128)(2,1)S(1)} %get-tuple-element.27.mine_ref), channel_id=1, source_target_pairs={{0,12},{1,13},{2,14},{3,15},{4,8},{5,9},{6,10},{7,11},{8,4},{9,5},... | collective-permute-start | bytes 393224 | tf_op jit(solution)/shard_map/ppermute | solution.py:341
  6.7 12.5 %collective-permute-start.6 = (bf16[64,1024]{1,0:T(8,128)(2,1)S(1)}, bf16[64,1024]{1,0:T(8,128)(2,1)S(1)}, u32[]{:S(2)}, u32[]{:S(2)}) collective-permute-start(bf16[64,1024]{1,0:T(8,128)(2,1)S(1)} %get-tuple-element.27.mine_ref), channel_id=1, source_target_pairs={{0,6},{1,7},{2,4},{3,5},{4,2},{5,3},{6,0},{7,1},{8,14},{9,15},{10,... | collective-permute-start | bytes 393224 | tf_op jit(solution)/shard_map/ppermute | solution.py:341
  7.9 17.9 %collective-permute-start.7 = (bf16[128,1024]{1,0:T(8,128)(2,1)S(1)}, bf16[128,1024]{1,0:T(8,128)(2,1)S(1)}, u32[]{:S(2)}, u32[]{:S(2)}) collective-permute-start(bf16[128,1024]{1,0:T(8,128)(2,1)S(1)} %pair.1.refs_0_), channel_id=1, source_target_pairs={{0,4},{1,3},{2,6},{3,1},{4,0},{5,7},{6,2},{7,5},{8,12},{9,11},{10,... | collective-permute-start | bytes 786440 | tf_op jit(solution)/shard_map/ppermute | solution.py:341
  10.9 18.3 %all-to-all-start = ((bf16[16,16,1024]{2,1,0:T(8,128)(2,1)}), bf16[16,16,1024]{2,1,0:T(8,128)(2,1)S(1)}, u32[]{:S(2)}, u32[]{:S(2)}) async-start(bf16[16,16,1024]{2,1,0:T(8,128)(2,1)} %pack.1), calls=%async_computation | async-start | bytes 1048576 | tf_op jit(solution)/shard_map/all_to_all | solution.py:385
  15.4 2.3 %copy-start = (s32[1024]{0:T(1024)S(1)}, s32[1024]{0:T(1024)}, u32[]{:S(2)}) copy-start(s32[1024]{0:T(1024)} %param.8) | copy-start | bytes 12292
  15.4 2.2 %copy-start.1 = (s32[4]{0:T(128)S(1)}, s32[4]{0:T(128)}, u32[]{:S(2)}) copy-start(s32[4]{0:T(128)} %lengths_ref.1) | copy-start | bytes 52
  15.4 11.0 %collective-permute-start.4 = (bf16[128,512]{1,0:T(8,128)(2,1)S(1)}, bf16[128,512]{1,0:T(8,128)(2,1)S(1)}, u32[]{:S(2)}, u32[]{:S(2)}) collective-permute-start(bf16[128,512]{1,0:T(8,128)(2,1)S(1)} %get-tuple-element.32.refs_0_), channel_id=1, source_target_pairs={{0,2},{1,3},{2,0},{3,1},{4,6},{5,7},{6,4},{7,5},{8,10},{9,11},{10,... | collective-permute-start | bytes 393224 | tf_op jit(solution)/shard_map/ppermute | solution.py:341
  17.3 10.2 %collective-permute-start.5 = (bf16[128,512]{1,0:T(8,128)(2,1)S(1)}, bf16[128,512]{1,0:T(8,128)(2,1)S(1)}, u32[]{:S(2)}, u32[]{:S(2)}) collective-permute-start(bf16[128,512]{1,0:T(8,128)(2,1)S(1)} %get-tuple-element.33), channel_id=1, source_target_pairs={{0,3},{1,2},{2,1},{3,0},{4,7},{5,6},{6,5},{7,4},{8,11},{9,10},{10,... | collective-permute-start | bytes 393224 | tf_op jit(solution)/shard_map/ppermute | solution.py:341
  17.3 10.2 %collective-permute-start.3 = (bf16[128,512]{1,0:T(8,128)(2,1)S(1)}, bf16[128,512]{1,0:T(8,128)(2,1)S(1)}, u32[]{:S(2)}, u32[]{:S(2)}) collective-permute-start(bf16[128,512]{1,0:T(8,128)(2,1)S(1)} %get-tuple-element.33), channel_id=1, source_target_pairs={{0,1},{1,0},{2,3},{3,2},{4,5},{5,4},{6,7},{7,6},{8,9},{9,8},{10,11... | collective-permute-start | bytes 393224 | tf_op jit(solution)/shard_map/ppermute | solution.py:341
  25.9 1.6 %collective-permute-start.8 = (bf16[64,512]{1,0:T(8,128)(2,1)S(1)}, bf16[64,512]{1,0:T(8,128)(2,1)S(1)}, u32[]{:S(2)}, u32[]{:S(2)}) collective-permute-start(bf16[64,512]{1,0:T(8,128)(2,1)S(1)} %get-tuple-element.37), channel_id=1, source_target_pairs={{0,1},{1,0},{2,3},{3,2},{4,5},{5,4},{6,7},{7,6},{8,9},{9,8},{10,11... | collective-permute-start | bytes 196616 | tf_op jit(solution)/shard_map/ppermute | solution.py:341
  26.0 1.5 %collective-permute-start.9 = (bf16[64,512]{1,0:T(8,128)(2,1)S(1)}, bf16[64,512]{1,0:T(8,128)(2,1)S(1)}, u32[]{:S(2)}, u32[]{:S(2)}) collective-permute-start(bf16[64,512]{1,0:T(8,128)(2,1)S(1)} %get-tuple-element.38), channel_id=1, source_target_pairs={{0,1},{1,0},{2,3},{3,2},{4,5},{5,4},{6,7},{7,6},{8,9},{9,8},{10,11... | collective-permute-start | bytes 196616 | tf_op jit(solution)/shard_map/ppermute | solution.py:341
  26.5 1.3 %collective-permute-start.10 = (bf16[64,512]{1,0:T(8,128)(2,1)S(1)}, bf16[64,512]{1,0:T(8,128)(2,1)S(1)}, u32[]{:S(2)}, u32[]{:S(2)}) collective-permute-start(bf16[64,512]{1,0:T(8,128)(2,1)S(1)} %get-tuple-element.39), channel_id=1, source_target_pairs={{0,1},{1,0},{2,3},{3,2},{4,5},{5,4},{6,7},{7,6},{8,9},{9,8},{10,11... | collective-permute-start | bytes 196616 | tf_op jit(solution)/shard_map/ppermute | solution.py:341
  31.0 1.6 %collective-permute-start.11 = (bf16[64,2048]{1,0:T(8,128)(2,1)S(1)}, bf16[64,2048]{1,0:T(8,128)(2,1)S(1)}, u32[]{:S(2)}, u32[]{:S(2)}) collective-permute-start(bf16[64,2048]{1,0:T(8,128)(2,1)S(1)} %get-tuple-element.43), channel_id=1, source_target_pairs={{0,1},{1,0},{2,3},{3,2},{4,5},{5,4},{6,7},{7,6},{8,9},{9,8},{10,11... | collective-permute-start | bytes 786440 | tf_op jit(solution)/shard_map/ppermute | solution.py:341

commit v13 on v12

--- a/solution.py
+++ b/solution.py
@@ -194,7 +194,7 @@
     width = HEADS * HD
 
     def chip_of(sender):
-        offset = jnp.where(sender % CORES == 0, ALONG, ACROSS)
+        offset = jnp.where(sender % CORES == 0, ACROSS, ALONG)
         chip = jnp.bitwise_xor(sender, offset) // CORES
         return [chip * CORES + core for core in range(CORES)]
 
@@ -367,7 +367,7 @@
             compiler_params=VMEM,
             name="pair",
         )(kv_near, other)
-        next_chip = swap(chip, ALONG, ACROSS)
+        next_chip = swap(chip, ACROSS, ALONG)
         q_near, _ = lax.optimization_barrier((q_near, chip))
 
     operands = (order_in, q_near) if apart else (order_in, q_near, kv_near)

time: 33.6 us -> 33.7 us (level)
  starting transfers between devices: 15.4 us -> 22.2 us
  waiting for transfers between devices: 9.58 us -> 2.87 us
    ppermute x12, waiting for transfers between devices: 8.32 us -> 1.91 us  [swap(): return lax.ppermute(array, 'ctx', pairs)]
    ppermute x12, starting transfers between devices: 11.5 us -> 16.9 us  [swap(): return lax.ppermute(array, 'ctx', pairs)]
    all_to_all x1, starting transfers between devices: 3.86 us -> 5.26 us  [on_device(): lax.all_to_all(packed, 'ctx', split_axis=0, concat_axis=0, tiled=True)]
  transfers between devices with their start and end apart: 13 -> 13, of which waited for: 6 -> 4; matrix products, arithmetic and copies ran while one was open for 0% -> 0% of each run, Pallas kernels for 14% -> 14%
where the time goes in v13:
time: 33.7 us; the launch traced here: 33.5 us
  starting transfers between devices  22.2 us (66%)
  Pallas kernels  8.31 us (25%)
  waiting for transfers between devices  2.87 us (9%)
    ppermute x12, starting transfers between devices, swap(): return lax.ppermute(array, 'ctx', pairs)  16.9 us
    all_to_all x1, starting transfers between devices, on_device(): lax.all_to_all(packed, 'ctx', split_axis=0, concat_axis=0, tiled=True)  5.26 us
    ppermute x12, waiting for transfers between devices, swap(): return lax.ppermute(array, 'ctx', pairs)  1.91 us
    pallas_call x1, Pallas kernels, on_device(): pl.pallas_call(attend_kernel, out_shape=(jax.ShapeDtypeStruct((held, HEAD...  1.83 us
    pallas_call x1, Pallas kernels, on_device(): pl.pallas_call(functools.partial(place_kernel, per_chip), out_shape=(jax....  1.57 us
    pallas_call x1, Pallas kernels, on_device(): pl.pallas_call(fetch_kernel, out_shape=[jax.ShapeDtypeStruct((rows, rows)...  1.17 us
    pallas_call x1, Pallas kernels, on_device(): pl.pallas_call(functools.partial(pack_kernel, chips), out_shape=message,...  1.07 us
    all_to_all x1, waiting for transfers between devices, on_device(): lax.all_to_all(packed, 'ctx', split_axis=0, concat_axis=0, tiled=True)  0.96 us
  transfers between devices with their start and end apart: 13, of which 4 were waited for; matrix products, arithmetic and copies ran while one was open for 0% of the time, Pallas kernels for 14%

profile of v13, /device:TPU:0, one launch (start us, length us, event | category | flops | bytes accessed | tf_op | source)
XLA Modules:
  0.0 33.5 jit_solution(1818340672312400474)
XLA Ops:
  0.0 1.2 %fetch.1 = (bf16[64,64]{1,0:T(8,128)(2,1)S(1)}, bf16[64,4096]{1,0:T(8,128)(2,1)S(1)}, bf16[64,1024]{1,0:T(8,128)(2,1)S(1)}) custom-call(s32[8,128]{1,0:T(8,128)} %bitcast.1, bf16[64,4096]{1,0:T(8,128)(2,1)} %q_hbm.1, bf16[64,512]{1,0:T(8,128)(2,1)} %k_hbm.1, bf16[64,512]{1,0:T(8,128)(2,1)} %v_hbm.1), custom_call_target="tpu_custom_call" | custom-call | tf_op jit(solution)/shard_map/fetch/pallas_call | solution.py:345
  1.2 0.5 %collective-permute-start = (bf16[64,1024]{1,0:T(8,128)(2,1)S(1)}, bf16[64,1024]{1,0:T(8,128)(2,1)S(1)}, u32[]{:S(2)}, u32[]{:S(2)}) collective-permute-start(bf16[64,1024]{1,0:T(8,128)(2,1)S(1)} %get-tuple-element.27.mine_ref), channel_id=1, source_target_pairs={{0,1},{1,0},{2,3},{3,2},{4,5},{5,4},{6,7},{7,6},{8,9},{9,8},{10,11... | collective-permute-start | bytes 393224 | tf_op jit(solution)/shard_map/ppermute | solution.py:341
  1.7 3.7 %collective-permute-start.2 = (bf16[64,1024]{1,0:T(8,128)(2,1)S(1)}, bf16[64,1024]{1,0:T(8,128)(2,1)S(1)}, u32[]{:S(2)}, u32[]{:S(2)}) collective-permute-start(bf16[64,1024]{1,0:T(8,128)(2,1)S(1)} %get-tuple-element.27.mine_ref), channel_id=1, source_target_pairs={{0,8},{1,9},{2,10},{3,11},{4,12},{5,13},{6,14},{7,15},{8,0},{9,1},... | collective-permute-start | bytes 393224 | tf_op jit(solution)/shard_map/ppermute | solution.py:341
  5.4 1.3 %collective-permute-start.1 = (bf16[64,1024]{1,0:T(8,128)(2,1)S(1)}, bf16[64,1024]{1,0:T(8,128)(2,1)S(1)}, u32[]{:S(2)}, u32[]{:S(2)}) collective-permute-start(bf16[64,1024]{1,0:T(8,128)(2,1)S(1)} %get-tuple-element.27.mine_ref), channel_id=1, source_target_pairs={{0,12},{1,13},{2,14},{3,15},{4,8},{5,9},{6,10},{7,11},{8,4},{9,5},... | collective-permute-start | bytes 393224 | tf_op jit(solution)/shard_map/ppermute | solution.py:341
  6.7 1.2 %collective-permute-start.6 = (bf16[64,1024]{1,0:T(8,128)(2,1)S(1)}, bf16[64,1024]{1,0:T(8,128)(2,1)S(1)}, u32[]{:S(2)}, u32[]{:S(2)}) collective-permute-start(bf16[64,1024]{1,0:T(8,128)(2,1)S(1)} %get-tuple-element.27.mine_ref), channel_id=1, source_target_pairs={{0,6},{1,7},{2,4},{3,5},{4,2},{5,3},{6,0},{7,1},{8,14},{9,15},{10,... | collective-permute-start | bytes 393224 | tf_op jit(solution)/shard_map/ppermute | solution.py:341
  7.9 0.0 collective-permute-done.other_ref
  7.9 0.6 %collective-permute-start.7 = (bf16[128,1024]{1,0:T(8,128)(2,1)S(1)}, bf16[128,1024]{1,0:T(8,128)(2,1)S(1)}, u32[]{:S(2)}, u32[]{:S(2)}) collective-permute-start(bf16[128,1024]{1,0:T(8,128)(2,1)S(1)} %pair.1.refs_0_), channel_id=1, source_target_pairs={{0,2},{1,5},{2,0},{3,7},{4,6},{5,1},{6,4},{7,3},{8,10},{9,13},{10,... | collective-permute-start | bytes 786440 | tf_op jit(solution)/shard_map/ppermute | solution.py:341
  8.5 1.1 %pack.1 = bf16[16,16,1024]{2,1,0:T(8,128)(2,1)} custom-call(bf16[64,64]{1,0:T(8,128)(2,1)S(1)} %get-tuple-element.25.order_ref, bf16[64,4096]{1,0:T(8,128)(2,1)S(1)} %get-tuple-element.28.q_ref), custom_call_target="tpu_custom_call" | custom-call | flops 33554432 | bytes 1048576 | tf_op jit(solution)/shard_map/pack/pallas_call | solution.py:374
  9.6 5.3 %all-to-all-start = ((bf16[16,16,1024]{2,1,0:T(8,128)(2,1)}), bf16[16,16,1024]{2,1,0:T(8,128)(2,1)S(1)}, u32[]{:S(2)}, u32[]{:S(2)}) async-start(bf16[16,16,1024]{2,1,0:T(8,128)(2,1)} %pack.1), calls=%async_computation | async-start | bytes 1048576 | tf_op jit(solution)/shard_map/all_to_all | solution.py:385
  14.8 0.5 %collective-permute-done.2.refs_1_ = bf16[64,1024]{1,0:T(8,128)(2,1)S(1)} collective-permute-done((bf16[64,1024]{1,0:T(8,128)(2,1)S(1)}, bf16[64,1024]{1,0:T(8,128)(2,1)S(1)}, u32[]{:S(2)}, u32[]{:S(2)}) %collective-permute-start.2) | collective-permute-done | bytes 131104 | tf_op jit(solution)/shard_map/ppermute | solution.py:341
  15.4 0.0 collective-permute-done.1.refs_0_
  15.4 0.0 copy-start
  15.4 0.0 copy-start.1
  15.4 1.8 %collective-permute-start.4 = (bf16[128,512]{1,0:T(8,128)(2,1)S(1)}, bf16[128,512]{1,0:T(8,128)(2,1)S(1)}, u32[]{:S(2)}, u32[]{:S(2)}) collective-permute-start(bf16[128,512]{1,0:T(8,128)(2,1)S(1)} %get-tuple-element.32.refs_0_), channel_id=1, source_target_pairs={{0,2},{1,3},{2,0},{3,1},{4,6},{5,7},{6,4},{7,5},{8,10},{9,11},{10,... | collective-permute-start | bytes 393224 | tf_op jit(solution)/shard_map/ppermute | solution.py:341
  17.3 0.0 collective-permute-start.5
  17.3 0.4 %collective-permute-start.3 = (bf16[128,512]{1,0:T(8,128)(2,1)S(1)}, bf16[128,512]{1,0:T(8,128)(2,1)S(1)}, u32[]{:S(2)}, u32[]{:S(2)}) collective-permute-start(bf16[128,512]{1,0:T(8,128)(2,1)S(1)} %get-tuple-element.33), channel_id=1, source_target_pairs={{0,1},{1,0},{2,3},{3,2},{4,5},{5,4},{6,7},{7,6},{8,9},{9,8},{10,11... | collective-permute-start | bytes 393224 | tf_op jit(solution)/shard_map/ppermute | solution.py:341
  17.6 0.0 copy-done
  17.6 0.0 copy-done.1
  17.6 1.6 %place.1 = (s32[128,128]{1,0:T(8,128)S(1)}, s32[128,128]{1,0:T(8,128)S(1)}, bf16[128,128]{1,0:T(8,128)(2,1)S(1)}) custom-call(s32[4]{0:T(128)S(1)} %copy-done.1, s32[8,128]{1,0:T(8,128)S(1)} %bitcast.2), custom_call_target="tpu_custom_call" | custom-call | tf_op jit(solution)/shard_map/place/pallas_call | solution.py:387
  19.2 0.0 collective-permute-done.6.refs_0_
  19.2 0.0 collective-permute-done.7.refs_1_
  19.2 0.1 heads.4
  19.3 6.6 %collective-permute-start.8 = (bf16[64,512]{1,0:T(8,128)(2,1)S(1)}, bf16[64,512]{1,0:T(8,128)(2,1)S(1)}, u32[]{:S(2)}, u32[]{:S(2)}) collective-permute-start(bf16[64,512]{1,0:T(8,128)(2,1)S(1)} %get-tuple-element.37), channel_id=1, source_target_pairs={{0,1},{1,0},{2,3},{3,2},{4,5},{5,4},{6,7},{7,6},{8,9},{9,8},{10,11... | collective-permute-start | bytes 196616 | tf_op jit(solution)/shard_map/ppermute | solution.py:341
  26.0 0.1 collective-permute-start.9
  26.0 0.0 collective-permute-done.4.refs_2_
  26.0 0.4 %collective-permute-start.10 = (bf16[64,512]{1,0:T(8,128)(2,1)S(1)}, bf16[64,512]{1,0:T(8,128)(2,1)S(1)}, u32[]{:S(2)}, u32[]{:S(2)}) collective-permute-start(bf16[64,512]{1,0:T(8,128)(2,1)S(1)} %get-tuple-element.39), channel_id=1, source_target_pairs={{0,1},{1,0},{2,3},{3,2},{4,5},{5,4},{6,7},{7,6},{8,9},{9,8},{10,11... | collective-permute-start | bytes 196616 | tf_op jit(solution)/shard_map/ppermute | solution.py:341
  26.5 0.7 %heads.5 = (bf16[128,512]{1,0:T(8,128)(2,1)S(1)}, bf16[128,512]{1,0:T(8,128)(2,1)}) custom-call(bf16[128,1024]{1,0:T(8,128)(2,1)S(1)} %pair.1.refs_0_), custom_call_target="tpu_custom_call" | custom-call | flops 1000000 | bytes 1048576 | tf_op jit(solution)/shard_map/heads/pallas_call | solution.py:405
  27.2 1.0 %collective-permute-done.5.refs_3_ = bf16[128,512]{1,0:T(8,128)(2,1)S(1)} collective-permute-done((bf16[128,512]{1,0:T(8,128)(2,1)S(1)}, bf16[128,512]{1,0:T(8,128)(2,1)S(1)}, u32[]{:S(2)}, u32[]{:S(2)}) %collective-permute-start.5) | collective-permute-done | bytes 131104 | tf_op jit(solution)/shard_map/ppermute | solution.py:341
  28.1 0.0 collective-permute-done.3.refs_1_
  28.2 0.0 collective-permute-done.8.refs_5_
  28.2 0.0 collective-permute-done.9.refs_6_
  28.2 0.0 collective-permute-done.10.refs_7_
  28.2 0.2 unpack.1
  28.4 1.0 %all-to-all-done.q_ref = bf16[16,16,1024]{2,1,0:T(8,128)(2,1)S(1)} async-done(((bf16[16,16,1024]{2,1,0:T(8,128)(2,1)}), bf16[16,16,1024]{2,1,0:T(8,128)(2,1)S(1)}, u32[]{:S(2)}, u32[]{:S(2)}) %all-to-all-start) | async-done | bytes 524320 | tf_op jit(solution)/shard_map/all_to_all | solution.py:385
  29.3 1.8 %attend.1 = (bf16[128,2048]{1,0:T(8,128)(2,1)S(1)}, bf16[64,2048]{1,0:T(8,128)(2,1)S(1)}) custom-call(bf16[16,16,1024]{2,1,0:T(8,128)(2,1)S(1)} %all-to-all-done.q_ref, s32[128,128]{1,0:T(8,128)S(1)} %get-tuple-element.29.pos_ref, s32[128,128]{1,0:T(8,128)S(1)} %get-tuple-element.30.start_ref, bf16[128,128]{1,0:T(8,128)(2,1)S(1)} %get-tuple-element.31.order_ref, ...), custom_call_target="tpu_custom_call" | custom-call | tf_op jit(solution)/shard_map/attend/pallas_call | solution.py:440
  31.2 0.3 collective-permute-start.11
  31.5 0.9 %write_own.1.half_hbm = bf16[64,4096]{1,0:T(8,128)(2,1)} custom-call(bf16[128,128]{1,0:T(8,128)(2,1)S(1)} %get-tuple-element.31.order_ref, bf16[128,2048]{1,0:T(8,128)(2,1)S(1)} %get-tuple-element.44.context_ref), custom_call_target="tpu_custom_call" | custom-call | tf_op jit(solution)/shard_map/write_own/pallas_call | solution.py:453
  32.4 0.4 %collective-permute-done.11.received_ref = bf16[64,2048]{1,0:T(8,128)(2,1)S(1)} collective-permute-done((bf16[64,2048]{1,0:T(8,128)(2,1)S(1)}, bf16[64,2048]{1,0:T(8,128)(2,1)S(1)}, u32[]{:S(2)}, u32[]{:S(2)}) %collective-permute-start.11) | collective-permute-done | bytes 262176 | tf_op jit(solution)/shard_map/ppermute | solution.py:341
  32.8 0.7 %write_received.1 = bf16[64,4096]{1,0:T(8,128)(2,1)} custom-call(bf16[64,2048]{1,0:T(8,128)(2,1)S(1)} %collective-permute-done.11.received_ref, bf16[64,4096]{1,0:T(8,128)(2,1)} %write_own.1.half_hbm), custom_call_target="tpu_custom_call", output_to_operand_aliasing={{}: (1, {})} | custom-call | tf_op jit(solution)/shard_map/write_received/pallas_call | solution.py:462
  (2 shorter events, 0.1 us)
Async XLA Ops:
  1.2 6.7 %collective-permute-start = (bf16[64,1024]{1,0:T(8,128)(2,1)S(1)}, bf16[64,1024]{1,0:T(8,128)(2,1)S(1)}, u32[]{:S(2)}, u32[]{:S(2)}) collective-permute-start(bf16[64,1024]{1,0:T(8,128)(2,1)S(1)} %get-tuple-element.27.mine_ref), channel_id=1, source_target_pairs={{0,1},{1,0},{2,3},{3,2},{4,5},{5,4},{6,7},{7,6},{8,9},{9,8},{10,11... | collective-permute-start | bytes 393224 | tf_op jit(solution)/shard_map/ppermute | solution.py:341
  1.7 13.7 %collective-permute-start.2 = (bf16[64,1024]{1,0:T(8,128)(2,1)S(1)}, bf16[64,1024]{1,0:T(8,128)(2,1)S(1)}, u32[]{:S(2)}, u32[]{:S(2)}) collective-permute-start(bf16[64,1024]{1,0:T(8,128)(2,1)S(1)} %get-tuple-element.27.mine_ref), channel_id=1, source_target_pairs={{0,8},{1,9},{2,10},{3,11},{4,12},{5,13},{6,14},{7,15},{8,0},{9,1},... | collective-permute-start | bytes 393224 | tf_op jit(solution)/shard_map/ppermute | solution.py:341
  5.4 10.0 %collective-permute-start.1 = (bf16[64,1024]{1,0:T(8,128)(2,1)S(1)}, bf16[64,1024]{1,0:T(8,128)(2,1)S(1)}, u32[]{:S(2)}, u32[]{:S(2)}) collective-permute-start(bf16[64,1024]{1,0:T(8,128)(2,1)S(1)} %get-tuple-element.27.mine_ref), channel_id=1, source_target_pairs={{0,12},{1,13},{2,14},{3,15},{4,8},{5,9},{6,10},{7,11},{8,4},{9,5},... | collective-permute-start | bytes 393224 | tf_op jit(solution)/shard_map/ppermute | solution.py:341
  6.7 12.5 %collective-permute-start.6 = (bf16[64,1024]{1,0:T(8,128)(2,1)S(1)}, bf16[64,1024]{1,0:T(8,128)(2,1)S(1)}, u32[]{:S(2)}, u32[]{:S(2)}) collective-permute-start(bf16[64,1024]{1,0:T(8,128)(2,1)S(1)} %get-tuple-element.27.mine_ref), channel_id=1, source_target_pairs={{0,6},{1,7},{2,4},{3,5},{4,2},{5,3},{6,0},{7,1},{8,14},{9,15},{10,... | collective-permute-start | bytes 393224 | tf_op jit(solution)/shard_map/ppermute | solution.py:341
  7.9 11.3 %collective-permute-start.7 = (bf16[128,1024]{1,0:T(8,128)(2,1)S(1)}, bf16[128,1024]{1,0:T(8,128)(2,1)S(1)}, u32[]{:S(2)}, u32[]{:S(2)}) collective-permute-start(bf16[128,1024]{1,0:T(8,128)(2,1)S(1)} %pair.1.refs_0_), channel_id=1, source_target_pairs={{0,2},{1,5},{2,0},{3,7},{4,6},{5,1},{6,4},{7,3},{8,10},{9,13},{10,... | collective-permute-start | bytes 786440 | tf_op jit(solution)/shard_map/ppermute | solution.py:341
  9.6 19.8 %all-to-all-start = ((bf16[16,16,1024]{2,1,0:T(8,128)(2,1)}), bf16[16,16,1024]{2,1,0:T(8,128)(2,1)S(1)}, u32[]{:S(2)}, u32[]{:S(2)}) async-start(bf16[16,16,1024]{2,1,0:T(8,128)(2,1)} %pack.1), calls=%async_computation | async-start | bytes 1048576 | tf_op jit(solution)/shard_map/all_to_all | solution.py:385
  15.4 2.3 %copy-start = (s32[1024]{0:T(1024)S(1)}, s32[1024]{0:T(1024)}, u32[]{:S(2)}) copy-start(s32[1024]{0:T(1024)} %param.8) | copy-start | bytes 12292
  15.4 2.2 %copy-start.1 = (s32[4]{0:T(128)S(1)}, s32[4]{0:T(128)}, u32[]{:S(2)}) copy-start(s32[4]{0:T(128)} %lengths_ref.1) | copy-start | bytes 52
  15.4 10.6 %collective-permute-start.4 = (bf16[128,512]{1,0:T(8,128)(2,1)S(1)}, bf16[128,512]{1,0:T(8,128)(2,1)S(1)}, u32[]{:S(2)}, u32[]{:S(2)}) collective-permute-start(bf16[128,512]{1,0:T(8,128)(2,1)S(1)} %get-tuple-element.32.refs_0_), channel_id=1, source_target_pairs={{0,2},{1,3},{2,0},{3,1},{4,6},{5,7},{6,4},{7,5},{8,10},{9,11},{10,... | collective-permute-start | bytes 393224 | tf_op jit(solution)/shard_map/ppermute | solution.py:341
  17.3 10.9 %collective-permute-start.5 = (bf16[128,512]{1,0:T(8,128)(2,1)S(1)}, bf16[128,512]{1,0:T(8,128)(2,1)S(1)}, u32[]{:S(2)}, u32[]{:S(2)}) collective-permute-start(bf16[128,512]{1,0:T(8,128)(2,1)S(1)} %get-tuple-element.33), channel_id=1, source_target_pairs={{0,3},{1,2},{2,1},{3,0},{4,7},{5,6},{6,5},{7,4},{8,11},{9,10},{10,... | collective-permute-start | bytes 393224 | tf_op jit(solution)/shard_map/ppermute | solution.py:341
  17.3 10.9 %collective-permute-start.3 = (bf16[128,512]{1,0:T(8,128)(2,1)S(1)}, bf16[128,512]{1,0:T(8,128)(2,1)S(1)}, u32[]{:S(2)}, u32[]{:S(2)}) collective-permute-start(bf16[128,512]{1,0:T(8,128)(2,1)S(1)} %get-tuple-element.33), channel_id=1, source_target_pairs={{0,1},{1,0},{2,3},{3,2},{4,5},{5,4},{6,7},{7,6},{8,9},{9,8},{10,11... | collective-permute-start | bytes 393224 | tf_op jit(solution)/shard_map/ppermute | solution.py:341
  19.3 8.8 %collective-permute-start.8 = (bf16[64,512]{1,0:T(8,128)(2,1)S(1)}, bf16[64,512]{1,0:T(8,128)(2,1)S(1)}, u32[]{:S(2)}, u32[]{:S(2)}) collective-permute-start(bf16[64,512]{1,0:T(8,128)(2,1)S(1)} %get-tuple-element.37), channel_id=1, source_target_pairs={{0,1},{1,0},{2,3},{3,2},{4,5},{5,4},{6,7},{7,6},{8,9},{9,8},{10,11... | collective-permute-start | bytes 196616 | tf_op jit(solution)/shard_map/ppermute | solution.py:341
  26.0 2.2 %collective-permute-start.9 = (bf16[64,512]{1,0:T(8,128)(2,1)S(1)}, bf16[64,512]{1,0:T(8,128)(2,1)S(1)}, u32[]{:S(2)}, u32[]{:S(2)}) collective-permute-start(bf16[64,512]{1,0:T(8,128)(2,1)S(1)} %get-tuple-element.38), channel_id=1, source_target_pairs={{0,1},{1,0},{2,3},{3,2},{4,5},{5,4},{6,7},{7,6},{8,9},{9,8},{10,11... | collective-permute-start | bytes 196616 | tf_op jit(solution)/shard_map/ppermute | solution.py:341
  26.0 2.1 %collective-permute-start.10 = (bf16[64,512]{1,0:T(8,128)(2,1)S(1)}, bf16[64,512]{1,0:T(8,128)(2,1)S(1)}, u32[]{:S(2)}, u32[]{:S(2)}) collective-permute-start(bf16[64,512]{1,0:T(8,128)(2,1)S(1)} %get-tuple-element.39), channel_id=1, source_target_pairs={{0,1},{1,0},{2,3},{3,2},{4,5},{5,4},{6,7},{7,6},{8,9},{9,8},{10,11... | collective-permute-start | bytes 196616 | tf_op jit(solution)/shard_map/ppermute | solution.py:341
  31.2 1.6 %collective-permute-start.11 = (bf16[64,2048]{1,0:T(8,128)(2,1)S(1)}, bf16[64,2048]{1,0:T(8,128)(2,1)S(1)}, u32[]{:S(2)}, u32[]{:S(2)}) collective-permute-start(bf16[64,2048]{1,0:T(8,128)(2,1)S(1)} %get-tuple-element.43), channel_id=1, source_target_pairs={{0,1},{1,0},{2,3},{3,2},{4,5},{5,4},{6,7},{7,6},{8,9},{9,8},{10,11... | collective-permute-start | bytes 786440 | tf_op jit(solution)/shard_map/ppermute | solution.py:341
